TPU v7x, 256 devices: a whole 4x4x8 slice. The times are simulated.
256 devices in a mesh: dp: 8 (over x, y_hi), fsdp: 32 (over y_lo, z, core).
Axes of the slice: x: 4, y: 4 (y_hi: 2, y_lo: 2; y = y_hi * 2 + y_lo), z: 8, core: 2. Of those that a mesh axis runs over, the one named last changes fastest.
Arguments:
- hidden: bfloat16 [65536, 5120], P(('dp', 'fsdp')), may hold values from -6 to 6
- queries: bfloat16 [65536, 2560], P(('dp', 'fsdp')), may hold values from -64 to 64
- upstream: bfloat16 [65536, 2560], P(('dp', 'fsdp')), may hold values from -6 to 6
- segment_ids: int32 [256, 256], P(('dp', 'fsdp')), may hold values from 0 to 3, never falling along the last dimension, each value on 1 to 128 neighbouring positions
- prompt_lengths: int32 [256, 4], P(('dp', 'fsdp')), may hold values from 1 to 128
- advantages: float32 [256, 4], P(('dp', 'fsdp')), may hold values from -16 to 16
- kv_weight: bfloat16 [5120, 1024], P('fsdp'), may hold values from -0.078125 to 0.078125
- master: float32 [5120, 1024], P('fsdp', 'dp'), may hold values from -3 to 3
- moment_one: float32 [5120, 1024], P('fsdp', 'dp'), may hold values from -0.03 to 0.03
- moment_two: float32 [5120, 1024], P('fsdp', 'dp'), may hold values from 1e-06 to 0.0001
Outputs:
- query_grad: bfloat16 [65536, 2560], P(('dp', 'fsdp'))
- hidden_grad: bfloat16 [65536, 5120], P(('dp', 'fsdp'))
- new_master: float32 [5120, 1024], P('fsdp', 'dp')
- new_moment_one: float32 [5120, 1024], P('fsdp', 'dp')
- new_moment_two: float32 [5120, 1024], P('fsdp', 'dp')
Inputs may be any that keep to these rules, and one draw needn't show every extreme that they name: `segment_ids`: in each row ids never fall, each rollout has 1 to 128 tokens and some rollout has exactly 128.
All inputs are finite; a program needn't handle non-finite values.
Results may differ from a plain program's by a relative error of at most 0.035.
The roundings to bfloat16 on the way count: a program that leaves them out, or rounds other values in their place, can miss the bound.
Values may be sent and summed in bfloat16 or wider, within the bound.
No kernel may reach another device: no remote copies, remote signals or barrier semaphores. Data moves between devices by JAX's collectives and lax.ppermute only.
A program may use at most 128 MiB of HBM per device.

v0:
```python
import jax
import jax.numpy as jnp
from jax import lax
from jax.sharding import PartitionSpec as P

HD = 128
STEP = 10


ROPE_BASE = 1000000.0


def positions_in_row(segs):
    length = segs.shape[0]
    index = jnp.arange(length, dtype=jnp.int32)
    previous = jnp.concatenate([segs[:1] - 1, segs[:-1]])
    starts = jnp.where(segs != previous, index, jnp.zeros_like(index))
    return index - lax.cummax(starts)


def token_terms(segs, prompts, advs):
    pos = positions_in_row(segs)
    onehot = segs[:, None] == jnp.arange(prompts.shape[0], dtype=jnp.int32)[None, :]
    prompt_tok = jnp.sum(
        jnp.where(onehot, prompts[None, :], jnp.zeros_like(prompts)[None, :]), axis=1
    )
    adv_tok = jnp.sum(jnp.where(onehot, advs[None, :], jnp.zeros_like(advs)[None, :]), axis=1)
    return (pos, pos >= prompt_tok, adv_tok)


def rotate(values):
    half = values.shape[-1] // 2
    return jnp.concatenate([-values[..., half:], values[..., :half]], axis=-1)


def attention_backward(kv_pre, queries, upstream, segs, pos, weight):
    length = segs.shape[0]
    kv_half = kv_pre.shape[1] // 2
    head_size = HD
    heads = kv_half // head_size
    group = queries.shape[1] // kv_half
    freq = ROPE_BASE ** (-(jnp.arange(head_size // 2, dtype=jnp.float32) * 2.0 / head_size))
    angle = pos.astype(jnp.float32)[:, None] * freq[None, :]
    cosine = jnp.concatenate([jnp.cos(angle), jnp.cos(angle)], axis=1)[:, None, :]
    sine = jnp.concatenate([jnp.sin(angle), jnp.sin(angle)], axis=1)[:, None, :]
    keys_pre = kv_pre[:, :kv_half].reshape(length, heads, head_size)
    keys = (keys_pre * cosine + rotate(keys_pre) * sine).astype(jnp.bfloat16)
    values = kv_pre[:, kv_half:].reshape(length, heads, head_size).astype(jnp.bfloat16)
    query_heads = queries.reshape(length, heads, group, head_size)
    scale = 1.0 / jnp.sqrt(jnp.float32(head_size))
    scores = (
        jnp.einsum("qkgd,tkd->kgqt", query_heads, keys, preferred_element_type=jnp.float32) * scale
    )
    index = jnp.arange(length, dtype=jnp.int32)
    allowed = (segs[:, None] == segs[None, :]) & (index[None, :] <= index[:, None])
    scores = jnp.where(allowed[None, None], scores, jnp.float32(-1e30))
    probs = jax.nn.softmax(scores, axis=-1)
    probs_low = probs.astype(jnp.bfloat16)
    output = jnp.einsum("kgqt,tkd->qkgd", probs_low, values, preferred_element_type=jnp.float32)
    grad_out = (
        (upstream.astype(jnp.float32) * weight[:, None])
        .astype(jnp.bfloat16)
        .reshape(length, heads, group, head_size)
    )
    delta = jnp.sum(grad_out.astype(jnp.float32) * output, axis=-1)
    delta = jnp.transpose(delta, (1, 2, 0))
    grad_probs = jnp.einsum("qkgd,tkd->kgqt", grad_out, values, preferred_element_type=jnp.float32)
    grad_scores = (probs * (grad_probs - delta[..., None])).astype(jnp.bfloat16)
    query_grad = (
        jnp.einsum("kgqt,tkd->qkgd", grad_scores, keys, preferred_element_type=jnp.float32) * scale
    ).astype(jnp.bfloat16)
    key_grad = (
        jnp.einsum("kgqt,qkgd->tkd", grad_scores, query_heads, preferred_element_type=jnp.float32)
        * scale
    )
    value_grad = jnp.einsum(
        "kgqt,qkgd->tkd", probs_low, grad_out, preferred_element_type=jnp.float32
    )
    key_grad_pre = key_grad * cosine - rotate(key_grad * sine)
    kv_grad = jnp.concatenate(
        [key_grad_pre.reshape(length, kv_half), value_grad.reshape(length, kv_half)], axis=1
    ).astype(jnp.bfloat16)
    return (query_grad.reshape(length, queries.shape[1]), kv_grad)


def body(
    hidden,
    queries,
    upstream,
    segment_ids,
    prompt_lengths,
    advantages,
    kv_weight,
    master,
    moment_one,
    moment_two,
):
    segs = segment_ids[0]
    pos, live, adv_tok = token_terms(segs, prompt_lengths[0], advantages[0])
    local_count = jnp.sum(live.astype(jnp.float32))
    count = lax.psum(local_count, ("dp", "fsdp"))
    total_tokens = hidden.shape[0] * lax.axis_size("dp") * lax.axis_size("fsdp")
    factor = jnp.float32(total_tokens) / jnp.maximum(count, jnp.float32(1.0))
    weight = jnp.where(live, adv_tok * factor, jnp.zeros_like(adv_tok))
    full_weight = lax.all_gather(kv_weight, "fsdp", axis=0, tiled=True)
    kv_pre = jnp.dot(hidden, full_weight, preferred_element_type=jnp.float32)
    query_grad, kv_grad = attention_backward(kv_pre, queries, upstream, segs, pos, weight)
    hidden_grad = lax.dot_general(
        kv_grad, full_weight, (((1,), (1,)), ((), ())), preferred_element_type=jnp.float32
    )
    term = lax.dot_general(
        hidden, kv_grad, (((0,), (0,)), ((), ())), preferred_element_type=jnp.float32
    )
    row_sums = lax.psum_scatter(term.astype(jnp.bfloat16), "fsdp", scatter_dimension=0, tiled=True)
    summed = lax.psum_scatter(row_sums, "dp", scatter_dimension=1, tiled=True).astype(jnp.float32)
    weight_grad = summed / jnp.float32(total_tokens)
    new_moment_one = 0.9 * moment_one + 0.1 * weight_grad
    new_moment_two = 0.999 * moment_two + 0.001 * weight_grad * weight_grad
    first_hat = new_moment_one / (1.0 - 0.9**STEP)
    second_hat = new_moment_two / (1.0 - 0.999**STEP)
    new_master = master - 0.001 * (first_hat / (jnp.sqrt(second_hat) + 1e-08) + 0.1 * master)
    return (
        query_grad,
        hidden_grad.astype(jnp.bfloat16),
        new_master,
        new_moment_one,
        new_moment_two,
    )


def solution(mesh):
    placed = (
        P(("dp", "fsdp"), None),
        P(("dp", "fsdp"), None),
        P(("dp", "fsdp"), None),
        P(("dp", "fsdp"), None),
        P(("dp", "fsdp"), None),
        P(("dp", "fsdp"), None),
        P("fsdp", None),
        P("fsdp", "dp"),
        P("fsdp", "dp"),
        P("fsdp", "dp"),
    )
    return jax.shard_map(
        body,
        mesh=mesh,
        in_specs=placed,
        out_specs=(
            P(("dp", "fsdp"), None),
            P(("dp", "fsdp"), None),
            P("fsdp", "dp"),
            P("fsdp", "dp"),
            P("fsdp", "dp"),
        ),
        check_vma=False,
    )
```

profile of v0, /device:TPU:2, one launch (start us, length us, event | category | flops | bytes accessed | tf_op | source)
XLA Modules:
  0.0 361.1 jit_solution(15903940844586977714)
XLA Ops:
  8.0 1.2 slice.37
  9.8 0.8 compare_select_fusion.1
  11.2 0.8 select_reduce_fusion.1
  12.6 78.7 %psum.7 = f32[]{:T(128)} all-reduce(f32[]{:T(128)} %fusion.20), channel_id=1, replica_groups=mesh['dp'=8,'fsdp'=32] {'dp','fsdp'}, use_global_device_ids=true, to_apply=%region_7.8 | all-reduce | flops 1 | bytes 8 | tf_op jit(solution)/shard_map/psum | solution.py:101
  92.0 0.8 select_reduce_fusion
  92.9 2.7 multiply_convert_fusion.1
  95.5 2.4 copy.125
  97.9 2.4 copy.122
  100.8 0.8 broadcast_multiply_fusion
  101.5 0.7 fusion.16
  102.3 5.6 %fusion.29 = f32[256,1024]{1,0:T(8,128)S(1)} fusion(bf16[256,5120]{1,0:T(8,128)(2,1)S(1)} %copy-done, bf16[5120,1024]{1,0:T(8,128)(2,1)} %all-gather.2.cloned.1.call-done), kind=kOutput, calls=%fused_computation.67 | convolution fusion | flops 2684354560 | bytes 14155776 | tf_op jit(solution)/shard_map/dot_general | solution.py:106
  107.9 0.9 slice.47
  108.8 1.2 copy.157
  110.0 0.8 convert_element_type.57
  110.8 1.1 copy.139
  112.0 1.8 fusion.15
  113.8 5.5 %fusion.28 = (f32[4,5,256]{2,1,0:T(8,128)S(1)}, f32[4,5,256,256]{2,3,1,0:T(8,128)}) fusion(pred[256,256]{0,1:T(8,128)(4,1)} %fusion.16, bf16[256,4,128,1]{0,2,3,1:T(8,128)(2,1)} %fusion.15, bf16[256,4,5,128]{0,3,2,1:T(8,128)(2,1)} %bitcast.104), kind=kOutput, calls=%fused_computation.66 | convolution fusion | flops 340787456 | bytes 6901760 | tf_op jit(solution)/shard_map/sub | solution.py:57
  119.3 3.2 fusion.8
  122.6 1.0 fusion.9
  124.1 1.0 fusion.2
  125.4 1.0 convolution_bitcast_fusion.1
  127.1 5.5 %convert_bitcast_fusion = bf16[5120,1024]{0,1:T(8,128)(2,1)} fusion(bf16[256,5120]{1,0:T(8,128)(2,1)S(1)} %copy-done, bf16[256,512]{0,1:T(8,128)(2,1)S(1)} %bitcast.109, bf16[256,512]{0,1:T(8,128)(2,1)S(1)} %bitcast.112), kind=kOutput, calls=%fused_computation.1 | convolution fusion | flops 2690646016 | bytes 13631488 | tf_op jit(solution)/shard_map/dot_general | solution.py:111
  132.6 14.4 %copy.153 = bf16[5120,1024]{1,0:T(8,128)(2,1)} copy(bf16[5120,1024]{0,1:T(8,128)(2,1)} %convert_bitcast_fusion) | data formatting | bytes 20971520
  147.2 0.7 copy-done.4
  147.9 3.3 multiply_convert_fusion
  151.3 2.4 copy.134
  153.7 124.3 %reduce-scatter.7.cloned.1.call-done = bf16[160,1024]{1,0:T(8,128)(2,1)} async-done(((bf16[5120,1024]{1,0:T(8,128)(2,1)}), bf16[160,1024]{1,0:T(8,128)(2,1)}) %reduce-scatter.7.cloned.1.call-update) | async-done | bytes 327696 | tf_op jit(solution)/shard_map/reduce_scatter | solution.py:114
  278.0 2.0 copy.155
  280.1 12.3 %convolution_convert_fusion = bf16[256,5120]{1,0:T(8,128)(2,1)} fusion(bf16[5120,1024]{1,0:T(8,128)(2,1)} %all-gather.2.cloned.1.call-done, bf16[256,512]{0,1:T(8,128)(2,1)S(1)} %bitcast.110, bf16[256,512]{0,1:T(8,128)(2,1)S(1)} %bitcast.113), kind=kOutput, calls=%fused_computation.2 | convolution fusion | flops 2686713856 | bytes 13631488 | tf_op jit(solution)/shard_map/dot_general | solution.py:108
  292.4 60.5 %reduce-scatter.9.cloned.1.call-done = bf16[128,160]{1,0:T(8,128)(2,1)} async-done(((bf16[1024,160]{1,0:T(8,128)(2,1)}), bf16[128,160]{1,0:T(8,128)(2,1)}) %reduce-scatter.9.cloned.1.call-update) | async-done | bytes 40976
  352.9 0.9 copy.156
  353.8 0.7 multiply_subtract_fusion
  (46 shorter events, 4.4 us)
Async XLA Ops:
  7.2 95.1 %copy-start = (bf16[256,5120]{1,0:T(8,128)(2,1)S(1)}, bf16[256,5120]{1,0:T(8,128)(2,1)}, u32[]{:S(2)}) copy-start(bf16[256,5120]{1,0:T(8,128)(2,1)} %param.10) | copy-start | bytes 7864324
  7.2 95.1 %all-gather.2.cloned.1.call-start = ((), (), s32[]{:S(2)}) async-start(), calls=%async_computation.2 | async-start | bytes 10813440 | tf_op jit(solution)/shard_map/all_gather | solution.py:105
  7.9 270.1 %reduce-scatter.7.cloned.1.call-start = ((), (), s32[]{:S(2)}) async-start(), calls=%async_computation.3 | async-start | bytes 10813440 | tf_op jit(solution)/shard_map/reduce_scatter | solution.py:114
  95.5 6.0 %copy-start.9 = (s32[1,256]{1,0:T(1,128)S(1)}, s32[1,256]{1,0:T(1,128)}, u32[]{:S(2)}) copy-start(s32[1,256]{1,0:T(1,128)} %param.13) | copy-start | bytes 3076
  119.3 3.2 copy-start.1
  119.3 4.8 %slice-start = ((s8[5242880]{0:T(1024)(128)(4,1)}), s8[4194304]{0:T(1024)(128)(4,1)S(1)}, s32[]{:S(2)}) async-start(s8[5242880]{0:T(1024)(128)(4,1)} %bitcast.102), calls=%async_computation.5 | async-start | bytes 8388608
  122.5 1.6 slice-start.1
  124.1 1.3 copy-start.3
  125.4 1.5 copy-start.2
  125.4 1.5 copy-start.5
  147.0 0.9 copy-start.4
  147.0 205.9 %reduce-scatter.9.cloned.1.call-start = ((), (), s32[]{:S(2)}) async-start(), calls=%async_computation.4 | async-start | bytes 589824
  280.1 73.8 %copy-start.6 = (f32[160,128]{1,0:T(8,128)S(1)}, f32[160,128]{1,0:T(8,128)}, u32[]{:S(2)}) copy-start(f32[160,128]{1,0:T(8,128)} %param.17) | copy-start | bytes 245764
  280.1 73.8 %copy-start.7 = (f32[160,128]{1,0:T(8,128)S(1)}, f32[160,128]{1,0:T(8,128)}, u32[]{:S(2)}) copy-start(f32[160,128]{1,0:T(8,128)} %param.18) | copy-start | bytes 245764
  280.1 73.8 %copy-start.8 = (f32[160,128]{1,0:T(8,128)S(1)}, f32[160,128]{1,0:T(8,128)}, u32[]{:S(2)}) copy-start(f32[160,128]{1,0:T(8,128)} %param.19) | copy-start | bytes 245764
Sparse Core Ops, SparseCore 0:
  9.9 78.3 all-gather.1
  147.1 130.8 reduce-scatter.6
  281.9 70.9 reduce-scatter.8
where the time goes:
time: 362 us; the launch traced here: 361 us
  waiting for transfers between devices  186 us (51%)
  blocking collectives  78.7 us (22%)
  matrix products  35.7 us (10%)
  local copies, waits for them, and re-layouts  31.5 us (9%)
  between operations  15.3 us (4%)
  other arithmetic  14 us (4%)
    reduce_scatter x1, waiting for transfers between devices, body(): lax.psum_scatter(term.astype(jnp.bfloat16), 'fsdp', scatter_dimension=0,...  124 us
    psum x1, blocking collectives, body(): count = lax.psum(local_count, ('dp', 'fsdp'))  78.7 us
    unnamed x4, waiting for transfers between devices  61.2 us
    unnamed x29, local copies, waits for them, and re-layouts  23.7 us
    dot_general x1, matrix products, body(): lax.dot_general(kv_grad, full_weight, (((1,), (1,)), ((), ())), preferred...  12.3 us
  transfers between devices with their start and end apart: 3, of which 2 were waited for; matrix products, arithmetic and copies ran while one was open for 9% of the time, Pallas kernels for 0%

commit v1 on v0

v1 whole, which is shorter than its diff:
```python
import jax
import jax.numpy as jnp
from jax import lax
from jax.experimental import pallas as pl
from jax.experimental.pallas import tpu as pltpu
from jax.sharding import Mesh, PartitionSpec as P

HD = 128
STEP = 10
ROPE_BASE = 1000000.0
GROUP = 5
KVH = 4
SCALE = HD**-0.5
RZ = 64
RA = 48
Y = ("yh", "yl")
F32 = jnp.float32
BF16 = jnp.bfloat16


def positions_in_row(segs):
    length = segs.shape[0]
    index = jnp.arange(length, dtype=jnp.int32)
    previous = jnp.concatenate([segs[:1] - 1, segs[:-1]])
    starts = jnp.where(segs != previous, index, jnp.zeros_like(index))
    return index - lax.cummax(starts)


def token_terms(segs, prompts, advs):
    pos = positions_in_row(segs)
    onehot = segs[:, None] == jnp.arange(prompts.shape[0], dtype=jnp.int32)[None, :]
    prompt_tok = jnp.sum(
        jnp.where(onehot, prompts[None, :], jnp.zeros_like(prompts)[None, :]), axis=1
    )
    adv_tok = jnp.sum(jnp.where(onehot, advs[None, :], jnp.zeros_like(advs)[None, :]), axis=1)
    return (pos, pos >= prompt_tok, adv_tok)


def shift(v, axis, n, k):
    return lax.ppermute(v, axis, [(i, (i + k) % n) for i in range(n)])


def swap(v, axis, n, bit):
    return lax.ppermute(v, axis, [(i, i ^ bit) for i in range(n)])


def total_of(v):
    for axis, n, bit in (
        ("c", 2, 1), ("x", 4, 1), ("x", 4, 2), ("yl", 2, 1), ("yh", 2, 1),
        ("z", 8, 1), ("z", 8, 2), ("z", 8, 4),
    ):
        v = v + swap(v, axis, n, bit)
    return v


def dot_nt(a, b):
    return lax.dot_general(a, b, (((1,), (1,)), ((), ())), preferred_element_type=F32)


def dot_tn(a, b):
    return lax.dot_general(a, b, (((0,), (0,)), ((), ())), preferred_element_type=F32)


def attention_kernel(kpre, vpre, q, up, cos, sin, start, weight, qg, kvg):
    length = kpre.shape[0]
    cosine, sine = cos[...], sin[...]
    kp = kpre[...]
    k = (kp * cosine + pltpu.roll(kp, HD // 2, 1) * sine).astype(BF16)
    v = vpre[...].astype(BF16)
    key_index = lax.broadcasted_iota(jnp.int32, (length, length), 0)
    query_index = lax.broadcasted_iota(jnp.int32, (length, length), 1)
    allowed = (key_index >= start[...]) & (key_index <= query_index)
    w = weight[...]
    dk = jnp.zeros((length, HD), F32)
    dv = jnp.zeros((length, HD), F32)
    for g in range(GROUP):
        cols = slice(g * HD, (g + 1) * HD)
        qh = q[:, cols]
        do = (up[:, cols].astype(F32) * w).astype(BF16)
        s = jnp.where(allowed, dot_nt(k, qh) * SCALE, F32(-1e30))
        e = jnp.exp(s - jnp.max(s, axis=0, keepdims=True))
        p = e * (1.0 / jnp.sum(e, axis=0, keepdims=True))
        low = p.astype(BF16)
        dp = dot_nt(v, do)
        delta = jnp.sum(low.astype(F32) * dp, axis=0, keepdims=True)
        ds = (p * (dp - delta)).astype(BF16)
        qg[:, cols] = (dot_tn(ds, k) * SCALE).astype(BF16)
        dk = dk + jnp.dot(ds, qh, preferred_element_type=F32)
        dv = dv + jnp.dot(low, do, preferred_element_type=F32)
    dk = dk * SCALE
    kvg[0] = (dk * cosine - pltpu.roll(dk, HD // 2, 1) * sine).astype(BF16)
    kvg[1] = dv.astype(BF16)


def attention_backward(kv_pre, queries, upstream, pos, weight):
    length = pos.shape[0]
    freq = ROPE_BASE ** (-(jnp.arange(HD // 2, dtype=F32) * 2.0 / HD))
    angle = pos.astype(F32)[:, None] * freq[None, :]
    cosine = jnp.concatenate([jnp.cos(angle), jnp.cos(angle)], axis=1)
    sine = jnp.concatenate([-jnp.sin(angle), jnp.sin(angle)], axis=1)
    start = (jnp.arange(length, dtype=jnp.int32) - pos)[None, :]
    whole = lambda shape: pl.BlockSpec(shape, lambda h: (0, 0))
    return pl.pallas_call(
        attention_kernel,
        grid=(KVH,),
        in_specs=[
            pl.BlockSpec((length, HD), lambda h: (0, h)),
            pl.BlockSpec((length, HD), lambda h: (0, h + KVH)),
            pl.BlockSpec((length, GROUP * HD), lambda h: (0, h)),
            pl.BlockSpec((length, GROUP * HD), lambda h: (0, h)),
            whole((length, HD)),
            whole((length, HD)),
            whole((1, length)),
            whole((length, 1)),
        ],
        out_specs=[
            pl.BlockSpec((length, GROUP * HD), lambda h: (0, h)),
            pl.BlockSpec((2, length, HD), lambda h: (0, 0, h)),
        ],
        out_shape=[
            jax.ShapeDtypeStruct((length, KVH * GROUP * HD), BF16),
            jax.ShapeDtypeStruct((2, length, KVH * HD), BF16),
        ],
        compiler_params=pltpu.CompilerParams(vmem_limit_bytes=32 * 2**20),
    )(kv_pre, kv_pre, queries, upstream, cosine, sine, start, weight[:, None])


def pick(v, index, axis):
    return lax.dynamic_index_in_dim(v, index, axis, keepdims=False)


def add_up(parts):
    total = parts[0].astype(F32)
    for part in parts[1:]:
        total = total + part.astype(F32)
    return total


def body(
    hidden,
    queries,
    upstream,
    segment_ids,
    prompt_lengths,
    advantages,
    kv_weight,
    master,
    moment_one,
    moment_two,
):
    barrier = lax.optimization_barrier
    x, z, c = lax.axis_index("x"), lax.axis_index("z"), lax.axis_index("c")
    y = lax.axis_index(Y)
    length, width = hidden.shape
    rows = kv_weight.shape[0]
    cols = kv_weight.shape[1]
    segs = segment_ids[0]
    full_weight = lax.all_gather(kv_weight, ("yl", "z", "c"), axis=0, tiled=True)
    pos, live, adv_tok = token_terms(segs, prompt_lengths[0], advantages[0])
    local_count = jnp.sum(live.astype(F32))
    count = total_of(jnp.broadcast_to(local_count, (8, 128)))[0, 0]
    total_tokens = length * 256
    factor = F32(total_tokens) / jnp.maximum(count, F32(1.0))
    weight = jnp.where(live, adv_tok * factor, jnp.zeros_like(adv_tok))

    hidden_t = hidden.T.reshape(16, 2, rows, length)
    mine = pick(hidden_t, c, 1)
    theirs = shift(pick(hidden_t, 1 - c, 1), "c", 2, 1)
    hidden_pair = jnp.concatenate([mine, theirs], axis=-1).reshape(2, 8, rows, 2 * length)
    hz = jnp.transpose(hidden_pair[:, :, :RZ], (1, 0, 2, 3)).reshape(16 * RZ, 2 * length)
    ha = hidden_pair[:, :, RZ : RZ + RA].reshape(16 * RA, 2 * length)
    hb = hidden_pair[:, :, RZ + RA :].reshape(2, 8 * RA, 2 * length)

    kv_pre = jnp.dot(hidden, full_weight, preferred_element_type=F32)
    query_grad, kv_grad = attention_backward(kv_pre, queries, upstream, pos, weight)
    kv_sib = shift(kv_grad, "c", 2, 1)
    pair = jnp.concatenate([kv_grad, kv_sib], axis=1)
    pair = jnp.concatenate([pair[0], pair[1]], axis=1)

    part_z = jnp.dot(hz, pair, preferred_element_type=F32).astype(BF16)
    sum_z = lax.psum_scatter(part_z, "z", scatter_dimension=0, tiled=True)

    def to_x(k):
        cols = lax.dynamic_slice_in_dim(pair, lax.rem(x + k, 4) * 2 * HD, 2 * HD, axis=1)
        return jnp.dot(ha, cols, preferred_element_type=F32).astype(BF16)

    def to_y(k):
        there = lax.rem(y + k, 4)
        cols = pick(pair.reshape(2 * length, 4, 2, HD), there // 2, 2).reshape(2 * length, 4 * HD)
        return jnp.dot(pick(hb, lax.rem(there, 2), 0), cols, preferred_element_type=F32).astype(BF16)

    def block_y(v, k):
        there = lax.rem(y + k, 4)
        v = v.reshape(2, -1, 2 * HD)
        at = (lax.rem(there, 2), 0, there // 2 * HD)
        return lax.dynamic_slice(v, at, (1, v.shape[1], HD))[0]

    def block_x(v, k, width):
        return lax.dynamic_slice_in_dim(v, lax.rem(x + k, 4) * width, width, axis=1)

    a_out = [to_x(k) for k in (0, 1, 2, 3)]
    b_out = [to_y(k) for k in (0, 1, 2, 3)]
    arrived = barrier(
        tuple(shift(a_out[k], "x", 4, k) for k in (1, 2, 3))
        + tuple(shift(b_out[k], Y, 4, k) for k in (1, 2, 3))
    )
    a = add_up([a_out[0], *arrived[:3]]).astype(BF16)
    b = add_up([b_out[0], *arrived[3:]]).astype(BF16)
    arrived = barrier(
        tuple(shift(block_y(a, k), Y, 4, k) for k in (1, 2, 3))
        + tuple(shift(block_x(b, k, HD), "x", 4, k) for k in (1, 2, 3))
    )
    a = add_up([block_y(a, 0), *arrived[:3]]).reshape(8, RA, HD)
    b = add_up([block_x(b, 0, HD), *arrived[3:]]).reshape(8, RA, HD)
    ab = jnp.concatenate([a, b], axis=1).astype(BF16)
    ab_parts = barrier(
        tuple(shift(pick(ab, lax.rem(z + k, 8), 0), "z", 8, k) for k in (4, 3, 5, 2, 6, 1, 7))
    )
    ab_sum = add_up([pick(ab, z, 0), *ab_parts])

    parts = barrier(tuple(shift(block_x(sum_z, k, 2 * HD), "x", 4, k) for k in (1, 2, 3)))
    s = add_up([block_x(sum_z, 0, 2 * HD), *parts]).astype(BF16)
    parts = barrier(tuple(shift(block_y(s, k), Y, 4, k) for k in (1, 2, 3)))
    s = add_up([block_y(s, 0), *parts])
    summed = jnp.concatenate([s, ab_sum], axis=0)

    hidden_grad = dot_nt(kv_grad[0], full_weight[:, : KVH * HD]) + dot_nt(
        kv_grad[1], full_weight[:, KVH * HD :]
    )
    weight_grad = summed / F32(total_tokens)
    new_moment_one = 0.9 * moment_one + 0.1 * weight_grad
    new_moment_two = 0.999 * moment_two + 0.001 * weight_grad * weight_grad
    first_hat = new_moment_one / (1.0 - 0.9**STEP)
    second_hat = new_moment_two / (1.0 - 0.999**STEP)
    new_master = master - 0.001 * (first_hat / (jnp.sqrt(second_hat) + 1e-08) + 0.1 * master)
    return (
        query_grad,
        hidden_grad.astype(BF16),
        new_master,
        new_moment_one,
        new_moment_two,
    )


def solution(mesh):
    names = ("x", "yh", "yl", "z", "c")
    fine = Mesh(mesh.devices.reshape(4, 2, 2, 8, 2), names)
    tokens = P(names, None)
    state = P(("yl", "z", "c"), ("x", "yh"))
    return jax.shard_map(
        body,
        mesh=fine,
        in_specs=(tokens,) * 6 + (P(("yl", "z", "c"), None), state, state, state),
        out_specs=(tokens, tokens, state, state, state),
        check_vma=False,
    )
```

time: 362 us -> 220 us (0.61)
  waiting for transfers between devices: 186 us -> 64.5 us
  blocking collectives: 78.7 us -> 0 us
  starting transfers between devices: 0.3 us -> 62.3 us
  local copies, waits for them, and re-layouts: 31.5 us -> 17.9 us
  Pallas kernels: 0 us -> 10.4 us
    reduce_scatter x1, waiting for transfers between devices: 124 us -> 0.01 us  [body(): sum_z = lax.psum_scatter(part_z, 'z', scatter_dimension=0, tiled=True)]
    psum x1 -> x0, blocking collectives: 78.7 us -> none  [body(): count = lax.psum(local_count, ('dp', 'fsdp'))]
    ppermute x0 -> x35, starting transfers between devices: none -> 62.2 us  [the longest x27 43.7 us: shift(): return lax.ppermute(v, axis, [(i, (i + k) % n) for i in range(n)])]
    unnamed x4 -> x2, waiting for transfers between devices: 61.2 us -> 0.7 us
    all_gather x1, waiting for transfers between devices: 0.01 us -> 34.2 us  [body(): lax.all_gather(kv_weight, ('yl', 'z', 'c'), axis=0, tiled=True)]
    ppermute x0 -> x35, waiting for transfers between devices: none -> 29.6 us  [the longest x27 16.3 us: shift(): return lax.ppermute(v, axis, [(i, (i + k) % n) for i in range(n)])]
    unnamed x29 -> x16, local copies, waits for them, and re-layouts: 23.7 us -> 3.04 us
    pallas_call x0 -> x1, Pallas kernels: none -> 10.4 us  [attention_backward(): pl.pallas_call(attention_kernel, grid=(KVH,), in_specs=[pl.BlockSpec((len...]
  transfers between devices with their start and end apart: 3 -> 37, of which waited for: 2 -> 14; matrix products, arithmetic and copies ran while one was open for 9% -> 27% of each run, Pallas kernels for 0% -> 5%
where the time goes in v1:
time: 220 us; the launch traced here: 217 us
  waiting for transfers between devices  64.5 us (29%)
  starting transfers between devices  62.3 us (28%)
  matrix products  32.6 us (15%)
  local copies, waits for them, and re-layouts  17.9 us (8%)
  between operations  15.8 us (7%)
  other arithmetic  13.2 us (6%)
  Pallas kernels  10.4 us (5%)
    ppermute x27, starting transfers between devices, shift(): return lax.ppermute(v, axis, [(i, (i + k) % n) for i in range(n)])  43.7 us
    all_gather x1, waiting for transfers between devices, body(): lax.all_gather(kv_weight, ('yl', 'z', 'c'), axis=0, tiled=True)  34.2 us
    ppermute x8, starting transfers between devices, swap(): return lax.ppermute(v, axis, [(i, i ^ bit) for i in range(n)])  18.5 us
    ppermute x27, waiting for transfers between devices, shift(): return lax.ppermute(v, axis, [(i, (i + k) % n) for i in range(n)])  16.3 us
    dot_general x2, matrix products, dot_nt(): lax.dot_general(a, b, (((1,), (1,)), ((), ())), preferred_element_type=F32)  13.4 us
    ppermute x8, waiting for transfers between devices, swap(): return lax.ppermute(v, axis, [(i, i ^ bit) for i in range(n)])  13.4 us
    pallas_call x1, Pallas kernels, attention_backward(): pl.pallas_call(attention_kernel, grid=(KVH,), in_specs=[pl.BlockSpec((len...  10.4 us
    concatenate x4, local copies, waits for them, and re-layouts, body(): pair = jnp.concatenate([pair[0], pair[1]], axis=1)  7.96 us
  transfers between devices with their start and end apart: 37, of which 14 were waited for; matrix products, arithmetic and copies ran while one was open for 27% of the time, Pallas kernels for 5%

profile of v1, /device:TPU:2, one launch (start us, length us, event | category | flops | bytes accessed | tf_op | source)
XLA Modules:
  0.0 216.6 jit_solution(14265546081354209571)
XLA Ops:
  13.3 3.0 %copy.25 = bf16[256,5120]{0,1:T(8,128)(2,1)S(1)} copy(bf16[256,5120]{1,0:T(8,128)(2,1)} %param.10) | data formatting | bytes 5242880 | tf_op args[0]
  17.0 2.4 %collective-permute-start.1 = (f32[8,128]{1,0:T(8,128)S(1)}, f32[8,128]{1,0:T(8,128)S(1)}, u32[]{:S(2)}, u32[]{:S(2)}) collective-permute-start(f32[8,128]{1,0:T(8,128)S(1)} %broadcast_add_fusion), channel_id=1, source_target_pairs={{0,64},{64,0},{128,192},{192,128},{1,65},{65,1},{129,193},{193,129... | collective-permute-start | bytes 12296 | tf_op jit(solution)/shard_map/ppermute | solution.py:44
  23.6 3.5 %collective-permute-done.2 = f32[8,128]{1,0:T(8,128)S(1)} collective-permute-done((f32[8,128]{1,0:T(8,128)S(1)}, f32[8,128]{1,0:T(8,128)S(1)}, u32[]{:S(2)}, u32[]{:S(2)}) %collective-permute-start.2) | collective-permute-done | bytes 4128 | tf_op jit(solution)/shard_map/ppermute | solution.py:44
  28.1 2.6 %collective-permute-done.3 = f32[8,128]{1,0:T(8,128)S(1)} collective-permute-done((f32[8,128]{1,0:T(8,128)S(1)}, f32[8,128]{1,0:T(8,128)S(1)}, u32[]{:S(2)}, u32[]{:S(2)}) %collective-permute-start.3) | collective-permute-done | bytes 4128 | tf_op jit(solution)/shard_map/ppermute | solution.py:44
  30.7 2.7 %collective-permute-start.4 = (f32[8,128]{1,0:T(8,128)S(1)}, f32[8,128]{1,0:T(8,128)S(1)}, u32[]{:S(2)}, u32[]{:S(2)}) collective-permute-start(f32[8,128]{1,0:T(8,128)S(1)} %add.299), channel_id=1, source_target_pairs={{0,32},{32,0},{1,33},{33,1},{2,34},{34,2},{3,35},{35,3},{4,36},{36... | collective-permute-start | bytes 12296 | tf_op jit(solution)/shard_map/ppermute | solution.py:44
  33.9 1.9 collective-permute-done.4
  37.2 2.3 %collective-permute-done.5 = f32[8,128]{1,0:T(8,128)S(1)} collective-permute-done((f32[8,128]{1,0:T(8,128)S(1)}, f32[8,128]{1,0:T(8,128)S(1)}, u32[]{:S(2)}, u32[]{:S(2)}) %collective-permute-start.5) | collective-permute-done | bytes 4128 | tf_op jit(solution)/shard_map/ppermute | solution.py:44
  39.5 2.7 %collective-permute-start.6 = (f32[8,128]{1,0:T(8,128)S(1)}, f32[8,128]{1,0:T(8,128)S(1)}, u32[]{:S(2)}, u32[]{:S(2)}) collective-permute-start(f32[8,128]{1,0:T(8,128)S(1)} %add.301), channel_id=1, source_target_pairs={{0,4},{2,6},{4,0},{6,2},{8,12},{10,14},{12,8},{14,10},{1,5},{3,7},... | collective-permute-start | bytes 12296 | tf_op jit(solution)/shard_map/ppermute | solution.py:44
  44.1 6.6 %collective-permute-start.7 = (f32[8,128]{1,0:T(8,128)S(1)}, f32[8,128]{1,0:T(8,128)S(1)}, u32[]{:S(2)}, u32[]{:S(2)}) collective-permute-start(f32[8,128]{1,0:T(8,128)S(1)} %add.302), channel_id=1, source_target_pairs={{0,8},{2,10},{4,12},{6,14},{8,0},{10,2},{12,4},{14,6},{1,9},{3,11}... | collective-permute-start | bytes 12296 | tf_op jit(solution)/shard_map/ppermute | solution.py:44
  53.8 34.2 %all-gather.2.cloned.1.call-done = bf16[5120,1024]{1,0:T(8,128)(2,1)} async-done(((bf16[160,1024]{1,0:T(8,128)(2,1)}), bf16[5120,1024]{1,0:T(8,128)(2,1)}) %all-gather.2.cloned.1.call-update) | async-done | bytes 10485776 | tf_op jit(solution)/shard_map/all_gather | solution.py:158
  88.0 6.4 %fusion.81.kpre.vpre = f32[256,1024]{1,0:T(8,128)S(1)} fusion(bf16[256,5120]{1,0:T(8,128)(2,1)} %param.10, bf16[5120,1024]{1,0:T(8,128)(2,1)} %all-gather.2.cloned.1.call-done), kind=kOutput, calls=%fused_computation.173 | convolution fusion | flops 2684354560 | bytes 14155776 | tf_op jit(solution)/shard_map/dot_general | solution.py:174
  94.4 10.4 %shard_map.137 = (bf16[256,2560]{1,0:T(8,128)(2,1)}, bf16[2,256,512]{2,1,0:T(8,128)(2,1)S(1)}) custom-call(f32[256,1024]{1,0:T(8,128)S(1)} %fusion.81.kpre.vpre, f32[256,1024]{1,0:T(8,128)S(1)} %fusion.81.kpre.vpre, bf16[256,2560]{1,0:T(8,128)(2,1)S(1)} %copy-done, bf16[256,2560]{1,0:T(8,128)(2,1)S(1)} %copy-done.1, f32[256,128]{1,0:T(8,128)S(1)} %get-tuple-element.97.cos, ...), custom_call_target="tpu_custom_call" | custom-call | tf_op jit(solution)/shard_map/pallas_call | solution.py:103
  107.9 2.6 %convolution_convert_fusion = bf16[1024,1024]{1,0:T(8,128)(2,1)} fusion(bf16[1024,512]{1,0:T(8,128)(2,1)S(1)} %bitcast.136, bf16[512,512]{1,0:T(8,128)(2,1)S(1)} %get-tuple-element.74, bf16[512,512]{1,0:T(8,128)(2,1)S(1)} %get-tuple-element.73), kind=kOutput, calls=%fused_computation.9 | convolution fusion | flops 1076887552 | bytes 4194304 | tf_op jit(solution)/shard_map/dot_general | solution.py:180
  118.4 2.1 collective-permute-start.18
  120.5 2.0 concatenate.48
  122.5 2.0 copy.27
  124.5 1.9 concatenate.49
  126.4 2.0 copy.28
  128.4 2.5 %fusion.13 = (bf16[512,4,1,128]{0,3,1,2:T(8,128)(2,1)}, bf16[512,4,1,128]{0,3,1,2:T(8,128)(2,1)S(1)}, bf16[512,4,1,128]{0,3,1,2:T(8,128)(2,1)S(1)}, bf16[512,4,1,128]{0,3,1,2:T(8,128)(2,1)S(1)}) fusion(s32[]{:T(128)S(6)} %select_n.181, bf16[512,2,2,128]{0,3,1,2:T(8,128)(2,1)} %copy.27, bf16[512,2,2,128]{0,3,1,2:T(8,128)(2,1)} %copy.28, s32[]{:T(128)S(6)} %select_n.178, ...), kind=kLoop, calls=%fused_computation.47 | loop fusion | flops 1048576 | bytes 3145744 | tf_op jit(solution)/shard_map/concatenate | solution.py:178
  134.0 2.9 %collective-permute-start.20 = (bf16[384,512]{1,0:T(8,128)(2,1)}, bf16[384,512]{1,0:T(8,128)(2,1)}, u32[]{:S(2)}, u32[]{:S(2)}) collective-permute-start(bf16[384,512]{1,0:T(8,128)(2,1)} %convolution_convert_fusion.3), channel_id=1, source_target_pairs={{0,32},{16,48},{32,0},{48,16},{1,33},{17,49},{33,1},{49,17},{2,34}... | collective-permute-start | bytes 1179656 | tf_op jit(solution)/shard_map/ppermute | solution.py:40
  141.0 4.1 %collective-permute-done.19 = bf16[384,512]{1,0:T(8,128)(2,1)S(1)} collective-permute-done((bf16[384,512]{1,0:T(8,128)(2,1)}, bf16[384,512]{1,0:T(8,128)(2,1)S(1)}, u32[]{:S(2)}, u32[]{:S(2)}) %collective-permute-start.19) | collective-permute-done | bytes 393248 | tf_op jit(solution)/shard_map/ppermute | solution.py:40
  145.0 7.9 %collective-permute-done.20 = bf16[384,512]{1,0:T(8,128)(2,1)} collective-permute-done((bf16[384,512]{1,0:T(8,128)(2,1)}, bf16[384,512]{1,0:T(8,128)(2,1)}, u32[]{:S(2)}, u32[]{:S(2)}) %collective-permute-start.20) | collective-permute-done | bytes 393248 | tf_op jit(solution)/shard_map/ppermute | solution.py:40
  155.9 1.9 collective-permute-start.22
  157.9 2.2 %collective-permute-start.23 = (bf16[384,128]{1,0:T(8,128)(2,1)S(1)}, bf16[384,128]{1,0:T(8,128)(2,1)S(1)}, u32[]{:S(2)}, u32[]{:S(2)}) collective-permute-start(bf16[384,128]{1,0:T(8,128)(2,1)S(1)} %get-tuple-element.80), channel_id=1, source_target_pairs={{0,32},{16,48},{32,0},{48,16},{1,33},{17,49},{33,1},{49,17},{2,34}... | collective-permute-start | bytes 294920 | tf_op jit(solution)/shard_map/ppermute | solution.py:40
  162.9 3.7 %collective-permute-start.26 = (bf16[384,128]{1,0:T(8,128)(2,1)S(1)}, bf16[384,128]{1,0:T(8,128)(2,1)S(1)}, u32[]{:S(2)}, u32[]{:S(2)}) collective-permute-start(bf16[384,128]{1,0:T(8,128)(2,1)S(1)} %get-tuple-element.77), channel_id=1, source_target_pairs={{0,128},{64,192},{128,0},{192,64},{1,129},{65,193},{129,1},{193,65... | collective-permute-start | bytes 294920 | tf_op jit(solution)/shard_map/ppermute | solution.py:40
  166.6 6.3 %fusion.2 = f32[256,5120]{1,0:T(8,128)} fusion(bf16[5120,1024]{1,0:T(8,128)(2,1)} %all-gather.2.cloned.1.call-done, bf16[2,256,512]{2,1,0:T(8,128)(2,1)S(1)} %get-tuple-element.33), kind=kOutput, calls=%fused_computation.3 | convolution fusion | flops 1342177280 | bytes 10747904 | tf_op jit(solution)/shard_map/dot_general | solution.py:57
  173.1 4.0 %collective-permute-start.28 = (bf16[96,128]{1,0:T(8,128)(2,1)S(1)}, bf16[96,128]{1,0:T(8,128)(2,1)S(1)}, u32[]{:S(2)}, u32[]{:S(2)}) collective-permute-start(bf16[96,128]{1,0:T(8,128)(2,1)S(1)} %get-tuple-element.86), channel_id=1, source_target_pairs={{0,8},{2,10},{4,12},{6,14},{8,0},{10,2},{12,4},{14,6},{1,9},{3,11}... | collective-permute-start | bytes 73736 | tf_op jit(solution)/shard_map/ppermute | solution.py:40
  178.5 3.7 %collective-permute-start.30 = (bf16[96,128]{1,0:T(8,128)(2,1)S(1)}, bf16[96,128]{1,0:T(8,128)(2,1)S(1)}, u32[]{:S(2)}, u32[]{:S(2)}) collective-permute-start(bf16[96,128]{1,0:T(8,128)(2,1)S(1)} %get-tuple-element.88), channel_id=1, source_target_pairs={{0,10},{2,12},{4,14},{6,0},{8,2},{10,4},{12,6},{14,8},{1,11},{3,13... | collective-permute-start | bytes 73736 | tf_op jit(solution)/shard_map/ppermute | solution.py:40
  183.3 3.1 %collective-permute-start.32 = (bf16[96,128]{1,0:T(8,128)(2,1)S(1)}, bf16[96,128]{1,0:T(8,128)(2,1)S(1)}, u32[]{:S(2)}, u32[]{:S(2)}) collective-permute-start(bf16[96,128]{1,0:T(8,128)(2,1)S(1)} %get-tuple-element.90), channel_id=1, source_target_pairs={{0,12},{2,14},{4,0},{6,2},{8,4},{10,6},{12,8},{14,10},{1,13},{3,15... | collective-permute-start | bytes 73736 | tf_op jit(solution)/shard_map/ppermute | solution.py:40
  188.1 2.5 %collective-permute-start.34 = (bf16[96,128]{1,0:T(8,128)(2,1)S(1)}, bf16[96,128]{1,0:T(8,128)(2,1)S(1)}, u32[]{:S(2)}, u32[]{:S(2)}) collective-permute-start(bf16[96,128]{1,0:T(8,128)(2,1)S(1)} %get-tuple-element.85), channel_id=1, source_target_pairs={{0,14},{2,0},{4,2},{6,4},{8,6},{10,8},{12,10},{14,12},{1,15},{3,1}... | collective-permute-start | bytes 73736 | tf_op jit(solution)/shard_map/ppermute | solution.py:40
  190.6 2.0 collective-permute-start.10
  194.9 7.1 %fusion = bf16[256,5120]{1,0:T(8,128)(2,1)} fusion(f32[256,5120]{1,0:T(8,128)} %fusion.2, bf16[5120,1024]{1,0:T(8,128)(2,1)} %all-gather.2.cloned.1.call-done, bf16[2,256,512]{2,1,0:T(8,128)(2,1)S(1)} %get-tuple-element.33), kind=kOutput, calls=%fused_computation.1 | convolution fusion | flops 1344798720 | bytes 13369344 | tf_op jit(solution)/shard_map/dot_general | solution.py:57
  (126 shorter events, 55.8 us)
Async XLA Ops:
  7.2 80.8 %all-gather.2.cloned.1.call-start = ((), (), s32[]{:S(2)}) async-start(), calls=%async_computation.1 | async-start | bytes 10813440 | tf_op jit(solution)/shard_map/all_gather | solution.py:158
  7.9 178.4 %reduce-scatter.2.cloned.1.call-start = ((), (), s32[]{:S(2)}) async-start(), calls=%async_computation.2 | async-start | bytes 2359296 | tf_op jit(solution)/shard_map/reduce_scatter | solution.py:181
  17.0 4.2 %collective-permute-start.1 = (f32[8,128]{1,0:T(8,128)S(1)}, f32[8,128]{1,0:T(8,128)S(1)}, u32[]{:S(2)}, u32[]{:S(2)}) collective-permute-start(f32[8,128]{1,0:T(8,128)S(1)} %broadcast_add_fusion), channel_id=1, source_target_pairs={{0,64},{64,0},{128,192},{192,128},{1,65},{65,1},{129,193},{193,129... | collective-permute-start | bytes 12296 | tf_op jit(solution)/shard_map/ppermute | solution.py:44
  21.0 84.0 %collective-permute-start.8 = (bf16[16,160,256]{2,1,0:T(8,128)(2,1)}, bf16[16,160,256]{2,1,0:T(8,128)(2,1)}, u32[]{:S(2)}, u32[]{:S(2)}) collective-permute-start(bf16[16,160,256]{2,1,0:T(8,128)(2,1)} %get-tuple-element.66), channel_id=1, source_target_pairs={{0,1},{1,0},{2,3},{3,2},{4,5},{5,4},{6,7},{7,6},{8,9},{9,8},{10,11... | collective-permute-start | bytes 3932168 | tf_op jit(solution)/shard_map/ppermute | solution.py:40
  21.9 5.2 %collective-permute-start.2 = (f32[8,128]{1,0:T(8,128)S(1)}, f32[8,128]{1,0:T(8,128)S(1)}, u32[]{:S(2)}, u32[]{:S(2)}) collective-permute-start(f32[8,128]{1,0:T(8,128)S(1)} %fusion.93), channel_id=1, source_target_pairs={{0,128},{64,192},{128,0},{192,64},{1,129},{65,193},{129,1},{193,65... | collective-permute-start | bytes 12296 | tf_op jit(solution)/shard_map/ppermute | solution.py:44
  30.7 5.1 %collective-permute-start.4 = (f32[8,128]{1,0:T(8,128)S(1)}, f32[8,128]{1,0:T(8,128)S(1)}, u32[]{:S(2)}, u32[]{:S(2)}) collective-permute-start(f32[8,128]{1,0:T(8,128)S(1)} %add.299), channel_id=1, source_target_pairs={{0,32},{32,0},{1,33},{33,1},{2,34},{34,2},{3,35},{35,3},{4,36},{36... | collective-permute-start | bytes 12296 | tf_op jit(solution)/shard_map/ppermute | solution.py:44
  39.5 4.6 %collective-permute-start.6 = (f32[8,128]{1,0:T(8,128)S(1)}, f32[8,128]{1,0:T(8,128)S(1)}, u32[]{:S(2)}, u32[]{:S(2)}) collective-permute-start(f32[8,128]{1,0:T(8,128)S(1)} %add.301), channel_id=1, source_target_pairs={{0,4},{2,6},{4,0},{6,2},{8,12},{10,14},{12,8},{14,10},{1,5},{3,7},... | collective-permute-start | bytes 12296 | tf_op jit(solution)/shard_map/ppermute | solution.py:44
  44.1 8.3 %collective-permute-start.7 = (f32[8,128]{1,0:T(8,128)S(1)}, f32[8,128]{1,0:T(8,128)S(1)}, u32[]{:S(2)}, u32[]{:S(2)}) collective-permute-start(f32[8,128]{1,0:T(8,128)S(1)} %add.302), channel_id=1, source_target_pairs={{0,8},{2,10},{4,12},{6,14},{8,0},{10,2},{12,4},{14,6},{1,9},{3,11}... | collective-permute-start | bytes 12296 | tf_op jit(solution)/shard_map/ppermute | solution.py:44
  113.2 24.8 %collective-permute-start.16 = (bf16[768,256]{1,0:T(8,128)(2,1)}, bf16[768,256]{1,0:T(8,128)(2,1)}, u32[]{:S(2)}, u32[]{:S(2)}) collective-permute-start(bf16[768,256]{1,0:T(8,128)(2,1)} %convolution_convert_fusion.7), channel_id=1, source_target_pairs={{0,64},{64,128},{128,192},{192,0},{1,65},{65,129},{129,193},{193,1... | collective-permute-start | bytes 1179656 | tf_op jit(solution)/shard_map/ppermute | solution.py:40
  115.8 25.2 %collective-permute-start.17 = (bf16[768,256]{1,0:T(8,128)(2,1)}, bf16[768,256]{1,0:T(8,128)(2,1)}, u32[]{:S(2)}, u32[]{:S(2)}) collective-permute-start(bf16[768,256]{1,0:T(8,128)(2,1)} %convolution_convert_fusion.6), channel_id=1, source_target_pairs={{0,128},{64,192},{128,0},{192,64},{1,129},{65,193},{129,1},{193,65... | collective-permute-start | bytes 1179656 | tf_op jit(solution)/shard_map/ppermute | solution.py:40
  118.4 22.6 %collective-permute-start.18 = (bf16[768,256]{1,0:T(8,128)(2,1)}, bf16[768,256]{1,0:T(8,128)(2,1)}, u32[]{:S(2)}, u32[]{:S(2)}) collective-permute-start(bf16[768,256]{1,0:T(8,128)(2,1)} %convolution_convert_fusion.5), channel_id=1, source_target_pairs={{0,192},{64,0},{128,64},{192,128},{1,193},{65,1},{129,65},{193,129... | collective-permute-start | bytes 1179656 | tf_op jit(solution)/shard_map/ppermute | solution.py:40
  132.1 12.9 %collective-permute-start.19 = (bf16[384,512]{1,0:T(8,128)(2,1)}, bf16[384,512]{1,0:T(8,128)(2,1)S(1)}, u32[]{:S(2)}, u32[]{:S(2)}) collective-permute-start(bf16[384,512]{1,0:T(8,128)(2,1)} %convolution_convert_fusion.4), channel_id=1, source_target_pairs={{0,16},{16,32},{32,48},{48,0},{1,17},{17,33},{33,49},{49,1},{2,18}... | collective-permute-start | bytes 1179656 | tf_op jit(solution)/shard_map/ppermute | solution.py:40
  134.0 18.9 %collective-permute-start.20 = (bf16[384,512]{1,0:T(8,128)(2,1)}, bf16[384,512]{1,0:T(8,128)(2,1)}, u32[]{:S(2)}, u32[]{:S(2)}) collective-permute-start(bf16[384,512]{1,0:T(8,128)(2,1)} %convolution_convert_fusion.3), channel_id=1, source_target_pairs={{0,32},{16,48},{32,0},{48,16},{1,33},{17,49},{33,1},{49,17},{2,34}... | collective-permute-start | bytes 1179656 | tf_op jit(solution)/shard_map/ppermute | solution.py:40
  138.1 16.1 %collective-permute-start.21 = (bf16[384,512]{1,0:T(8,128)(2,1)}, bf16[384,512]{1,0:T(8,128)(2,1)}, u32[]{:S(2)}, u32[]{:S(2)}) collective-permute-start(bf16[384,512]{1,0:T(8,128)(2,1)} %convolution_convert_fusion.2), channel_id=1, source_target_pairs={{0,48},{16,0},{32,16},{48,32},{1,49},{17,1},{33,17},{49,33},{2,50}... | collective-permute-start | bytes 1179656 | tf_op jit(solution)/shard_map/ppermute | solution.py:40
  155.9 10.6 %collective-permute-start.22 = (bf16[384,128]{1,0:T(8,128)(2,1)S(1)}, bf16[384,128]{1,0:T(8,128)(2,1)S(1)}, u32[]{:S(2)}, u32[]{:S(2)}) collective-permute-start(bf16[384,128]{1,0:T(8,128)(2,1)S(1)} %get-tuple-element.81), channel_id=1, source_target_pairs={{0,16},{16,32},{32,48},{48,0},{1,17},{17,33},{33,49},{49,1},{2,18}... | collective-permute-start | bytes 294920 | tf_op jit(solution)/shard_map/ppermute | solution.py:40
  157.9 15.0 %collective-permute-start.23 = (bf16[384,128]{1,0:T(8,128)(2,1)S(1)}, bf16[384,128]{1,0:T(8,128)(2,1)S(1)}, u32[]{:S(2)}, u32[]{:S(2)}) collective-permute-start(bf16[384,128]{1,0:T(8,128)(2,1)S(1)} %get-tuple-element.80), channel_id=1, source_target_pairs={{0,32},{16,48},{32,0},{48,16},{1,33},{17,49},{33,1},{49,17},{2,34}... | collective-permute-start | bytes 294920 | tf_op jit(solution)/shard_map/ppermute | solution.py:40
  160.1 12.8 %collective-permute-start.24 = (bf16[384,128]{1,0:T(8,128)(2,1)S(1)}, bf16[384,128]{1,0:T(8,128)(2,1)S(1)}, u32[]{:S(2)}, u32[]{:S(2)}) collective-permute-start(bf16[384,128]{1,0:T(8,128)(2,1)S(1)} %get-tuple-element.79), channel_id=1, source_target_pairs={{0,48},{16,0},{32,16},{48,32},{1,49},{17,1},{33,17},{49,33},{2,50}... | collective-permute-start | bytes 294920 | tf_op jit(solution)/shard_map/ppermute | solution.py:40
  162.6 10.3 %collective-permute-start.25 = (bf16[384,128]{1,0:T(8,128)(2,1)S(1)}, bf16[384,128]{1,0:T(8,128)(2,1)S(1)}, u32[]{:S(2)}, u32[]{:S(2)}) collective-permute-start(bf16[384,128]{1,0:T(8,128)(2,1)S(1)} %get-tuple-element.78), channel_id=1, source_target_pairs={{0,64},{64,128},{128,192},{192,0},{1,65},{65,129},{129,193},{193,1... | collective-permute-start | bytes 294920 | tf_op jit(solution)/shard_map/ppermute | solution.py:40
  162.9 10.0 %collective-permute-start.26 = (bf16[384,128]{1,0:T(8,128)(2,1)S(1)}, bf16[384,128]{1,0:T(8,128)(2,1)S(1)}, u32[]{:S(2)}, u32[]{:S(2)}) collective-permute-start(bf16[384,128]{1,0:T(8,128)(2,1)S(1)} %get-tuple-element.77), channel_id=1, source_target_pairs={{0,128},{64,192},{128,0},{192,64},{1,129},{65,193},{129,1},{193,65... | collective-permute-start | bytes 294920 | tf_op jit(solution)/shard_map/ppermute | solution.py:40
  166.6 6.4 %collective-permute-start.27 = (bf16[384,128]{1,0:T(8,128)(2,1)S(1)}, bf16[384,128]{1,0:T(8,128)(2,1)S(1)}, u32[]{:S(2)}, u32[]{:S(2)}) collective-permute-start(bf16[384,128]{1,0:T(8,128)(2,1)S(1)} %get-tuple-element.76), channel_id=1, source_target_pairs={{0,192},{64,0},{128,64},{192,128},{1,193},{65,1},{129,65},{193,129... | collective-permute-start | bytes 294920 | tf_op jit(solution)/shard_map/ppermute | solution.py:40
  173.1 14.1 %collective-permute-start.28 = (bf16[96,128]{1,0:T(8,128)(2,1)S(1)}, bf16[96,128]{1,0:T(8,128)(2,1)S(1)}, u32[]{:S(2)}, u32[]{:S(2)}) collective-permute-start(bf16[96,128]{1,0:T(8,128)(2,1)S(1)} %get-tuple-element.86), channel_id=1, source_target_pairs={{0,8},{2,10},{4,12},{6,14},{8,0},{10,2},{12,4},{14,6},{1,9},{3,11}... | collective-permute-start | bytes 73736 | tf_op jit(solution)/shard_map/ppermute | solution.py:40
  177.2 10.9 %collective-permute-start.29 = (bf16[96,128]{1,0:T(8,128)(2,1)S(1)}, bf16[96,128]{1,0:T(8,128)(2,1)S(1)}, u32[]{:S(2)}, u32[]{:S(2)}) collective-permute-start(bf16[96,128]{1,0:T(8,128)(2,1)S(1)} %get-tuple-element.87), channel_id=1, source_target_pairs={{0,6},{2,8},{4,10},{6,12},{8,14},{10,0},{12,2},{14,4},{1,7},{3,9},... | collective-permute-start | bytes 73736 | tf_op jit(solution)/shard_map/ppermute | solution.py:40
  178.5 12.1 %collective-permute-start.30 = (bf16[96,128]{1,0:T(8,128)(2,1)S(1)}, bf16[96,128]{1,0:T(8,128)(2,1)S(1)}, u32[]{:S(2)}, u32[]{:S(2)}) collective-permute-start(bf16[96,128]{1,0:T(8,128)(2,1)S(1)} %get-tuple-element.88), channel_id=1, source_target_pairs={{0,10},{2,12},{4,14},{6,0},{8,2},{10,4},{12,6},{14,8},{1,11},{3,13... | collective-permute-start | bytes 73736 | tf_op jit(solution)/shard_map/ppermute | solution.py:40
  182.2 10.4 %collective-permute-start.31 = (bf16[96,128]{1,0:T(8,128)(2,1)S(1)}, bf16[96,128]{1,0:T(8,128)(2,1)S(1)}, u32[]{:S(2)}, u32[]{:S(2)}) collective-permute-start(bf16[96,128]{1,0:T(8,128)(2,1)S(1)} %get-tuple-element.89), channel_id=1, source_target_pairs={{0,4},{2,6},{4,8},{6,10},{8,12},{10,14},{12,0},{14,2},{1,5},{3,7},... | collective-permute-start | bytes 73736 | tf_op jit(solution)/shard_map/ppermute | solution.py:40
  183.3 10.6 %collective-permute-start.32 = (bf16[96,128]{1,0:T(8,128)(2,1)S(1)}, bf16[96,128]{1,0:T(8,128)(2,1)S(1)}, u32[]{:S(2)}, u32[]{:S(2)}) collective-permute-start(bf16[96,128]{1,0:T(8,128)(2,1)S(1)} %get-tuple-element.90), channel_id=1, source_target_pairs={{0,12},{2,14},{4,0},{6,2},{8,4},{10,6},{12,8},{14,10},{1,13},{3,15... | collective-permute-start | bytes 73736 | tf_op jit(solution)/shard_map/ppermute | solution.py:40
  187.3 14.7 %collective-permute-start.33 = (bf16[96,128]{1,0:T(8,128)(2,1)S(1)}, bf16[96,128]{1,0:T(8,128)(2,1)S(1)}, u32[]{:S(2)}, u32[]{:S(2)}) collective-permute-start(bf16[96,128]{1,0:T(8,128)(2,1)S(1)} %fusion.58), channel_id=1, source_target_pairs={{0,2},{2,4},{4,6},{6,8},{8,10},{10,12},{12,14},{14,0},{1,3},{3,5},... | collective-permute-start | bytes 73736 | tf_op jit(solution)/shard_map/ppermute | solution.py:40
  188.1 13.9 %collective-permute-start.34 = (bf16[96,128]{1,0:T(8,128)(2,1)S(1)}, bf16[96,128]{1,0:T(8,128)(2,1)S(1)}, u32[]{:S(2)}, u32[]{:S(2)}) collective-permute-start(bf16[96,128]{1,0:T(8,128)(2,1)S(1)} %get-tuple-element.85), channel_id=1, source_target_pairs={{0,14},{2,0},{4,2},{6,4},{8,6},{10,8},{12,10},{14,12},{1,15},{3,1}... | collective-permute-start | bytes 73736 | tf_op jit(solution)/shard_map/ppermute | solution.py:40
  190.6 11.4 %collective-permute-start.10 = (bf16[128,256]{1,0:T(8,128)(2,1)S(1)}, bf16[128,256]{1,0:T(8,128)(2,1)S(1)}, u32[]{:S(2)}, u32[]{:S(2)}) collective-permute-start(bf16[128,256]{1,0:T(8,128)(2,1)S(1)} %get-tuple-element.84), channel_id=1, source_target_pairs={{0,64},{64,128},{128,192},{192,0},{1,65},{65,129},{129,193},{193,1... | collective-permute-start | bytes 196616 | tf_op jit(solution)/shard_map/ppermute | solution.py:40
  192.6 9.4 %collective-permute-start.11 = (bf16[128,256]{1,0:T(8,128)(2,1)S(1)}, bf16[128,256]{1,0:T(8,128)(2,1)S(1)}, u32[]{:S(2)}, u32[]{:S(2)}) collective-permute-start(bf16[128,256]{1,0:T(8,128)(2,1)S(1)} %get-tuple-element.83), channel_id=1, source_target_pairs={{0,128},{64,192},{128,0},{192,64},{1,129},{65,193},{129,1},{193,65... | collective-permute-start | bytes 196616 | tf_op jit(solution)/shard_map/ppermute | solution.py:40
  193.8 8.1 %collective-permute-start.12 = (bf16[128,256]{1,0:T(8,128)(2,1)S(1)}, bf16[128,256]{1,0:T(8,128)(2,1)S(1)}, u32[]{:S(2)}, u32[]{:S(2)}) collective-permute-start(bf16[128,256]{1,0:T(8,128)(2,1)S(1)} %get-tuple-element.82), channel_id=1, source_target_pairs={{0,192},{64,0},{128,64},{192,128},{1,193},{65,1},{129,65},{193,129... | collective-permute-start | bytes 196616 | tf_op jit(solution)/shard_map/ppermute | solution.py:40
  202.9 5.0 %collective-permute-start.13 = (bf16[64,128]{1,0:T(8,128)(2,1)S(1)}, bf16[64,128]{1,0:T(8,128)(2,1)S(1)}, u32[]{:S(2)}, u32[]{:S(2)}) collective-permute-start(bf16[64,128]{1,0:T(8,128)(2,1)S(1)} %get-tuple-element.93), channel_id=1, source_target_pairs={{0,16},{16,32},{32,48},{48,0},{1,17},{17,33},{33,49},{49,1},{2,18}... | collective-permute-start | bytes 49160 | tf_op jit(solution)/shard_map/ppermute | solution.py:40
  203.4 5.2 %collective-permute-start.14 = (bf16[64,128]{1,0:T(8,128)(2,1)S(1)}, bf16[64,128]{1,0:T(8,128)(2,1)S(1)}, u32[]{:S(2)}, u32[]{:S(2)}) collective-permute-start(bf16[64,128]{1,0:T(8,128)(2,1)S(1)} %get-tuple-element.92), channel_id=1, source_target_pairs={{0,32},{16,48},{32,0},{48,16},{1,33},{17,49},{33,1},{49,17},{2,34}... | collective-permute-start | bytes 49160 | tf_op jit(solution)/shard_map/ppermute | solution.py:40
  (12 other events, 205.5 us)
Sparse Core Ops, SparseCore 0:
  9.9 78.0 all-gather.1
  110.6 41.3 reduce-scatter.1

commit v2 on v1

--- a/solution.py
+++ b/solution.py
@@ -61,12 +61,14 @@
     return lax.dot_general(a, b, (((0,), (0,)), ((), ())), preferred_element_type=F32)
 
 
-def attention_kernel(kpre, vpre, q, up, cos, sin, start, weight, qg, kvg):
-    length = kpre.shape[0]
+def attention_kernel(hidden, wk, wv, q, up, cos, sin, start, weight, qg, kvg):
+    length = hidden.shape[0]
     cosine, sine = cos[...], sin[...]
-    kp = kpre[...]
+    both = jnp.concatenate([wk[...], wv[...]], axis=1)
+    pre = jnp.dot(hidden[...], both, preferred_element_type=F32)
+    kp = pre[:, :HD]
     k = (kp * cosine + pltpu.roll(kp, HD // 2, 1) * sine).astype(BF16)
-    v = vpre[...].astype(BF16)
+    v = pre[:, HD:].astype(BF16)
     key_index = lax.broadcasted_iota(jnp.int32, (length, length), 0)
     query_index = lax.broadcasted_iota(jnp.int32, (length, length), 1)
     allowed = (key_index >= start[...]) & (key_index <= query_index)
@@ -88,11 +90,12 @@
         dk = dk + jnp.dot(ds, qh, preferred_element_type=F32)
         dv = dv + jnp.dot(low, do, preferred_element_type=F32)
     dk = dk * SCALE
-    kvg[0] = (dk * cosine - pltpu.roll(dk, HD // 2, 1) * sine).astype(BF16)
-    kvg[1] = dv.astype(BF16)
-
-
-def attention_backward(kv_pre, queries, upstream, pos, weight):
+    at = pl.multiple_of(pl.program_id(0) * HD, HD)
+    kvg[:, pl.ds(at, HD)] = (dk * cosine - pltpu.roll(dk, HD // 2, 1) * sine).astype(BF16)
+    kvg[:, pl.ds(at + KVH * HD, HD)] = dv.astype(BF16)
+
+
+def attention_backward(hidden, full_weight, queries, upstream, pos, weight):
     length = pos.shape[0]
     freq = ROPE_BASE ** (-(jnp.arange(HD // 2, dtype=F32) * 2.0 / HD))
     angle = pos.astype(F32)[:, None] * freq[None, :]
@@ -104,8 +107,9 @@
         attention_kernel,
         grid=(KVH,),
         in_specs=[
-            pl.BlockSpec((length, HD), lambda h: (0, h)),
-            pl.BlockSpec((length, HD), lambda h: (0, h + KVH)),
+            whole(hidden.shape),
+            pl.BlockSpec((hidden.shape[1], HD), lambda h: (0, h)),
+            pl.BlockSpec((hidden.shape[1], HD), lambda h: (0, h + KVH)),
             pl.BlockSpec((length, GROUP * HD), lambda h: (0, h)),
             pl.BlockSpec((length, GROUP * HD), lambda h: (0, h)),
             whole((length, HD)),
@@ -115,14 +119,95 @@
         ],
         out_specs=[
             pl.BlockSpec((length, GROUP * HD), lambda h: (0, h)),
-            pl.BlockSpec((2, length, HD), lambda h: (0, 0, h)),
+            whole((length, 2 * KVH * HD)),
         ],
         out_shape=[
             jax.ShapeDtypeStruct((length, KVH * GROUP * HD), BF16),
-            jax.ShapeDtypeStruct((2, length, KVH * HD), BF16),
+            jax.ShapeDtypeStruct((length, 2 * KVH * HD), BF16),
         ],
         compiler_params=pltpu.CompilerParams(vmem_limit_bytes=32 * 2**20),
-    )(kv_pre, kv_pre, queries, upstream, cosine, sine, start, weight[:, None])
+    )(hidden, full_weight, full_weight, queries, upstream, cosine, sine, start, weight[:, None])
+
+
+def hidden_grad_kernel(kv, w, out):
+    out[...] = dot_nt(kv[...], w[...]).astype(BF16)
+
+
+def hidden_gradient(kv_grad, full_weight):
+    length, cols = kv_grad.shape
+    width = full_weight.shape[0]
+    block = width // 8
+    return pl.pallas_call(
+        hidden_grad_kernel,
+        grid=(8,),
+        in_specs=[
+            pl.BlockSpec((length, cols), lambda i: (0, 0)),
+            pl.BlockSpec((block, cols), lambda i: (i, 0)),
+        ],
+        out_specs=pl.BlockSpec((length, block), lambda i: (0, i)),
+        out_shape=jax.ShapeDtypeStruct((length, width), BF16),
+        compiler_params=pltpu.CompilerParams(vmem_limit_bytes=24 * 2**20),
+    )(kv_grad, full_weight)
+
+
+def terms_kernel(place, ha, hb, pair, *refs):
+    a_out, b_out, by_yh = refs[:4], refs[4:8], refs[8]
+    for yh in range(2):
+        for x in range(4):
+            block = (2 * x + yh) * HD
+            by_yh[yh, :, x * HD : (x + 1) * HD] = pair[:, block : block + HD]
+    for k in range(4):
+        at = pl.multiple_of(lax.rem(place[0] + k, 4) * 2 * HD, 2 * HD)
+        cols = pair[:, pl.ds(at, 2 * HD)]
+        a_out[k][...] = jnp.dot(ha[...], cols, preferred_element_type=F32).astype(BF16)
+    for k in range(4):
+        there = lax.rem(place[1] + k, 4)
+        yl, yh = lax.rem(there, 2), lax.div(there, 2)
+        b_out[k][...] = jnp.dot(hb[yl], by_yh[yh], preferred_element_type=F32).astype(BF16)
+
+
+VMEM = pl.BlockSpec(memory_space=pltpu.VMEM)
+SMEM = pl.BlockSpec(memory_space=pltpu.SMEM)
+
+
+def terms(place, ha, hb, pair):
+    a_shape = jax.ShapeDtypeStruct((ha.shape[0], 2 * HD), BF16)
+    b_shape = jax.ShapeDtypeStruct((hb.shape[1], 4 * HD), BF16)
+    return pl.pallas_call(
+        terms_kernel,
+        in_specs=[SMEM, VMEM, VMEM, VMEM],
+        out_specs=[VMEM] * 8,
+        out_shape=[a_shape] * 4 + [b_shape] * 4,
+        scratch_shapes=[pltpu.VMEM((2, pair.shape[0], 4 * HD), BF16)],
+        compiler_params=pltpu.CompilerParams(vmem_limit_bytes=24 * 2**20),
+    )(place, ha, hb, pair)
+
+
+def turn_kernel(place, *refs):
+    a_in, b_in, a_out, b_out, a_sum, b_sum = refs[:4], refs[4:8], refs[8:12], refs[12:16], *refs[16:]
+    a_sum[...] = add_up([r[...] for r in a_in]).astype(BF16)
+    b_sum[...] = add_up([r[...] for r in b_in]).astype(BF16)
+    half = a_sum.shape[0] // 2
+    for k in range(4):
+        there = lax.rem(place[1] + k, 4)
+        row = pl.multiple_of(lax.rem(there, 2) * half, half)
+        col = pl.multiple_of(lax.div(there, 2) * HD, HD)
+        a_out[k][...] = a_sum[pl.ds(row, half), pl.ds(col, HD)]
+        col = pl.multiple_of(lax.rem(place[0] + k, 4) * HD, HD)
+        b_out[k][...] = b_sum[:, pl.ds(col, HD)]
+
+
+def turn(place, a_in, b_in):
+    rows = b_in[0].shape[0]
+    shape = jax.ShapeDtypeStruct((rows, HD), BF16)
+    return pl.pallas_call(
+        turn_kernel,
+        in_specs=[SMEM] + [VMEM] * 8,
+        out_specs=[VMEM] * 8,
+        out_shape=[shape] * 8,
+        scratch_shapes=[pltpu.VMEM(a_in[0].shape, BF16), pltpu.VMEM(b_in[0].shape, BF16)],
+        compiler_params=pltpu.CompilerParams(vmem_limit_bytes=24 * 2**20),
+    )(place, *a_in, *b_in)
 
 
 def pick(v, index, axis):
@@ -171,23 +256,15 @@
     ha = hidden_pair[:, :, RZ : RZ + RA].reshape(16 * RA, 2 * length)
     hb = hidden_pair[:, :, RZ + RA :].reshape(2, 8 * RA, 2 * length)
 
-    kv_pre = jnp.dot(hidden, full_weight, preferred_element_type=F32)
-    query_grad, kv_grad = attention_backward(kv_pre, queries, upstream, pos, weight)
-    kv_sib = shift(kv_grad, "c", 2, 1)
-    pair = jnp.concatenate([kv_grad, kv_sib], axis=1)
-    pair = jnp.concatenate([pair[0], pair[1]], axis=1)
+    hidden, hz, ha, hb = barrier((hidden, hz, ha, hb))
+
+    query_grad, kv_grad = attention_backward(hidden, full_weight, queries, upstream, pos, weight)
+    pair = jnp.concatenate([kv_grad, shift(kv_grad, "c", 2, 1)], axis=0)
 
     part_z = jnp.dot(hz, pair, preferred_element_type=F32).astype(BF16)
     sum_z = lax.psum_scatter(part_z, "z", scatter_dimension=0, tiled=True)
 
-    def to_x(k):
-        cols = lax.dynamic_slice_in_dim(pair, lax.rem(x + k, 4) * 2 * HD, 2 * HD, axis=1)
-        return jnp.dot(ha, cols, preferred_element_type=F32).astype(BF16)
-
-    def to_y(k):
-        there = lax.rem(y + k, 4)
-        cols = pick(pair.reshape(2 * length, 4, 2, HD), there // 2, 2).reshape(2 * length, 4 * HD)
-        return jnp.dot(pick(hb, lax.rem(there, 2), 0), cols, preferred_element_type=F32).astype(BF16)
+    place = jnp.stack([x, y])
 
     def block_y(v, k):
         there = lax.rem(y + k, 4)
@@ -198,35 +275,35 @@
     def block_x(v, k, width):
         return lax.dynamic_slice_in_dim(v, lax.rem(x + k, 4) * width, width, axis=1)
 
-    a_out = [to_x(k) for k in (0, 1, 2, 3)]
-    b_out = [to_y(k) for k in (0, 1, 2, 3)]
+    out = barrier(tuple(terms(place, ha, hb, pair)) + (kv_grad,))
+    sent = tuple(shift(out[k], "x", 4, k) for k in (1, 2, 3))
+    sent += tuple(shift(out[4 + k], Y, 4, k) for k in (1, 2, 3))
+    hidden_grad = hidden_gradient(out[8], full_weight)
+    arrived = barrier(sent + (hidden_grad,))
+    hidden_grad = arrived[6]
+    out = turn(place, (out[0], *arrived[:3]), (out[4], *arrived[3:6]))
     arrived = barrier(
-        tuple(shift(a_out[k], "x", 4, k) for k in (1, 2, 3))
-        + tuple(shift(b_out[k], Y, 4, k) for k in (1, 2, 3))
-    )
-    a = add_up([a_out[0], *arrived[:3]]).astype(BF16)
-    b = add_up([b_out[0], *arrived[3:]]).astype(BF16)
+        tuple(shift(out[k], Y, 4, k) for k in (1, 2, 3))
+        + tuple(shift(out[4 + k], "x", 4, k) for k in (1, 2, 3))
+    )
+    a = add_up([out[0], *arrived[:3]]).reshape(8, RA, HD)
+    b = add_up([out[4], *arrived[3:]]).reshape(8, RA, HD)
+    ab = jnp.concatenate([a, b], axis=1).astype(BF16).reshape(2, 4, 2 * RA, HD)
+
+    ab, sum_z = barrier((ab, sum_z))
     arrived = barrier(
-        tuple(shift(block_y(a, k), Y, 4, k) for k in (1, 2, 3))
-        + tuple(shift(block_x(b, k, HD), "x", 4, k) for k in (1, 2, 3))
-    )
-    a = add_up([block_y(a, 0), *arrived[:3]]).reshape(8, RA, HD)
-    b = add_up([block_x(b, 0, HD), *arrived[3:]]).reshape(8, RA, HD)
-    ab = jnp.concatenate([a, b], axis=1).astype(BF16)
-    ab_parts = barrier(
-        tuple(shift(pick(ab, lax.rem(z + k, 8), 0), "z", 8, k) for k in (4, 3, 5, 2, 6, 1, 7))
-    )
-    ab_sum = add_up([pick(ab, z, 0), *ab_parts])
-
-    parts = barrier(tuple(shift(block_x(sum_z, k, 2 * HD), "x", 4, k) for k in (1, 2, 3)))
-    s = add_up([block_x(sum_z, 0, 2 * HD), *parts]).astype(BF16)
-    parts = barrier(tuple(shift(block_y(s, k), Y, 4, k) for k in (1, 2, 3)))
-    s = add_up([block_y(s, 0), *parts])
-    summed = jnp.concatenate([s, ab_sum], axis=0)
-
-    hidden_grad = dot_nt(kv_grad[0], full_weight[:, : KVH * HD]) + dot_nt(
-        kv_grad[1], full_weight[:, KVH * HD :]
-    )
+        (swap(pick(ab, 1 - z // 4, 0), "z", 8, 4),)
+        + tuple(shift(block_x(sum_z, k, 2 * HD), "x", 4, k) for k in (1, 2, 3))
+    )
+    ab = add_up([pick(ab, z // 4, 0), arrived[0]]).astype(BF16)
+    s = add_up([block_x(sum_z, 0, 2 * HD), *arrived[1:]]).astype(BF16)
+    arrived = barrier(
+        tuple(swap(pick(ab, lax.rem(z, 4) ^ k, 0), "z", 8, k) for k in (1, 2, 3))
+        + tuple(shift(block_y(s, k), Y, 4, k) for k in (1, 2, 3))
+    )
+    ab = add_up([pick(ab, lax.rem(z, 4), 0), *arrived[:3]])
+    s = add_up([block_y(s, 0), *arrived[3:]])
+    summed = jnp.concatenate([s, ab], axis=0)
     weight_grad = summed / F32(total_tokens)
     new_moment_one = 0.9 * moment_one + 0.1 * weight_grad
     new_moment_two = 0.999 * moment_two + 0.001 * weight_grad * weight_grad
@@ -235,7 +312,7 @@
     new_master = master - 0.001 * (first_hat / (jnp.sqrt(second_hat) + 1e-08) + 0.1 * master)
     return (
         query_grad,
-        hidden_grad.astype(BF16),
+        hidden_grad,
         new_master,
         new_moment_one,
         new_moment_two,

time: 220 us -> 205 us (0.932)
  matrix products: 32.6 us -> 2.66 us
  Pallas kernels: 10.4 us -> 30.4 us
  starting transfers between devices: 62.3 us -> 45.4 us
  local copies, waits for them, and re-layouts: 17.9 us -> 26.9 us
  waiting for transfers between devices: 64.5 us -> 71.6 us
  other arithmetic: 13.2 us -> 10.5 us
    dot_general x11 -> x0, matrix products: 30 us -> none  [the longest x2 13.4 us: dot_nt(): lax.dot_general(a, b, (((1,), (1,)), ((), ())), preferred_element_type=F32)]
    pallas_call x1 -> x4, Pallas kernels: 10.4 us -> 30.4 us  [the longest x1 20.6 us: attention_backward(): pl.pallas_call(attention_kernel, grid=(KVH,), in_specs=[whole(hidden.shap...]
    ppermute x27 -> x20, starting transfers between devices: 43.7 us -> 25.7 us  [shift(): return lax.ppermute(v, axis, [(i, (i + k) % n) for i in range(n)])]
    unnamed x16 -> x38, local copies, waits for them, and re-layouts: 3.04 us -> 18.9 us
    concatenate x5 -> x1, local copies, waits for them, and re-layouts: 7.99 us -> 0.03 us  [body(): pair = jnp.concatenate([kv_grad, shift(kv_grad, 'c', 2, 1)], axis=0)]
    all_gather x1, waiting for transfers between devices: 34.2 us -> 26.7 us  [body(): lax.all_gather(kv_weight, ('yl', 'z', 'c'), axis=0, tiled=True)]
    ppermute x8 -> x12, waiting for transfers between devices: 13.4 us -> 20.7 us  [swap(): return lax.ppermute(v, axis, [(i, i ^ bit) for i in range(n)])]
    ppermute x27 -> x20, waiting for transfers between devices: 16.3 us -> 23.4 us  [shift(): return lax.ppermute(v, axis, [(i, (i + k) % n) for i in range(n)])]
  transfers between devices with their start and end apart: 37 -> 34, of which waited for: 14 -> 17; matrix products, arithmetic and copies ran while one was open for 27% -> 10% of each run, Pallas kernels for 5% -> 5%
where the time goes in v2:
time: 205 us; the launch traced here: 203 us
  waiting for transfers between devices  71.6 us (35%)
  starting transfers between devices  45.4 us (22%)
  Pallas kernels  30.4 us (15%)
  local copies, waits for them, and re-layouts  26.9 us (13%)
  between operations  15.8 us (8%)
  other arithmetic  10.5 us (5%)
  matrix products  2.66 us (1%)
    all_gather x1, waiting for transfers between devices, body(): lax.all_gather(kv_weight, ('yl', 'z', 'c'), axis=0, tiled=True)  26.7 us
    ppermute x20, starting transfers between devices, shift(): return lax.ppermute(v, axis, [(i, (i + k) % n) for i in range(n)])  25.7 us
    ppermute x20, waiting for transfers between devices, shift(): return lax.ppermute(v, axis, [(i, (i + k) % n) for i in range(n)])  23.4 us
    ppermute x12, waiting for transfers between devices, swap(): return lax.ppermute(v, axis, [(i, i ^ bit) for i in range(n)])  20.7 us
    pallas_call x1, Pallas kernels, attention_backward(): pl.pallas_call(attention_kernel, grid=(KVH,), in_specs=[whole(hidden.shap...  20.6 us
    ppermute x12, starting transfers between devices, swap(): return lax.ppermute(v, axis, [(i, i ^ bit) for i in range(n)])  19.7 us
    unnamed x38, local copies, waits for them, and re-layouts  18.9 us
    pallas_call x1, Pallas kernels, hidden_gradient(): pl.pallas_call(hidden_grad_kernel, grid=(8,), in_specs=[pl.BlockSpec((len...  5.97 us
  transfers between devices with their start and end apart: 34, of which 17 were waited for; matrix products, arithmetic and copies ran while one was open for 10% of the time, Pallas kernels for 5%

profile of v2, /device:TPU:2, one launch (start us, length us, event | category | flops | bytes accessed | tf_op | source)
XLA Modules:
  0.0 203.2 jit_solution(17105797036701446465)
XLA Ops:
  13.3 4.4 %copy.28 = bf16[256,5120]{0,1:T(8,128)(2,1)} copy(bf16[256,5120]{1,0:T(8,128)(2,1)} %hidden) | data formatting | bytes 5242880 | tf_op args[0]
  18.4 2.4 %collective-permute-start.2 = (f32[8,128]{1,0:T(8,128)S(1)}, f32[8,128]{1,0:T(8,128)S(1)}, u32[]{:S(2)}, u32[]{:S(2)}) collective-permute-start(f32[8,128]{1,0:T(8,128)S(1)} %broadcast_add_fusion), channel_id=1, source_target_pairs={{0,64},{64,0},{128,192},{192,128},{1,65},{65,1},{129,193},{193,129... | collective-permute-start | bytes 12296 | tf_op jit(solution)/shard_map/ppermute | solution.py:44
  20.8 3.0 %dynamic-slice_bitcast_fusion = (bf16[16,160,256]{2,1,0:T(8,128)(2,1)}, bf16[16,1,160,256]{3,2,1,0:T(8,128)(2,1)S(1)}) fusion(bf16[16,2,160,256]{3,2,1,0:T(8,128)(2,1)} %bitcast.71, s32[]{:T(128)S(6)} %select_n.106, s32[]{:T(128)S(6)} %select_n.105), kind=kLoop, calls=%fused_computation.5 | loop fusion | bytes 5242888 | tf_op jit(solution)/shard_map/jit(dynamic_index_in_dim)/squeeze | solution.py:214
  25.4 4.4 %collective-permute-done.3 = f32[8,128]{1,0:T(8,128)S(1)} collective-permute-done((f32[8,128]{1,0:T(8,128)S(1)}, f32[8,128]{1,0:T(8,128)S(1)}, u32[]{:S(2)}, u32[]{:S(2)}) %collective-permute-start.3) | collective-permute-done | bytes 4128 | tf_op jit(solution)/shard_map/ppermute | solution.py:44
  29.8 3.6 %collective-permute-done.4 = f32[8,128]{1,0:T(8,128)S(1)} collective-permute-done((f32[8,128]{1,0:T(8,128)S(1)}, f32[8,128]{1,0:T(8,128)S(1)}, u32[]{:S(2)}, u32[]{:S(2)}) %collective-permute-start.4) | collective-permute-done | bytes 4128 | tf_op jit(solution)/shard_map/ppermute | solution.py:44
  35.4 3.1 %collective-permute-done.5 = f32[8,128]{1,0:T(8,128)S(1)} collective-permute-done((f32[8,128]{1,0:T(8,128)S(1)}, f32[8,128]{1,0:T(8,128)S(1)}, u32[]{:S(2)}, u32[]{:S(2)}) %collective-permute-start.5) | collective-permute-done | bytes 4128 | tf_op jit(solution)/shard_map/ppermute | solution.py:44
  38.7 3.5 %collective-permute-done.6 = f32[8,128]{1,0:T(8,128)S(1)} collective-permute-done((f32[8,128]{1,0:T(8,128)S(1)}, f32[8,128]{1,0:T(8,128)S(1)}, u32[]{:S(2)}, u32[]{:S(2)}) %collective-permute-start.6) | collective-permute-done | bytes 4128 | tf_op jit(solution)/shard_map/ppermute | solution.py:44
  44.4 2.4 %collective-permute-done.7 = f32[8,128]{1,0:T(8,128)S(1)} collective-permute-done((f32[8,128]{1,0:T(8,128)S(1)}, f32[8,128]{1,0:T(8,128)S(1)}, u32[]{:S(2)}, u32[]{:S(2)}) %collective-permute-start.7) | collective-permute-done | bytes 4128 | tf_op jit(solution)/shard_map/ppermute | solution.py:44
  46.8 5.4 %collective-permute-start.8 = (f32[8,128]{1,0:T(8,128)S(1)}, f32[8,128]{1,0:T(8,128)S(1)}, u32[]{:S(2)}, u32[]{:S(2)}) collective-permute-start(f32[8,128]{1,0:T(8,128)S(1)} %add.196), channel_id=1, source_target_pairs={{0,8},{2,10},{4,12},{6,14},{8,0},{10,2},{12,4},{14,6},{1,9},{3,11}... | collective-permute-start | bytes 12296 | tf_op jit(solution)/shard_map/ppermute | solution.py:44
  52.6 1.8 collective-permute-done.8
  58.6 2.5 %pad_maximum_fusion = (bf16[2,8,48,512]{3,2,1,0:T(8,128)(2,1)S(1)}, bf16[2,8,48,512]{3,2,1,0:T(8,128)(2,1)}) fusion(bf16[2,8,160,256]{3,2,1,0:T(8,128)(2,1)} %bitcast.73, bf16[2,8,160,256]{3,2,1,0:T(8,128)(2,1)} %bitcast.70), kind=kLoop, calls=%fused_computation.9 | loop fusion | flops 3145728 | bytes 4194304 | tf_op jit(solution)/shard_map/concatenate | solution.py:254
  61.1 26.7 %all-gather.2.cloned.1.call-done.wk.wv.w = bf16[5120,1024]{1,0:T(8,128)(2,1)} async-done(((bf16[160,1024]{1,0:T(8,128)(2,1)}), bf16[5120,1024]{1,0:T(8,128)(2,1)}) %all-gather.2.cloned.1.call-update) | async-done | bytes 10485776 | tf_op jit(solution)/shard_map/all_gather | solution.py:243
  87.8 4.0 %copy-done = bf16[5120,1024]{1,0:T(8,128)(2,1)S(1)} copy-done((bf16[5120,1024]{1,0:T(8,128)(2,1)S(1)}, bf16[5120,1024]{1,0:T(8,128)(2,1)}, u32[]{:S(2)}) %copy-start) | copy-done | bytes 10485784
  96.2 20.6 %shard_map.137 = (bf16[256,2560]{1,0:T(8,128)(2,1)}, bf16[256,1024]{1,0:T(8,128)(2,1)S(1)}) custom-call(bf16[256,5120]{1,0:T(8,128)(2,1)S(1)} %copy-done.2, bf16[5120,1024]{1,0:T(8,128)(2,1)S(1)} %copy-done, bf16[5120,1024]{1,0:T(8,128)(2,1)S(1)} %copy-done, bf16[256,2560]{1,0:T(8,128)(2,1)S(1)} %copy-done.6, bf16[256,2560]{1,0:T(8,128)(2,1)S(1)} %copy-done.7, ...), custom_call_target="tpu_custom_call" | custom-call | tf_op jit(solution)/shard_map/pallas_call | solution.py:106
  118.8 2.7 %convolution_convert_fusion = bf16[1024,1024]{1,0:T(8,128)(2,1)} fusion(bf16[1024,512]{1,0:T(8,128)(2,1)S(1)} %bitcast.74, bf16[512,1024]{1,0:T(8,128)(2,1)S(1)} %constant_dynamic-update-slice_fusion.pair), kind=kOutput, calls=%fused_computation.4 | convolution fusion | flops 1074790400 | bytes 4194304 | tf_op jit(solution)/shard_map/dot_general | solution.py:264
  122.5 2.5 %shard_map.138 = (bf16[768,256]{1,0:T(8,128)(2,1)S(1)}, bf16[768,256]{1,0:T(8,128)(2,1)S(1)}, bf16[768,256]{1,0:T(8,128)(2,1)S(1)}, bf16[768,256]{1,0:T(8,128)(2...) custom-call(s32[2]{0:T(128)S(1)} %pad_add_fusion.place, ...), custom_call_target="tpu_custom_call" | custom-call | tf_op jit(solution)/shard_map/pallas_call | solution.py:176
  125.0 1.9 collective-permute-start.10
  128.0 2.0 collective-permute-start.12
  131.0 2.7 %collective-permute-start.14 = (bf16[384,512]{1,0:T(8,128)(2,1)S(1)}, bf16[384,512]{1,0:T(8,128)(2,1)S(1)}, u32[]{:S(2)}, u32[]{:S(2)}) collective-permute-start(bf16[384,512]{1,0:T(8,128)(2,1)S(1)} %get-tuple-element.78), channel_id=1, source_target_pairs={{0,32},{16,48},{32,0},{48,16},{1,33},{17,49},{33,1},{49,17},{2,34}... | collective-permute-start | bytes 1179656 | tf_op jit(solution)/shard_map/ppermute | solution.py:40
  133.7 10.5 %collective-permute-done.10.refs_1_ = bf16[768,256]{1,0:T(8,128)(2,1)S(1)} collective-permute-done((bf16[768,256]{1,0:T(8,128)(2,1)S(1)}, bf16[768,256]{1,0:T(8,128)(2,1)S(1)}, u32[]{:S(2)}, u32[]{:S(2)}) %collective-permute-start.10) | collective-permute-done | bytes 393248 | tf_op jit(solution)/shard_map/ppermute | solution.py:40
  144.2 2.3 %collective-permute-start.15 = (bf16[384,512]{1,0:T(8,128)(2,1)S(1)}, bf16[384,512]{1,0:T(8,128)(2,1)S(1)}, u32[]{:S(2)}, u32[]{:S(2)}) collective-permute-start(bf16[384,512]{1,0:T(8,128)(2,1)S(1)} %get-tuple-element.79), channel_id=1, source_target_pairs={{0,48},{16,0},{32,16},{48,32},{1,49},{17,1},{33,17},{49,33},{2,50}... | collective-permute-start | bytes 1179656 | tf_op jit(solution)/shard_map/ppermute | solution.py:40
  146.4 4.1 %copy-done.1 = bf16[5120,1024]{1,0:T(8,128)(2,1)S(1)} copy-done((bf16[5120,1024]{1,0:T(8,128)(2,1)S(1)}, bf16[5120,1024]{1,0:T(8,128)(2,1)}, u32[]{:S(2)}) %copy-start.1) | copy-done | bytes 10485784
  150.5 6.0 %shard_map.139 = bf16[256,5120]{1,0:T(8,128)(2,1)} custom-call(bf16[256,1024]{1,0:T(8,128)(2,1)S(1)} %copy-done.5, bf16[5120,1024]{1,0:T(8,128)(2,1)S(1)} %copy-done.1), custom_call_target="tpu_custom_call" | custom-call | tf_op jit(solution)/shard_map/pallas_call | solution.py:140
  161.3 2.4 %collective-permute-start.19 = (bf16[384,128]{1,0:T(8,128)(2,1)S(1)}, bf16[384,128]{1,0:T(8,128)(2,1)S(1)}, u32[]{:S(2)}, u32[]{:S(2)}) collective-permute-start(bf16[384,128]{1,0:T(8,128)(2,1)S(1)} %get-tuple-element.94), channel_id=1, source_target_pairs={{0,64},{64,128},{128,192},{192,0},{1,65},{65,129},{129,193},{193,1... | collective-permute-start | bytes 294920 | tf_op jit(solution)/shard_map/ppermute | solution.py:40
  165.9 4.0 %collective-permute-done.20 = bf16[384,128]{1,0:T(8,128)(2,1)S(1)} collective-permute-done((bf16[384,128]{1,0:T(8,128)(2,1)S(1)}, bf16[384,128]{1,0:T(8,128)(2,1)S(1)}, u32[]{:S(2)}, u32[]{:S(2)}) %collective-permute-start.20) | collective-permute-done | bytes 98336 | tf_op jit(solution)/shard_map/ppermute | solution.py:40
  174.5 2.5 %collective-permute-start.25 = (bf16[128,256]{1,0:T(8,128)(2,1)S(1)}, bf16[128,256]{1,0:T(8,128)(2,1)S(1)}, u32[]{:S(2)}, u32[]{:S(2)}) collective-permute-start(bf16[128,256]{1,0:T(8,128)(2,1)S(1)} %get-tuple-element.126), channel_id=1, source_target_pairs={{0,192},{64,0},{128,64},{192,128},{1,193},{65,1},{129,65},{193,129... | collective-permute-start | bytes 196616 | tf_op jit(solution)/shard_map/ppermute | solution.py:40
  177.1 2.1 %collective-permute-done.24 = bf16[128,256]{1,0:T(8,128)(2,1)S(1)} collective-permute-done((bf16[128,256]{1,0:T(8,128)(2,1)S(1)}, bf16[128,256]{1,0:T(8,128)(2,1)S(1)}, u32[]{:S(2)}, u32[]{:S(2)}) %collective-permute-start.24) | collective-permute-done | bytes 65568 | tf_op jit(solution)/shard_map/ppermute | solution.py:40
  179.5 1.9 collective-permute-done.22
  182.4 5.4 %collective-permute-start.26 = (bf16[96,128]{1,0:T(8,128)(2,1)S(1)}, bf16[96,128]{1,0:T(8,128)(2,1)S(1)}, u32[]{:S(2)}, u32[]{:S(2)}) collective-permute-start(bf16[96,128]{1,0:T(8,128)(2,1)S(1)} %get-tuple-element.131), channel_id=1, source_target_pairs={{0,2},{2,0},{4,6},{6,4},{8,10},{10,8},{12,14},{14,12},{1,3},{3,1},... | collective-permute-start | bytes 73736 | tf_op jit(solution)/shard_map/ppermute | solution.py:44
  187.8 2.5 %collective-permute-start.28 = (bf16[96,128]{1,0:T(8,128)(2,1)S(1)}, bf16[96,128]{1,0:T(8,128)(2,1)S(1)}, u32[]{:S(2)}, u32[]{:S(2)}) collective-permute-start(bf16[96,128]{1,0:T(8,128)(2,1)S(1)} %get-tuple-element.129), channel_id=1, source_target_pairs={{0,6},{2,4},{4,2},{6,0},{8,14},{10,12},{12,10},{14,8},{1,7},{3,5},... | collective-permute-start | bytes 73736 | tf_op jit(solution)/shard_map/ppermute | solution.py:44
  190.3 2.7 %collective-permute-start.31 = (bf16[64,128]{1,0:T(8,128)(2,1)S(1)}, bf16[64,128]{1,0:T(8,128)(2,1)S(1)}, u32[]{:S(2)}, u32[]{:S(2)}) collective-permute-start(bf16[64,128]{1,0:T(8,128)(2,1)S(1)} %get-tuple-element.132), channel_id=1, source_target_pairs={{0,48},{16,0},{32,16},{48,32},{1,49},{17,1},{33,17},{49,33},{2,50}... | collective-permute-start | bytes 49160 | tf_op jit(solution)/shard_map/ppermute | solution.py:40
  193.0 2.5 %collective-permute-done.30 = bf16[64,128]{1,0:T(8,128)(2,1)S(1)} collective-permute-done((bf16[64,128]{1,0:T(8,128)(2,1)S(1)}, bf16[64,128]{1,0:T(8,128)(2,1)S(1)}, u32[]{:S(2)}, u32[]{:S(2)}) %collective-permute-start.30) | collective-permute-done | bytes 16416 | tf_op jit(solution)/shard_map/ppermute | solution.py:40
  (128 shorter events, 39.2 us)
Async XLA Ops:
  7.2 80.6 %all-gather.2.cloned.1.call-start = ((), (), s32[]{:S(2)}) async-start(), calls=%async_computation.1 | async-start | bytes 10813440 | tf_op jit(solution)/shard_map/all_gather | solution.py:243
  7.9 163.2 %reduce-scatter.2.cloned.1.call-start = ((), (), s32[]{:S(2)}) async-start(), calls=%async_computation.2 | async-start | bytes 2359296 | tf_op jit(solution)/shard_map/reduce_scatter | solution.py:265
  13.2 4.5 %collective-permute-start.1 = (f32[8,128]{1,0:T(8,128)S(1)}, f32[8,128]{1,0:T(8,128)S(1)}, u32[]{:S(2)}, u32[]{:S(2)}) collective-permute-start(f32[8,128]{1,0:T(8,128)S(1)} %broadcast_in_dim.57), channel_id=1, source_target_pairs={{0,1},{1,0},{2,3},{3,2},{4,5},{5,4},{6,7},{7,6},{8,9},{9,8},{10,11... | collective-permute-start | bytes 12296 | tf_op jit(solution)/shard_map/ppermute | solution.py:44
  18.4 5.5 %collective-permute-start.2 = (f32[8,128]{1,0:T(8,128)S(1)}, f32[8,128]{1,0:T(8,128)S(1)}, u32[]{:S(2)}, u32[]{:S(2)}) collective-permute-start(f32[8,128]{1,0:T(8,128)S(1)} %broadcast_add_fusion), channel_id=1, source_target_pairs={{0,64},{64,0},{128,192},{192,128},{1,65},{65,1},{129,193},{193,129... | collective-permute-start | bytes 12296 | tf_op jit(solution)/shard_map/ppermute | solution.py:44
  23.7 32.8 %collective-permute-start = (bf16[16,160,256]{2,1,0:T(8,128)(2,1)}, bf16[16,160,256]{2,1,0:T(8,128)(2,1)S(1)}, u32[]{:S(2)}, u32[]{:S(2)}) collective-permute-start(bf16[16,160,256]{2,1,0:T(8,128)(2,1)} %get-tuple-element.124), channel_id=1, source_target_pairs={{0,1},{1,0},{2,3},{3,2},{4,5},{5,4},{6,7},{7,6},{8,9},{9,8},{10,11... | collective-permute-start | bytes 3932168 | tf_op jit(solution)/shard_map/ppermute | solution.py:40
  24.6 5.2 %collective-permute-start.3 = (f32[8,128]{1,0:T(8,128)S(1)}, f32[8,128]{1,0:T(8,128)S(1)}, u32[]{:S(2)}, u32[]{:S(2)}) collective-permute-start(f32[8,128]{1,0:T(8,128)S(1)} %fusion.14), channel_id=1, source_target_pairs={{0,128},{64,192},{128,0},{192,64},{1,129},{65,193},{129,1},{193,65... | collective-permute-start | bytes 12296 | tf_op jit(solution)/shard_map/ppermute | solution.py:44
  29.8 3.6 %collective-permute-start.4 = (f32[8,128]{1,0:T(8,128)S(1)}, f32[8,128]{1,0:T(8,128)S(1)}, u32[]{:S(2)}, u32[]{:S(2)}) collective-permute-start(f32[8,128]{1,0:T(8,128)S(1)} %add.192), channel_id=1, source_target_pairs={{0,16},{16,0},{1,17},{17,1},{2,18},{18,2},{3,19},{19,3},{4,20},{20... | collective-permute-start | bytes 12296 | tf_op jit(solution)/shard_map/ppermute | solution.py:44
  33.4 5.1 %collective-permute-start.5 = (f32[8,128]{1,0:T(8,128)S(1)}, f32[8,128]{1,0:T(8,128)S(1)}, u32[]{:S(2)}, u32[]{:S(2)}) collective-permute-start(f32[8,128]{1,0:T(8,128)S(1)} %add.193), channel_id=1, source_target_pairs={{0,32},{32,0},{1,33},{33,1},{2,34},{34,2},{3,35},{35,3},{4,36},{36... | collective-permute-start | bytes 12296 | tf_op jit(solution)/shard_map/ppermute | solution.py:44
  42.2 4.6 %collective-permute-start.7 = (f32[8,128]{1,0:T(8,128)S(1)}, f32[8,128]{1,0:T(8,128)S(1)}, u32[]{:S(2)}, u32[]{:S(2)}) collective-permute-start(f32[8,128]{1,0:T(8,128)S(1)} %add.195), channel_id=1, source_target_pairs={{0,4},{2,6},{4,0},{6,2},{8,12},{10,14},{12,8},{14,10},{1,5},{3,7},... | collective-permute-start | bytes 12296 | tf_op jit(solution)/shard_map/ppermute | solution.py:44
  46.8 7.6 %collective-permute-start.8 = (f32[8,128]{1,0:T(8,128)S(1)}, f32[8,128]{1,0:T(8,128)S(1)}, u32[]{:S(2)}, u32[]{:S(2)}) collective-permute-start(f32[8,128]{1,0:T(8,128)S(1)} %add.196), channel_id=1, source_target_pairs={{0,8},{2,10},{4,12},{6,14},{8,0},{10,2},{12,4},{14,6},{1,9},{3,11}... | collective-permute-start | bytes 12296 | tf_op jit(solution)/shard_map/ppermute | solution.py:44
  125.0 19.1 %collective-permute-start.10 = (bf16[768,256]{1,0:T(8,128)(2,1)S(1)}, bf16[768,256]{1,0:T(8,128)(2,1)S(1)}, u32[]{:S(2)}, u32[]{:S(2)}) collective-permute-start(bf16[768,256]{1,0:T(8,128)(2,1)S(1)} %get-tuple-element.74), channel_id=1, source_target_pairs={{0,64},{64,128},{128,192},{192,0},{1,65},{65,129},{129,193},{193,1... | collective-permute-start | bytes 1179656 | tf_op jit(solution)/shard_map/ppermute | solution.py:40
  126.9 29.5 %collective-permute-start.11 = (bf16[768,256]{1,0:T(8,128)(2,1)S(1)}, bf16[768,256]{1,0:T(8,128)(2,1)S(1)}, u32[]{:S(2)}, u32[]{:S(2)}) collective-permute-start(bf16[768,256]{1,0:T(8,128)(2,1)S(1)} %get-tuple-element.75), channel_id=1, source_target_pairs={{0,128},{64,192},{128,0},{192,64},{1,129},{65,193},{129,1},{193,65... | collective-permute-start | bytes 1179656 | tf_op jit(solution)/shard_map/ppermute | solution.py:40
  128.0 28.5 %collective-permute-start.12 = (bf16[768,256]{1,0:T(8,128)(2,1)S(1)}, bf16[768,256]{1,0:T(8,128)(2,1)S(1)}, u32[]{:S(2)}, u32[]{:S(2)}) collective-permute-start(bf16[768,256]{1,0:T(8,128)(2,1)S(1)} %get-tuple-element.76), channel_id=1, source_target_pairs={{0,192},{64,0},{128,64},{192,128},{1,193},{65,1},{129,65},{193,129... | collective-permute-start | bytes 1179656 | tf_op jit(solution)/shard_map/ppermute | solution.py:40
  130.0 26.5 %collective-permute-start.13 = (bf16[384,512]{1,0:T(8,128)(2,1)S(1)}, bf16[384,512]{1,0:T(8,128)(2,1)S(1)}, u32[]{:S(2)}, u32[]{:S(2)}) collective-permute-start(bf16[384,512]{1,0:T(8,128)(2,1)S(1)} %get-tuple-element.77), channel_id=1, source_target_pairs={{0,16},{16,32},{32,48},{48,0},{1,17},{17,33},{33,49},{49,1},{2,18}... | collective-permute-start | bytes 1179656 | tf_op jit(solution)/shard_map/ppermute | solution.py:40
  131.0 25.5 %collective-permute-start.14 = (bf16[384,512]{1,0:T(8,128)(2,1)S(1)}, bf16[384,512]{1,0:T(8,128)(2,1)S(1)}, u32[]{:S(2)}, u32[]{:S(2)}) collective-permute-start(bf16[384,512]{1,0:T(8,128)(2,1)S(1)} %get-tuple-element.78), channel_id=1, source_target_pairs={{0,32},{16,48},{32,0},{48,16},{1,33},{17,49},{33,1},{49,17},{2,34}... | collective-permute-start | bytes 1179656 | tf_op jit(solution)/shard_map/ppermute | solution.py:40
  144.2 12.3 %collective-permute-start.15 = (bf16[384,512]{1,0:T(8,128)(2,1)S(1)}, bf16[384,512]{1,0:T(8,128)(2,1)S(1)}, u32[]{:S(2)}, u32[]{:S(2)}) collective-permute-start(bf16[384,512]{1,0:T(8,128)(2,1)S(1)} %get-tuple-element.79), channel_id=1, source_target_pairs={{0,48},{16,0},{32,16},{48,32},{1,49},{17,1},{33,17},{49,33},{2,50}... | collective-permute-start | bytes 1179656 | tf_op jit(solution)/shard_map/ppermute | solution.py:40
  157.9 7.0 %collective-permute-start.16 = (bf16[384,128]{1,0:T(8,128)(2,1)S(1)}, bf16[384,128]{1,0:T(8,128)(2,1)S(1)}, u32[]{:S(2)}, u32[]{:S(2)}) collective-permute-start(bf16[384,128]{1,0:T(8,128)(2,1)S(1)} %get-tuple-element.91), channel_id=1, source_target_pairs={{0,16},{16,32},{32,48},{48,0},{1,17},{17,33},{33,49},{49,1},{2,18}... | collective-permute-start | bytes 294920 | tf_op jit(solution)/shard_map/ppermute | solution.py:40
  158.0 7.8 %collective-permute-start.17 = (bf16[384,128]{1,0:T(8,128)(2,1)S(1)}, bf16[384,128]{1,0:T(8,128)(2,1)S(1)}, u32[]{:S(2)}, u32[]{:S(2)}) collective-permute-start(bf16[384,128]{1,0:T(8,128)(2,1)S(1)} %get-tuple-element.92), channel_id=1, source_target_pairs={{0,32},{16,48},{32,0},{48,16},{1,33},{17,49},{33,1},{49,17},{2,34}... | collective-permute-start | bytes 294920 | tf_op jit(solution)/shard_map/ppermute | solution.py:40
  159.5 6.3 %collective-permute-start.18 = (bf16[384,128]{1,0:T(8,128)(2,1)S(1)}, bf16[384,128]{1,0:T(8,128)(2,1)S(1)}, u32[]{:S(2)}, u32[]{:S(2)}) collective-permute-start(bf16[384,128]{1,0:T(8,128)(2,1)S(1)} %get-tuple-element.93), channel_id=1, source_target_pairs={{0,48},{16,0},{32,16},{48,32},{1,49},{17,1},{33,17},{49,33},{2,50}... | collective-permute-start | bytes 294920 | tf_op jit(solution)/shard_map/ppermute | solution.py:40
  161.3 4.7 %collective-permute-start.19 = (bf16[384,128]{1,0:T(8,128)(2,1)S(1)}, bf16[384,128]{1,0:T(8,128)(2,1)S(1)}, u32[]{:S(2)}, u32[]{:S(2)}) collective-permute-start(bf16[384,128]{1,0:T(8,128)(2,1)S(1)} %get-tuple-element.94), channel_id=1, source_target_pairs={{0,64},{64,128},{128,192},{192,0},{1,65},{65,129},{129,193},{193,1... | collective-permute-start | bytes 294920 | tf_op jit(solution)/shard_map/ppermute | solution.py:40
  163.7 6.2 %collective-permute-start.20 = (bf16[384,128]{1,0:T(8,128)(2,1)S(1)}, bf16[384,128]{1,0:T(8,128)(2,1)S(1)}, u32[]{:S(2)}, u32[]{:S(2)}) collective-permute-start(bf16[384,128]{1,0:T(8,128)(2,1)S(1)} %get-tuple-element.95), channel_id=1, source_target_pairs={{0,128},{64,192},{128,0},{192,64},{1,129},{65,193},{129,1},{193,65... | collective-permute-start | bytes 294920 | tf_op jit(solution)/shard_map/ppermute | solution.py:40
  164.9 6.0 %collective-permute-start.21 = (bf16[384,128]{1,0:T(8,128)(2,1)S(1)}, bf16[384,128]{1,0:T(8,128)(2,1)S(1)}, u32[]{:S(2)}, u32[]{:S(2)}) collective-permute-start(bf16[384,128]{1,0:T(8,128)(2,1)S(1)} %get-tuple-element.96), channel_id=1, source_target_pairs={{0,192},{64,0},{128,64},{192,128},{1,193},{65,1},{129,65},{193,129... | collective-permute-start | bytes 294920 | tf_op jit(solution)/shard_map/ppermute | solution.py:40
  171.1 10.3 %collective-permute-start.22 = (bf16[4,96,128]{2,1,0:T(8,128)(2,1)S(1)}, bf16[4,96,128]{2,1,0:T(8,128)(2,1)S(1)}, u32[]{:S(2)}, u32[]{:S(2)}) collective-permute-start(bf16[4,96,128]{2,1,0:T(8,128)(2,1)S(1)} %dynamic-slice_bitcast_fusion.1), channel_id=1, source_target_pairs={{0,8},{2,10},{4,12},{6,14},{8,0},{10,2},{12,4},{14,6},{1,9},{3,11}... | collective-permute-start | bytes 294920 | tf_op jit(solution)/shard_map/ppermute | solution.py:44
  172.2 4.9 %collective-permute-start.23 = (bf16[128,256]{1,0:T(8,128)(2,1)S(1)}, bf16[128,256]{1,0:T(8,128)(2,1)S(1)}, u32[]{:S(2)}, u32[]{:S(2)}) collective-permute-start(bf16[128,256]{1,0:T(8,128)(2,1)S(1)} %get-tuple-element.128), channel_id=1, source_target_pairs={{0,64},{64,128},{128,192},{192,0},{1,65},{65,129},{129,193},{193,1... | collective-permute-start | bytes 196616 | tf_op jit(solution)/shard_map/ppermute | solution.py:40
  173.3 5.9 %collective-permute-start.24 = (bf16[128,256]{1,0:T(8,128)(2,1)S(1)}, bf16[128,256]{1,0:T(8,128)(2,1)S(1)}, u32[]{:S(2)}, u32[]{:S(2)}) collective-permute-start(bf16[128,256]{1,0:T(8,128)(2,1)S(1)} %get-tuple-element.127), channel_id=1, source_target_pairs={{0,128},{64,192},{128,0},{192,64},{1,129},{65,193},{129,1},{193,65... | collective-permute-start | bytes 196616 | tf_op jit(solution)/shard_map/ppermute | solution.py:40
  174.5 5.0 %collective-permute-start.25 = (bf16[128,256]{1,0:T(8,128)(2,1)S(1)}, bf16[128,256]{1,0:T(8,128)(2,1)S(1)}, u32[]{:S(2)}, u32[]{:S(2)}) collective-permute-start(bf16[128,256]{1,0:T(8,128)(2,1)S(1)} %get-tuple-element.126), channel_id=1, source_target_pairs={{0,192},{64,0},{128,64},{192,128},{1,193},{65,1},{129,65},{193,129... | collective-permute-start | bytes 196616 | tf_op jit(solution)/shard_map/ppermute | solution.py:40
  182.3 8.0 %collective-permute-start.29 = (bf16[64,128]{1,0:T(8,128)(2,1)S(1)}, bf16[64,128]{1,0:T(8,128)(2,1)S(1)}, u32[]{:S(2)}, u32[]{:S(2)}) collective-permute-start(bf16[64,128]{1,0:T(8,128)(2,1)S(1)} %get-tuple-element.134), channel_id=1, source_target_pairs={{0,16},{16,32},{32,48},{48,0},{1,17},{17,33},{33,49},{49,1},{2,18}... | collective-permute-start | bytes 49160 | tf_op jit(solution)/shard_map/ppermute | solution.py:40
  182.4 13.1 %collective-permute-start.26 = (bf16[96,128]{1,0:T(8,128)(2,1)S(1)}, bf16[96,128]{1,0:T(8,128)(2,1)S(1)}, u32[]{:S(2)}, u32[]{:S(2)}) collective-permute-start(bf16[96,128]{1,0:T(8,128)(2,1)S(1)} %get-tuple-element.131), channel_id=1, source_target_pairs={{0,2},{2,0},{4,6},{6,4},{8,10},{10,8},{12,14},{14,12},{1,3},{3,1},... | collective-permute-start | bytes 73736 | tf_op jit(solution)/shard_map/ppermute | solution.py:44
  187.8 7.7 %collective-permute-start.27 = (bf16[96,128]{1,0:T(8,128)(2,1)S(1)}, bf16[96,128]{1,0:T(8,128)(2,1)S(1)}, u32[]{:S(2)}, u32[]{:S(2)}) collective-permute-start(bf16[96,128]{1,0:T(8,128)(2,1)S(1)} %get-tuple-element.130), channel_id=1, source_target_pairs={{0,4},{2,6},{4,0},{6,2},{8,12},{10,14},{12,8},{14,10},{1,5},{3,7},... | collective-permute-start | bytes 73736 | tf_op jit(solution)/shard_map/ppermute | solution.py:44
  187.8 7.7 %collective-permute-start.28 = (bf16[96,128]{1,0:T(8,128)(2,1)S(1)}, bf16[96,128]{1,0:T(8,128)(2,1)S(1)}, u32[]{:S(2)}, u32[]{:S(2)}) collective-permute-start(bf16[96,128]{1,0:T(8,128)(2,1)S(1)} %get-tuple-element.129), channel_id=1, source_target_pairs={{0,6},{2,4},{4,2},{6,0},{8,14},{10,12},{12,10},{14,8},{1,7},{3,5},... | collective-permute-start | bytes 73736 | tf_op jit(solution)/shard_map/ppermute | solution.py:44
  190.3 5.2 %collective-permute-start.30 = (bf16[64,128]{1,0:T(8,128)(2,1)S(1)}, bf16[64,128]{1,0:T(8,128)(2,1)S(1)}, u32[]{:S(2)}, u32[]{:S(2)}) collective-permute-start(bf16[64,128]{1,0:T(8,128)(2,1)S(1)} %get-tuple-element.133), channel_id=1, source_target_pairs={{0,32},{16,48},{32,0},{48,16},{1,33},{17,49},{33,1},{49,17},{2,34}... | collective-permute-start | bytes 49160 | tf_op jit(solution)/shard_map/ppermute | solution.py:40
  190.3 5.2 %collective-permute-start.31 = (bf16[64,128]{1,0:T(8,128)(2,1)S(1)}, bf16[64,128]{1,0:T(8,128)(2,1)S(1)}, u32[]{:S(2)}, u32[]{:S(2)}) collective-permute-start(bf16[64,128]{1,0:T(8,128)(2,1)S(1)} %get-tuple-element.132), channel_id=1, source_target_pairs={{0,48},{16,0},{32,16},{48,32},{1,49},{17,1},{33,17},{49,33},{2,50}... | collective-permute-start | bytes 49160 | tf_op jit(solution)/shard_map/ppermute | solution.py:40
  (20 other events, 248.1 us)
Sparse Core Ops, SparseCore 0:
  9.9 77.8 all-gather.1
  121.6 41.0 reduce-scatter.1

commit v3 on v2

--- a/solution.py
+++ b/solution.py
@@ -11,8 +11,8 @@
 GROUP = 5
 KVH = 4
 SCALE = HD**-0.5
-RZ = 64
-RA = 48
+RZ = 80
+RA = 40
 Y = ("yh", "yl")
 F32 = jnp.float32
 BF16 = jnp.bfloat16
@@ -61,14 +61,12 @@
     return lax.dot_general(a, b, (((0,), (0,)), ((), ())), preferred_element_type=F32)
 
 
-def attention_kernel(hidden, wk, wv, q, up, cos, sin, start, weight, qg, kvg):
-    length = hidden.shape[0]
+def attention_kernel(kpre, vpre, q, up, cos, sin, start, weight, qg, kvg):
+    length = kpre.shape[0]
     cosine, sine = cos[...], sin[...]
-    both = jnp.concatenate([wk[...], wv[...]], axis=1)
-    pre = jnp.dot(hidden[...], both, preferred_element_type=F32)
-    kp = pre[:, :HD]
+    kp = kpre[...]
     k = (kp * cosine + pltpu.roll(kp, HD // 2, 1) * sine).astype(BF16)
-    v = pre[:, HD:].astype(BF16)
+    v = vpre[...].astype(BF16)
     key_index = lax.broadcasted_iota(jnp.int32, (length, length), 0)
     query_index = lax.broadcasted_iota(jnp.int32, (length, length), 1)
     allowed = (key_index >= start[...]) & (key_index <= query_index)
@@ -95,7 +93,7 @@
     kvg[:, pl.ds(at + KVH * HD, HD)] = dv.astype(BF16)
 
 
-def attention_backward(hidden, full_weight, queries, upstream, pos, weight):
+def attention_backward(kv_pre, queries, upstream, pos, weight):
     length = pos.shape[0]
     freq = ROPE_BASE ** (-(jnp.arange(HD // 2, dtype=F32) * 2.0 / HD))
     angle = pos.astype(F32)[:, None] * freq[None, :]
@@ -107,9 +105,8 @@
         attention_kernel,
         grid=(KVH,),
         in_specs=[
-            whole(hidden.shape),
-            pl.BlockSpec((hidden.shape[1], HD), lambda h: (0, h)),
-            pl.BlockSpec((hidden.shape[1], HD), lambda h: (0, h + KVH)),
+            pl.BlockSpec((length, HD), lambda h: (0, h)),
+            pl.BlockSpec((length, HD), lambda h: (0, h + KVH)),
             pl.BlockSpec((length, GROUP * HD), lambda h: (0, h)),
             pl.BlockSpec((length, GROUP * HD), lambda h: (0, h)),
             whole((length, HD)),
@@ -126,7 +123,7 @@
             jax.ShapeDtypeStruct((length, 2 * KVH * HD), BF16),
         ],
         compiler_params=pltpu.CompilerParams(vmem_limit_bytes=32 * 2**20),
-    )(hidden, full_weight, full_weight, queries, upstream, cosine, sine, start, weight[:, None])
+    )(kv_pre, kv_pre, queries, upstream, cosine, sine, start, weight[:, None])
 
 
 def hidden_grad_kernel(kv, w, out):
@@ -146,7 +143,7 @@
         ],
         out_specs=pl.BlockSpec((length, block), lambda i: (0, i)),
         out_shape=jax.ShapeDtypeStruct((length, width), BF16),
-        compiler_params=pltpu.CompilerParams(vmem_limit_bytes=24 * 2**20),
+        compiler_params=pltpu.CompilerParams(vmem_limit_bytes=48 * 2**20),
     )(kv_grad, full_weight)
 
 
@@ -258,7 +255,8 @@
 
     hidden, hz, ha, hb = barrier((hidden, hz, ha, hb))
 
-    query_grad, kv_grad = attention_backward(hidden, full_weight, queries, upstream, pos, weight)
+    kv_pre = jnp.dot(hidden, full_weight, preferred_element_type=F32)
+    query_grad, kv_grad = attention_backward(kv_pre, queries, upstream, pos, weight)
     pair = jnp.concatenate([kv_grad, shift(kv_grad, "c", 2, 1)], axis=0)
 
     part_z = jnp.dot(hz, pair, preferred_element_type=F32).astype(BF16)

time: 205 us -> 191 us (0.932)
  local copies, waits for them, and re-layouts: 26.9 us -> 13.5 us
  starting transfers between devices: 45.4 us -> 53.4 us
  matrix products: 2.66 us -> 9.61 us
  Pallas kernels: 30.4 us -> 23.6 us
  waiting for transfers between devices: 71.6 us -> 66.8 us
  other arithmetic: 10.5 us -> 7.91 us
    ppermute x20, waiting for transfers between devices: 23.4 us -> 8.44 us  [shift(): return lax.ppermute(v, axis, [(i, (i + k) % n) for i in range(n)])]
    unnamed x38 -> x20, local copies, waits for them, and re-layouts: 18.9 us -> 5.4 us
    pallas_call x1, Pallas kernels: 20.6 us -> 10.3 us  [attention_backward(): pl.pallas_call(attention_kernel, grid=(KVH,), in_specs=[pl.BlockSpec((len...]
    ppermute x20, starting transfers between devices: 25.7 us -> 35.6 us  [shift(): return lax.ppermute(v, axis, [(i, (i + k) % n) for i in range(n)])]
    ppermute x12, waiting for transfers between devices: 20.7 us -> 29.2 us  [swap(): return lax.ppermute(v, axis, [(i, i ^ bit) for i in range(n)])]
    dot_general x0 -> x1, matrix products: none -> 6.5 us  [body(): kv_pre = jnp.dot(hidden, full_weight, preferred_element_type=F32)]
    pallas_call x1, Pallas kernels: 5.97 us -> 9.78 us  [hidden_gradient(): pl.pallas_call(hidden_grad_kernel, grid=(8,), in_specs=[pl.BlockSpec((len...]
  transfers between devices with their start and end apart: 34 -> 34, of which waited for: 17 -> 14; matrix products, arithmetic and copies ran while one was open for 10% -> 9% of each run, Pallas kernels for 5% -> 7%
where the time goes in v3:
time: 191 us
  waiting for transfers between devices  66.8 us (35%)
  starting transfers between devices  53.4 us (28%)
  Pallas kernels  23.6 us (12%)
  between operations  15.8 us (8%)
  local copies, waits for them, and re-layouts  13.5 us (7%)
  matrix products  9.61 us (5%)
  other arithmetic  7.91 us (4%)
    ppermute x20, starting transfers between devices, shift(): return lax.ppermute(v, axis, [(i, (i + k) % n) for i in range(n)])  35.6 us
    ppermute x12, waiting for transfers between devices, swap(): return lax.ppermute(v, axis, [(i, i ^ bit) for i in range(n)])  29.2 us
    all_gather x1, waiting for transfers between devices, body(): lax.all_gather(kv_weight, ('yl', 'z', 'c'), axis=0, tiled=True)  28.5 us
    ppermute x12, starting transfers between devices, swap(): return lax.ppermute(v, axis, [(i, i ^ bit) for i in range(n)])  17.7 us
    pallas_call x1, Pallas kernels, attention_backward(): pl.pallas_call(attention_kernel, grid=(KVH,), in_specs=[pl.BlockSpec((len...  10.3 us
    pallas_call x1, Pallas kernels, hidden_gradient(): pl.pallas_call(hidden_grad_kernel, grid=(8,), in_specs=[pl.BlockSpec((len...  9.78 us
    ppermute x20, waiting for transfers between devices, shift(): return lax.ppermute(v, axis, [(i, (i + k) % n) for i in range(n)])  8.44 us
    dot_general x1, matrix products, body(): kv_pre = jnp.dot(hidden, full_weight, preferred_element_type=F32)  6.5 us
  transfers between devices with their start and end apart: 34, of which 14 were waited for; matrix products, arithmetic and copies ran while one was open for 9% of the time, Pallas kernels for 7%

profile of v3, /device:TPU:2, one launch (start us, length us, event | category | flops | bytes accessed | tf_op | source)
XLA Modules:
  0.0 190.6 jit_solution(10529382860992126515)
XLA Ops:
  13.3 4.4 %copy.28 = bf16[256,5120]{0,1:T(8,128)(2,1)} copy(bf16[256,5120]{1,0:T(8,128)(2,1)} %param.10) | data formatting | bytes 5242880 | tf_op args[0]
  18.4 2.4 %collective-permute-start.2 = (f32[8,128]{1,0:T(8,128)S(1)}, f32[8,128]{1,0:T(8,128)S(1)}, u32[]{:S(2)}, u32[]{:S(2)}) collective-permute-start(f32[8,128]{1,0:T(8,128)S(1)} %broadcast_add_fusion), channel_id=1, source_target_pairs={{0,64},{64,0},{128,192},{192,128},{1,65},{65,1},{129,193},{193,129... | collective-permute-start | bytes 12296 | tf_op jit(solution)/shard_map/ppermute | solution.py:44
  20.8 3.0 %dynamic-slice_bitcast_fusion = (bf16[16,160,256]{2,1,0:T(8,128)(2,1)}, bf16[16,1,160,256]{3,2,1,0:T(8,128)(2,1)S(1)}) fusion(bf16[16,2,160,256]{3,2,1,0:T(8,128)(2,1)} %bitcast.73, s32[]{:T(128)S(6)} %select_n.106, s32[]{:T(128)S(6)} %select_n.105), kind=kLoop, calls=%fused_computation.7 | loop fusion | bytes 5242888 | tf_op jit(solution)/shard_map/jit(dynamic_index_in_dim)/squeeze | solution.py:211
  25.4 4.4 %collective-permute-done.3 = f32[8,128]{1,0:T(8,128)S(1)} collective-permute-done((f32[8,128]{1,0:T(8,128)S(1)}, f32[8,128]{1,0:T(8,128)S(1)}, u32[]{:S(2)}, u32[]{:S(2)}) %collective-permute-start.3) | collective-permute-done | bytes 4128 | tf_op jit(solution)/shard_map/ppermute | solution.py:44
  29.8 3.6 %collective-permute-done.4 = f32[8,128]{1,0:T(8,128)S(1)} collective-permute-done((f32[8,128]{1,0:T(8,128)S(1)}, f32[8,128]{1,0:T(8,128)S(1)}, u32[]{:S(2)}, u32[]{:S(2)}) %collective-permute-start.4) | collective-permute-done | bytes 4128 | tf_op jit(solution)/shard_map/ppermute | solution.py:44
  35.4 3.2 %collective-permute-done.5 = f32[8,128]{1,0:T(8,128)S(1)} collective-permute-done((f32[8,128]{1,0:T(8,128)S(1)}, f32[8,128]{1,0:T(8,128)S(1)}, u32[]{:S(2)}, u32[]{:S(2)}) %collective-permute-start.5) | collective-permute-done | bytes 4128 | tf_op jit(solution)/shard_map/ppermute | solution.py:44
  38.7 3.5 %collective-permute-done.6 = f32[8,128]{1,0:T(8,128)S(1)} collective-permute-done((f32[8,128]{1,0:T(8,128)S(1)}, f32[8,128]{1,0:T(8,128)S(1)}, u32[]{:S(2)}, u32[]{:S(2)}) %collective-permute-start.6) | collective-permute-done | bytes 4128 | tf_op jit(solution)/shard_map/ppermute | solution.py:44
  43.8 3.0 %collective-permute-done.7 = f32[8,128]{1,0:T(8,128)S(1)} collective-permute-done((f32[8,128]{1,0:T(8,128)S(1)}, f32[8,128]{1,0:T(8,128)S(1)}, u32[]{:S(2)}, u32[]{:S(2)}) %collective-permute-start.7) | collective-permute-done | bytes 4128 | tf_op jit(solution)/shard_map/ppermute | solution.py:44
  46.8 5.4 %collective-permute-start.8 = (f32[8,128]{1,0:T(8,128)S(1)}, f32[8,128]{1,0:T(8,128)S(1)}, u32[]{:S(2)}, u32[]{:S(2)}) collective-permute-start(f32[8,128]{1,0:T(8,128)S(1)} %add.196), channel_id=1, source_target_pairs={{0,8},{2,10},{4,12},{6,14},{8,0},{10,2},{12,4},{14,6},{1,9},{3,11}... | collective-permute-start | bytes 12296 | tf_op jit(solution)/shard_map/ppermute | solution.py:44
  52.6 1.8 collective-permute-done.8
  59.2 28.5 %all-gather.2.cloned.1.call-done.w = bf16[5120,1024]{1,0:T(8,128)(2,1)} async-done(((bf16[160,1024]{1,0:T(8,128)(2,1)}), bf16[5120,1024]{1,0:T(8,128)(2,1)}) %all-gather.2.cloned.1.call-update) | async-done | bytes 10485776 | tf_op jit(solution)/shard_map/all_gather | solution.py:240
  87.7 6.5 %fusion.12.kpre.vpre = f32[256,1024]{1,0:T(8,128)S(1)} fusion(bf16[256,5120]{1,0:T(8,128)(2,1)} %param.10, bf16[5120,1024]{1,0:T(8,128)(2,1)} %all-gather.2.cloned.1.call-done.w), kind=kOutput, calls=%fused_computation.64 | convolution fusion | flops 2684354560 | bytes 14155776 | tf_op jit(solution)/shard_map/dot_general | solution.py:258
  94.3 10.3 %shard_map.137 = (bf16[256,2560]{1,0:T(8,128)(2,1)}, bf16[256,1024]{1,0:T(8,128)(2,1)S(1)}) custom-call(f32[256,1024]{1,0:T(8,128)S(1)} %fusion.12.kpre.vpre, f32[256,1024]{1,0:T(8,128)S(1)} %fusion.12.kpre.vpre, bf16[256,2560]{1,0:T(8,128)(2,1)S(1)} %copy-done, bf16[256,2560]{1,0:T(8,128)(2,1)S(1)} %copy-done.1, f32[256,128]{1,0:T(8,128)S(1)} %get-tuple-element.138.cos, ...), custom_call_target="tpu_custom_call" | custom-call | tf_op jit(solution)/shard_map/pallas_call | solution.py:104
  106.5 3.1 %convolution_convert_fusion = bf16[1280,1024]{1,0:T(8,128)(2,1)} fusion(bf16[1280,512]{1,0:T(8,128)(2,1)S(1)} %bitcast.76, bf16[512,1024]{1,0:T(8,128)(2,1)S(1)} %constant_dynamic-update-slice_fusion.pair), kind=kOutput, calls=%fused_computation | convolution fusion | flops 1343488000 | bytes 4980736 | tf_op jit(solution)/shard_map/dot_general | solution.py:262
  109.8 2.2 %shard_map.138 = (bf16[640,256]{1,0:T(8,128)(2,1)S(1)}, bf16[640,256]{1,0:T(8,128)(2,1)S(1)}, bf16[640,256]{1,0:T(8,128)(2,1)S(1)}, bf16[640,256]{1,0:T(8,128)(2...) custom-call(s32[2]{0:T(128)S(1)} %pad_add_fusion.place, ...), custom_call_target="tpu_custom_call" | custom-call | tf_op jit(solution)/shard_map/pallas_call | solution.py:173
  114.8 2.4 %collective-permute-start.12 = (bf16[640,256]{1,0:T(8,128)(2,1)S(1)}, bf16[640,256]{1,0:T(8,128)(2,1)S(1)}, u32[]{:S(2)}, u32[]{:S(2)}) collective-permute-start(bf16[640,256]{1,0:T(8,128)(2,1)S(1)} %get-tuple-element.76), channel_id=1, source_target_pairs={{0,192},{64,0},{128,64},{192,128},{1,193},{65,1},{129,65},{193,129... | collective-permute-start | bytes 983048 | tf_op jit(solution)/shard_map/ppermute | solution.py:40
  118.4 2.4 %collective-permute-start.14 = (bf16[320,512]{1,0:T(8,128)(2,1)S(1)}, bf16[320,512]{1,0:T(8,128)(2,1)S(1)}, u32[]{:S(2)}, u32[]{:S(2)}) collective-permute-start(bf16[320,512]{1,0:T(8,128)(2,1)S(1)} %get-tuple-element.78), channel_id=1, source_target_pairs={{0,32},{16,48},{32,0},{48,16},{1,33},{17,49},{33,1},{49,17},{2,34}... | collective-permute-start | bytes 983048 | tf_op jit(solution)/shard_map/ppermute | solution.py:40
  122.6 2.6 %collective-permute-start.15 = (bf16[320,512]{1,0:T(8,128)(2,1)S(1)}, bf16[320,512]{1,0:T(8,128)(2,1)S(1)}, u32[]{:S(2)}, u32[]{:S(2)}) collective-permute-start(bf16[320,512]{1,0:T(8,128)(2,1)S(1)} %get-tuple-element.79), channel_id=1, source_target_pairs={{0,48},{16,0},{32,16},{48,32},{1,49},{17,1},{33,17},{49,33},{2,50}... | collective-permute-start | bytes 983048 | tf_op jit(solution)/shard_map/ppermute | solution.py:40
  125.2 9.8 %shard_map.139 = bf16[256,5120]{1,0:T(8,128)(2,1)} custom-call(bf16[256,1024]{1,0:T(8,128)(2,1)S(1)} %get-tuple-element.80.kv, bf16[5120,1024]{1,0:T(8,128)(2,1)} %all-gather.2.cloned.1.call-done.w), custom_call_target="tpu_custom_call" | custom-call | tf_op jit(solution)/shard_map/pallas_call | solution.py:137
  136.3 4.4 %collective-permute-start.16 = (bf16[320,128]{1,0:T(8,128)(2,1)S(1)}, bf16[320,128]{1,0:T(8,128)(2,1)S(1)}, u32[]{:S(2)}, u32[]{:S(2)}) collective-permute-start(bf16[320,128]{1,0:T(8,128)(2,1)S(1)} %get-tuple-element.91), channel_id=1, source_target_pairs={{0,16},{16,32},{32,48},{48,0},{1,17},{17,33},{33,49},{49,1},{2,18}... | collective-permute-start | bytes 245768 | tf_op jit(solution)/shard_map/ppermute | solution.py:40
  140.7 2.2 %collective-permute-start.17 = (bf16[320,128]{1,0:T(8,128)(2,1)S(1)}, bf16[320,128]{1,0:T(8,128)(2,1)S(1)}, u32[]{:S(2)}, u32[]{:S(2)}) collective-permute-start(bf16[320,128]{1,0:T(8,128)(2,1)S(1)} %get-tuple-element.92), channel_id=1, source_target_pairs={{0,32},{16,48},{32,0},{48,16},{1,33},{17,49},{33,1},{49,17},{2,34}... | collective-permute-start | bytes 245768 | tf_op jit(solution)/shard_map/ppermute | solution.py:40
  142.9 2.5 %collective-permute-start.18 = (bf16[320,128]{1,0:T(8,128)(2,1)S(1)}, bf16[320,128]{1,0:T(8,128)(2,1)S(1)}, u32[]{:S(2)}, u32[]{:S(2)}) collective-permute-start(bf16[320,128]{1,0:T(8,128)(2,1)S(1)} %get-tuple-element.93), channel_id=1, source_target_pairs={{0,48},{16,0},{32,16},{48,32},{1,49},{17,1},{33,17},{49,33},{2,50}... | collective-permute-start | bytes 245768 | tf_op jit(solution)/shard_map/ppermute | solution.py:40
  145.4 2.4 %collective-permute-start.19 = (bf16[320,128]{1,0:T(8,128)(2,1)S(1)}, bf16[320,128]{1,0:T(8,128)(2,1)S(1)}, u32[]{:S(2)}, u32[]{:S(2)}) collective-permute-start(bf16[320,128]{1,0:T(8,128)(2,1)S(1)} %get-tuple-element.94), channel_id=1, source_target_pairs={{0,64},{64,128},{128,192},{192,0},{1,65},{65,129},{129,193},{193,1... | collective-permute-start | bytes 245768 | tf_op jit(solution)/shard_map/ppermute | solution.py:40
  147.8 2.1 %collective-permute-start.21 = (bf16[320,128]{1,0:T(8,128)(2,1)S(1)}, bf16[320,128]{1,0:T(8,128)(2,1)S(1)}, u32[]{:S(2)}, u32[]{:S(2)}) collective-permute-start(bf16[320,128]{1,0:T(8,128)(2,1)S(1)} %get-tuple-element.96), channel_id=1, source_target_pairs={{0,192},{64,0},{128,64},{192,128},{1,193},{65,1},{129,65},{193,129... | collective-permute-start | bytes 245768 | tf_op jit(solution)/shard_map/ppermute | solution.py:40
  149.9 3.9 %collective-permute-done.20 = bf16[320,128]{1,0:T(8,128)(2,1)S(1)} collective-permute-done((bf16[320,128]{1,0:T(8,128)(2,1)S(1)}, bf16[320,128]{1,0:T(8,128)(2,1)S(1)}, u32[]{:S(2)}, u32[]{:S(2)}) %collective-permute-start.20) | collective-permute-done | bytes 81952 | tf_op jit(solution)/shard_map/ppermute | solution.py:40
  156.5 2.8 %collective-permute-start.24 = (bf16[160,256]{1,0:T(8,128)(2,1)S(1)}, bf16[160,256]{1,0:T(8,128)(2,1)S(1)}, u32[]{:S(2)}, u32[]{:S(2)}) collective-permute-start(bf16[160,256]{1,0:T(8,128)(2,1)S(1)} %get-tuple-element.127), channel_id=1, source_target_pairs={{0,128},{64,192},{128,0},{192,64},{1,129},{65,193},{129,1},{193,65... | collective-permute-start | bytes 245768 | tf_op jit(solution)/shard_map/ppermute | solution.py:40
  159.3 2.5 %collective-permute-start.25 = (bf16[160,256]{1,0:T(8,128)(2,1)S(1)}, bf16[160,256]{1,0:T(8,128)(2,1)S(1)}, u32[]{:S(2)}, u32[]{:S(2)}) collective-permute-start(bf16[160,256]{1,0:T(8,128)(2,1)S(1)} %get-tuple-element.126), channel_id=1, source_target_pairs={{0,192},{64,0},{128,64},{192,128},{1,193},{65,1},{129,65},{193,129... | collective-permute-start | bytes 245768 | tf_op jit(solution)/shard_map/ppermute | solution.py:40
  163.9 6.5 %collective-permute-done.22 = bf16[4,80,128]{2,1,0:T(8,128)(2,1)S(1)} collective-permute-done((bf16[4,80,128]{2,1,0:T(8,128)(2,1)S(1)}, bf16[4,80,128]{2,1,0:T(8,128)(2,1)S(1)}, u32[]{:S(2)}, u32[]{:S(2)}) %collective-permute-start.22) | collective-permute-done | bytes 81952 | tf_op jit(solution)/shard_map/ppermute | solution.py:44
  172.7 2.0 %collective-permute-start.31 = (bf16[80,128]{1,0:T(8,128)(2,1)S(1)}, bf16[80,128]{1,0:T(8,128)(2,1)S(1)}, u32[]{:S(2)}, u32[]{:S(2)}) collective-permute-start(bf16[80,128]{1,0:T(8,128)(2,1)S(1)} %get-tuple-element.129), channel_id=1, source_target_pairs={{0,48},{16,0},{32,16},{48,32},{1,49},{17,1},{33,17},{49,33},{2,50}... | collective-permute-start | bytes 61448 | tf_op jit(solution)/shard_map/ppermute | solution.py:40
  174.7 2.5 %collective-permute-start.26 = (bf16[80,128]{1,0:T(8,128)(2,1)S(1)}, bf16[80,128]{1,0:T(8,128)(2,1)S(1)}, u32[]{:S(2)}, u32[]{:S(2)}) collective-permute-start(bf16[80,128]{1,0:T(8,128)(2,1)S(1)} %get-tuple-element.134), channel_id=1, source_target_pairs={{0,2},{2,0},{4,6},{6,4},{8,10},{10,8},{12,14},{14,12},{1,3},{3,1},... | collective-permute-start | bytes 61448 | tf_op jit(solution)/shard_map/ppermute | solution.py:44
  177.4 2.3 %collective-permute-start.28 = (bf16[80,128]{1,0:T(8,128)(2,1)S(1)}, bf16[80,128]{1,0:T(8,128)(2,1)S(1)}, u32[]{:S(2)}, u32[]{:S(2)}) collective-permute-start(bf16[80,128]{1,0:T(8,128)(2,1)S(1)} %get-tuple-element.132), channel_id=1, source_target_pairs={{0,6},{2,4},{4,2},{6,0},{8,14},{10,12},{12,10},{14,8},{1,7},{3,5},... | collective-permute-start | bytes 61448 | tf_op jit(solution)/shard_map/ppermute | solution.py:44
  179.7 2.2 %collective-permute-done.27 = bf16[80,128]{1,0:T(8,128)(2,1)S(1)} collective-permute-done((bf16[80,128]{1,0:T(8,128)(2,1)S(1)}, bf16[80,128]{1,0:T(8,128)(2,1)S(1)}, u32[]{:S(2)}, u32[]{:S(2)}) %collective-permute-start.27) | collective-permute-done | bytes 20512 | tf_op jit(solution)/shard_map/ppermute | solution.py:44
  (111 shorter events, 34.0 us)
Async XLA Ops:
  7.2 80.6 %all-gather.2.cloned.1.call-start = ((), (), s32[]{:S(2)}) async-start(), calls=%async_computation.1 | async-start | bytes 10813440 | tf_op jit(solution)/shard_map/all_gather | solution.py:240
  7.9 146.1 %reduce-scatter.2.cloned.1.call-start = ((), (), s32[]{:S(2)}) async-start(), calls=%async_computation.2 | async-start | bytes 2949120 | tf_op jit(solution)/shard_map/reduce_scatter | solution.py:263
  13.2 4.5 %collective-permute-start.1 = (f32[8,128]{1,0:T(8,128)S(1)}, f32[8,128]{1,0:T(8,128)S(1)}, u32[]{:S(2)}, u32[]{:S(2)}) collective-permute-start(f32[8,128]{1,0:T(8,128)S(1)} %broadcast_in_dim.57), channel_id=1, source_target_pairs={{0,1},{1,0},{2,3},{3,2},{4,5},{5,4},{6,7},{7,6},{8,9},{9,8},{10,11... | collective-permute-start | bytes 12296 | tf_op jit(solution)/shard_map/ppermute | solution.py:44
  18.4 5.5 %collective-permute-start.2 = (f32[8,128]{1,0:T(8,128)S(1)}, f32[8,128]{1,0:T(8,128)S(1)}, u32[]{:S(2)}, u32[]{:S(2)}) collective-permute-start(f32[8,128]{1,0:T(8,128)S(1)} %broadcast_add_fusion), channel_id=1, source_target_pairs={{0,64},{64,0},{128,192},{192,128},{1,65},{65,1},{129,193},{193,129... | collective-permute-start | bytes 12296 | tf_op jit(solution)/shard_map/ppermute | solution.py:44
  23.7 32.1 %collective-permute-start = (bf16[16,160,256]{2,1,0:T(8,128)(2,1)}, bf16[16,160,256]{2,1,0:T(8,128)(2,1)S(1)}, u32[]{:S(2)}, u32[]{:S(2)}) collective-permute-start(bf16[16,160,256]{2,1,0:T(8,128)(2,1)} %get-tuple-element.124), channel_id=1, source_target_pairs={{0,1},{1,0},{2,3},{3,2},{4,5},{5,4},{6,7},{7,6},{8,9},{9,8},{10,11... | collective-permute-start | bytes 3932168 | tf_op jit(solution)/shard_map/ppermute | solution.py:40
  24.6 5.2 %collective-permute-start.3 = (f32[8,128]{1,0:T(8,128)S(1)}, f32[8,128]{1,0:T(8,128)S(1)}, u32[]{:S(2)}, u32[]{:S(2)}) collective-permute-start(f32[8,128]{1,0:T(8,128)S(1)} %fusion.17), channel_id=1, source_target_pairs={{0,128},{64,192},{128,0},{192,64},{1,129},{65,193},{129,1},{193,65... | collective-permute-start | bytes 12296 | tf_op jit(solution)/shard_map/ppermute | solution.py:44
  29.8 3.6 %collective-permute-start.4 = (f32[8,128]{1,0:T(8,128)S(1)}, f32[8,128]{1,0:T(8,128)S(1)}, u32[]{:S(2)}, u32[]{:S(2)}) collective-permute-start(f32[8,128]{1,0:T(8,128)S(1)} %add.192), channel_id=1, source_target_pairs={{0,16},{16,0},{1,17},{17,1},{2,18},{18,2},{3,19},{19,3},{4,20},{20... | collective-permute-start | bytes 12296 | tf_op jit(solution)/shard_map/ppermute | solution.py:44
  33.4 5.2 %collective-permute-start.5 = (f32[8,128]{1,0:T(8,128)S(1)}, f32[8,128]{1,0:T(8,128)S(1)}, u32[]{:S(2)}, u32[]{:S(2)}) collective-permute-start(f32[8,128]{1,0:T(8,128)S(1)} %add.193), channel_id=1, source_target_pairs={{0,32},{32,0},{1,33},{33,1},{2,34},{34,2},{3,35},{35,3},{4,36},{36... | collective-permute-start | bytes 12296 | tf_op jit(solution)/shard_map/ppermute | solution.py:44
  42.2 4.6 %collective-permute-start.7 = (f32[8,128]{1,0:T(8,128)S(1)}, f32[8,128]{1,0:T(8,128)S(1)}, u32[]{:S(2)}, u32[]{:S(2)}) collective-permute-start(f32[8,128]{1,0:T(8,128)S(1)} %add.195), channel_id=1, source_target_pairs={{0,4},{2,6},{4,0},{6,2},{8,12},{10,14},{12,8},{14,10},{1,5},{3,7},... | collective-permute-start | bytes 12296 | tf_op jit(solution)/shard_map/ppermute | solution.py:44
  46.8 7.6 %collective-permute-start.8 = (f32[8,128]{1,0:T(8,128)S(1)}, f32[8,128]{1,0:T(8,128)S(1)}, u32[]{:S(2)}, u32[]{:S(2)}) collective-permute-start(f32[8,128]{1,0:T(8,128)S(1)} %add.196), channel_id=1, source_target_pairs={{0,8},{2,10},{4,12},{6,14},{8,0},{10,2},{12,4},{14,6},{1,9},{3,11}... | collective-permute-start | bytes 12296 | tf_op jit(solution)/shard_map/ppermute | solution.py:44
  112.0 10.6 %collective-permute-start.10 = (bf16[640,256]{1,0:T(8,128)(2,1)S(1)}, bf16[640,256]{1,0:T(8,128)(2,1)S(1)}, u32[]{:S(2)}, u32[]{:S(2)}) collective-permute-start(bf16[640,256]{1,0:T(8,128)(2,1)S(1)} %get-tuple-element.74), channel_id=1, source_target_pairs={{0,64},{64,128},{128,192},{192,0},{1,65},{65,129},{129,193},{193,1... | collective-permute-start | bytes 983048 | tf_op jit(solution)/shard_map/ppermute | solution.py:40
  113.7 21.3 %collective-permute-start.11 = (bf16[640,256]{1,0:T(8,128)(2,1)S(1)}, bf16[640,256]{1,0:T(8,128)(2,1)S(1)}, u32[]{:S(2)}, u32[]{:S(2)}) collective-permute-start(bf16[640,256]{1,0:T(8,128)(2,1)S(1)} %get-tuple-element.75), channel_id=1, source_target_pairs={{0,128},{64,192},{128,0},{192,64},{1,129},{65,193},{129,1},{193,65... | collective-permute-start | bytes 983048 | tf_op jit(solution)/shard_map/ppermute | solution.py:40
  114.8 20.3 %collective-permute-start.12 = (bf16[640,256]{1,0:T(8,128)(2,1)S(1)}, bf16[640,256]{1,0:T(8,128)(2,1)S(1)}, u32[]{:S(2)}, u32[]{:S(2)}) collective-permute-start(bf16[640,256]{1,0:T(8,128)(2,1)S(1)} %get-tuple-element.76), channel_id=1, source_target_pairs={{0,192},{64,0},{128,64},{192,128},{1,193},{65,1},{129,65},{193,129... | collective-permute-start | bytes 983048 | tf_op jit(solution)/shard_map/ppermute | solution.py:40
  117.2 17.9 %collective-permute-start.13 = (bf16[320,512]{1,0:T(8,128)(2,1)S(1)}, bf16[320,512]{1,0:T(8,128)(2,1)S(1)}, u32[]{:S(2)}, u32[]{:S(2)}) collective-permute-start(bf16[320,512]{1,0:T(8,128)(2,1)S(1)} %get-tuple-element.77), channel_id=1, source_target_pairs={{0,16},{16,32},{32,48},{48,0},{1,17},{17,33},{33,49},{49,1},{2,18}... | collective-permute-start | bytes 983048 | tf_op jit(solution)/shard_map/ppermute | solution.py:40
  118.4 16.6 %collective-permute-start.14 = (bf16[320,512]{1,0:T(8,128)(2,1)S(1)}, bf16[320,512]{1,0:T(8,128)(2,1)S(1)}, u32[]{:S(2)}, u32[]{:S(2)}) collective-permute-start(bf16[320,512]{1,0:T(8,128)(2,1)S(1)} %get-tuple-element.78), channel_id=1, source_target_pairs={{0,32},{16,48},{32,0},{48,16},{1,33},{17,49},{33,1},{49,17},{2,34}... | collective-permute-start | bytes 983048 | tf_op jit(solution)/shard_map/ppermute | solution.py:40
  122.6 12.4 %collective-permute-start.15 = (bf16[320,512]{1,0:T(8,128)(2,1)S(1)}, bf16[320,512]{1,0:T(8,128)(2,1)S(1)}, u32[]{:S(2)}, u32[]{:S(2)}) collective-permute-start(bf16[320,512]{1,0:T(8,128)(2,1)S(1)} %get-tuple-element.79), channel_id=1, source_target_pairs={{0,48},{16,0},{32,16},{48,32},{1,49},{17,1},{33,17},{49,33},{2,50}... | collective-permute-start | bytes 983048 | tf_op jit(solution)/shard_map/ppermute | solution.py:40
  136.3 11.6 %collective-permute-start.16 = (bf16[320,128]{1,0:T(8,128)(2,1)S(1)}, bf16[320,128]{1,0:T(8,128)(2,1)S(1)}, u32[]{:S(2)}, u32[]{:S(2)}) collective-permute-start(bf16[320,128]{1,0:T(8,128)(2,1)S(1)} %get-tuple-element.91), channel_id=1, source_target_pairs={{0,16},{16,32},{32,48},{48,0},{1,17},{17,33},{33,49},{49,1},{2,18}... | collective-permute-start | bytes 245768 | tf_op jit(solution)/shard_map/ppermute | solution.py:40
  140.7 9.2 %collective-permute-start.17 = (bf16[320,128]{1,0:T(8,128)(2,1)S(1)}, bf16[320,128]{1,0:T(8,128)(2,1)S(1)}, u32[]{:S(2)}, u32[]{:S(2)}) collective-permute-start(bf16[320,128]{1,0:T(8,128)(2,1)S(1)} %get-tuple-element.92), channel_id=1, source_target_pairs={{0,32},{16,48},{32,0},{48,16},{1,33},{17,49},{33,1},{49,17},{2,34}... | collective-permute-start | bytes 245768 | tf_op jit(solution)/shard_map/ppermute | solution.py:40
  142.9 7.0 %collective-permute-start.18 = (bf16[320,128]{1,0:T(8,128)(2,1)S(1)}, bf16[320,128]{1,0:T(8,128)(2,1)S(1)}, u32[]{:S(2)}, u32[]{:S(2)}) collective-permute-start(bf16[320,128]{1,0:T(8,128)(2,1)S(1)} %get-tuple-element.93), channel_id=1, source_target_pairs={{0,48},{16,0},{32,16},{48,32},{1,49},{17,1},{33,17},{49,33},{2,50}... | collective-permute-start | bytes 245768 | tf_op jit(solution)/shard_map/ppermute | solution.py:40
  145.4 4.5 %collective-permute-start.19 = (bf16[320,128]{1,0:T(8,128)(2,1)S(1)}, bf16[320,128]{1,0:T(8,128)(2,1)S(1)}, u32[]{:S(2)}, u32[]{:S(2)}) collective-permute-start(bf16[320,128]{1,0:T(8,128)(2,1)S(1)} %get-tuple-element.94), channel_id=1, source_target_pairs={{0,64},{64,128},{128,192},{192,0},{1,65},{65,129},{129,193},{193,1... | collective-permute-start | bytes 245768 | tf_op jit(solution)/shard_map/ppermute | solution.py:40
  147.8 5.9 %collective-permute-start.20 = (bf16[320,128]{1,0:T(8,128)(2,1)S(1)}, bf16[320,128]{1,0:T(8,128)(2,1)S(1)}, u32[]{:S(2)}, u32[]{:S(2)}) collective-permute-start(bf16[320,128]{1,0:T(8,128)(2,1)S(1)} %get-tuple-element.95), channel_id=1, source_target_pairs={{0,128},{64,192},{128,0},{192,64},{1,129},{65,193},{129,1},{193,65... | collective-permute-start | bytes 245768 | tf_op jit(solution)/shard_map/ppermute | solution.py:40
  147.8 5.9 %collective-permute-start.21 = (bf16[320,128]{1,0:T(8,128)(2,1)S(1)}, bf16[320,128]{1,0:T(8,128)(2,1)S(1)}, u32[]{:S(2)}, u32[]{:S(2)}) collective-permute-start(bf16[320,128]{1,0:T(8,128)(2,1)S(1)} %get-tuple-element.96), channel_id=1, source_target_pairs={{0,192},{64,0},{128,64},{192,128},{1,193},{65,1},{129,65},{193,129... | collective-permute-start | bytes 245768 | tf_op jit(solution)/shard_map/ppermute | solution.py:40
  155.0 7.8 %collective-permute-start.23 = (bf16[160,256]{1,0:T(8,128)(2,1)S(1)}, bf16[160,256]{1,0:T(8,128)(2,1)S(1)}, u32[]{:S(2)}, u32[]{:S(2)}) collective-permute-start(bf16[160,256]{1,0:T(8,128)(2,1)S(1)} %get-tuple-element.128), channel_id=1, source_target_pairs={{0,64},{64,128},{128,192},{192,0},{1,65},{65,129},{129,193},{193,1... | collective-permute-start | bytes 245768 | tf_op jit(solution)/shard_map/ppermute | solution.py:40
  156.5 6.3 %collective-permute-start.24 = (bf16[160,256]{1,0:T(8,128)(2,1)S(1)}, bf16[160,256]{1,0:T(8,128)(2,1)S(1)}, u32[]{:S(2)}, u32[]{:S(2)}) collective-permute-start(bf16[160,256]{1,0:T(8,128)(2,1)S(1)} %get-tuple-element.127), channel_id=1, source_target_pairs={{0,128},{64,192},{128,0},{192,64},{1,129},{65,193},{129,1},{193,65... | collective-permute-start | bytes 245768 | tf_op jit(solution)/shard_map/ppermute | solution.py:40
  159.3 4.6 %collective-permute-start.25 = (bf16[160,256]{1,0:T(8,128)(2,1)S(1)}, bf16[160,256]{1,0:T(8,128)(2,1)S(1)}, u32[]{:S(2)}, u32[]{:S(2)}) collective-permute-start(bf16[160,256]{1,0:T(8,128)(2,1)S(1)} %get-tuple-element.126), channel_id=1, source_target_pairs={{0,192},{64,0},{128,64},{192,128},{1,193},{65,1},{129,65},{193,129... | collective-permute-start | bytes 245768 | tf_op jit(solution)/shard_map/ppermute | solution.py:40
  161.8 8.5 %collective-permute-start.22 = (bf16[4,80,128]{2,1,0:T(8,128)(2,1)S(1)}, bf16[4,80,128]{2,1,0:T(8,128)(2,1)S(1)}, u32[]{:S(2)}, u32[]{:S(2)}) collective-permute-start(bf16[4,80,128]{2,1,0:T(8,128)(2,1)S(1)} %dynamic-slice_bitcast_fusion.1), channel_id=1, source_target_pairs={{0,8},{2,10},{4,12},{6,14},{8,0},{10,2},{12,4},{14,6},{1,9},{3,11}... | collective-permute-start | bytes 245768 | tf_op jit(solution)/shard_map/ppermute | solution.py:44
  171.4 6.0 %collective-permute-start.29 = (bf16[80,128]{1,0:T(8,128)(2,1)S(1)}, bf16[80,128]{1,0:T(8,128)(2,1)S(1)}, u32[]{:S(2)}, u32[]{:S(2)}) collective-permute-start(bf16[80,128]{1,0:T(8,128)(2,1)S(1)} %get-tuple-element.131), channel_id=1, source_target_pairs={{0,16},{16,32},{32,48},{48,0},{1,17},{17,33},{33,49},{49,1},{2,18}... | collective-permute-start | bytes 61448 | tf_op jit(solution)/shard_map/ppermute | solution.py:40
  171.4 8.3 %collective-permute-start.30 = (bf16[80,128]{1,0:T(8,128)(2,1)S(1)}, bf16[80,128]{1,0:T(8,128)(2,1)S(1)}, u32[]{:S(2)}, u32[]{:S(2)}) collective-permute-start(bf16[80,128]{1,0:T(8,128)(2,1)S(1)} %get-tuple-element.130), channel_id=1, source_target_pairs={{0,32},{16,48},{32,0},{48,16},{1,33},{17,49},{33,1},{49,17},{2,34}... | collective-permute-start | bytes 61448 | tf_op jit(solution)/shard_map/ppermute | solution.py:40
  172.7 7.1 %collective-permute-start.31 = (bf16[80,128]{1,0:T(8,128)(2,1)S(1)}, bf16[80,128]{1,0:T(8,128)(2,1)S(1)}, u32[]{:S(2)}, u32[]{:S(2)}) collective-permute-start(bf16[80,128]{1,0:T(8,128)(2,1)S(1)} %get-tuple-element.129), channel_id=1, source_target_pairs={{0,48},{16,0},{32,16},{48,32},{1,49},{17,1},{33,17},{49,33},{2,50}... | collective-permute-start | bytes 61448 | tf_op jit(solution)/shard_map/ppermute | solution.py:40
  174.7 5.0 %collective-permute-start.26 = (bf16[80,128]{1,0:T(8,128)(2,1)S(1)}, bf16[80,128]{1,0:T(8,128)(2,1)S(1)}, u32[]{:S(2)}, u32[]{:S(2)}) collective-permute-start(bf16[80,128]{1,0:T(8,128)(2,1)S(1)} %get-tuple-element.134), channel_id=1, source_target_pairs={{0,2},{2,0},{4,6},{6,4},{8,10},{10,8},{12,14},{14,12},{1,3},{3,1},... | collective-permute-start | bytes 61448 | tf_op jit(solution)/shard_map/ppermute | solution.py:44
  177.3 4.7 %collective-permute-start.27 = (bf16[80,128]{1,0:T(8,128)(2,1)S(1)}, bf16[80,128]{1,0:T(8,128)(2,1)S(1)}, u32[]{:S(2)}, u32[]{:S(2)}) collective-permute-start(bf16[80,128]{1,0:T(8,128)(2,1)S(1)} %get-tuple-element.133), channel_id=1, source_target_pairs={{0,4},{2,6},{4,0},{6,2},{8,12},{10,14},{12,8},{14,10},{1,5},{3,7},... | collective-permute-start | bytes 61448 | tf_op jit(solution)/shard_map/ppermute | solution.py:44
  177.4 5.6 %collective-permute-start.28 = (bf16[80,128]{1,0:T(8,128)(2,1)S(1)}, bf16[80,128]{1,0:T(8,128)(2,1)S(1)}, u32[]{:S(2)}, u32[]{:S(2)}) collective-permute-start(bf16[80,128]{1,0:T(8,128)(2,1)S(1)} %get-tuple-element.132), channel_id=1, source_target_pairs={{0,6},{2,4},{4,2},{6,0},{8,14},{10,12},{12,10},{14,8},{1,7},{3,5},... | collective-permute-start | bytes 61448 | tf_op jit(solution)/shard_map/ppermute | solution.py:44
  (11 other events, 171.9 us)
Sparse Core Ops, SparseCore 0:
  9.9 77.8 all-gather.1
  109.8 43.1 reduce-scatter.1

commit v4 on v3

--- a/solution.py
+++ b/solution.py
@@ -11,8 +11,7 @@
 GROUP = 5
 KVH = 4
 SCALE = HD**-0.5
-RZ = 80
-RA = 40
+RZ = 104
 Y = ("yh", "yl")
 F32 = jnp.float32
 BF16 = jnp.bfloat16
@@ -147,64 +146,48 @@
     )(kv_grad, full_weight)
 
 
-def terms_kernel(place, ha, hb, pair, *refs):
-    a_out, b_out, by_yh = refs[:4], refs[4:8], refs[8]
-    for yh in range(2):
-        for x in range(4):
-            block = (2 * x + yh) * HD
-            by_yh[yh, :, x * HD : (x + 1) * HD] = pair[:, block : block + HD]
+def terms_kernel(place, ha, pair, *outs):
     for k in range(4):
         at = pl.multiple_of(lax.rem(place[0] + k, 4) * 2 * HD, 2 * HD)
         cols = pair[:, pl.ds(at, 2 * HD)]
-        a_out[k][...] = jnp.dot(ha[...], cols, preferred_element_type=F32).astype(BF16)
-    for k in range(4):
-        there = lax.rem(place[1] + k, 4)
-        yl, yh = lax.rem(there, 2), lax.div(there, 2)
-        b_out[k][...] = jnp.dot(hb[yl], by_yh[yh], preferred_element_type=F32).astype(BF16)
+        outs[k][...] = jnp.dot(ha[...], cols, preferred_element_type=F32).astype(BF16)
 
 
 VMEM = pl.BlockSpec(memory_space=pltpu.VMEM)
 SMEM = pl.BlockSpec(memory_space=pltpu.SMEM)
 
 
-def terms(place, ha, hb, pair):
-    a_shape = jax.ShapeDtypeStruct((ha.shape[0], 2 * HD), BF16)
-    b_shape = jax.ShapeDtypeStruct((hb.shape[1], 4 * HD), BF16)
+def terms(place, ha, pair):
     return pl.pallas_call(
         terms_kernel,
-        in_specs=[SMEM, VMEM, VMEM, VMEM],
-        out_specs=[VMEM] * 8,
-        out_shape=[a_shape] * 4 + [b_shape] * 4,
-        scratch_shapes=[pltpu.VMEM((2, pair.shape[0], 4 * HD), BF16)],
+        in_specs=[SMEM, VMEM, VMEM],
+        out_specs=[VMEM] * 4,
+        out_shape=[jax.ShapeDtypeStruct((ha.shape[0], 2 * HD), BF16)] * 4,
         compiler_params=pltpu.CompilerParams(vmem_limit_bytes=24 * 2**20),
-    )(place, ha, hb, pair)
+    )(place, ha, pair)
 
 
 def turn_kernel(place, *refs):
-    a_in, b_in, a_out, b_out, a_sum, b_sum = refs[:4], refs[4:8], refs[8:12], refs[12:16], *refs[16:]
-    a_sum[...] = add_up([r[...] for r in a_in]).astype(BF16)
-    b_sum[...] = add_up([r[...] for r in b_in]).astype(BF16)
-    half = a_sum.shape[0] // 2
+    parts, outs, total = refs[:4], refs[4:8], refs[8]
+    total[...] = add_up([r[...] for r in parts]).astype(BF16)
+    half = total.shape[0] // 2
     for k in range(4):
         there = lax.rem(place[1] + k, 4)
         row = pl.multiple_of(lax.rem(there, 2) * half, half)
         col = pl.multiple_of(lax.div(there, 2) * HD, HD)
-        a_out[k][...] = a_sum[pl.ds(row, half), pl.ds(col, HD)]
-        col = pl.multiple_of(lax.rem(place[0] + k, 4) * HD, HD)
-        b_out[k][...] = b_sum[:, pl.ds(col, HD)]
-
-
-def turn(place, a_in, b_in):
-    rows = b_in[0].shape[0]
-    shape = jax.ShapeDtypeStruct((rows, HD), BF16)
+        outs[k][...] = total[pl.ds(row, half), pl.ds(col, HD)]
+
+
+def turn(place, parts):
+    rows = parts[0].shape[0]
     return pl.pallas_call(
         turn_kernel,
-        in_specs=[SMEM] + [VMEM] * 8,
-        out_specs=[VMEM] * 8,
-        out_shape=[shape] * 8,
-        scratch_shapes=[pltpu.VMEM(a_in[0].shape, BF16), pltpu.VMEM(b_in[0].shape, BF16)],
+        in_specs=[SMEM] + [VMEM] * 4,
+        out_specs=[VMEM] * 4,
+        out_shape=[jax.ShapeDtypeStruct((rows // 2, HD), BF16)] * 4,
+        scratch_shapes=[pltpu.VMEM(parts[0].shape, BF16)],
         compiler_params=pltpu.CompilerParams(vmem_limit_bytes=24 * 2**20),
-    )(place, *a_in, *b_in)
+    )(place, *parts)
 
 
 def pick(v, index, axis):
@@ -250,10 +233,8 @@
     theirs = shift(pick(hidden_t, 1 - c, 1), "c", 2, 1)
     hidden_pair = jnp.concatenate([mine, theirs], axis=-1).reshape(2, 8, rows, 2 * length)
     hz = jnp.transpose(hidden_pair[:, :, :RZ], (1, 0, 2, 3)).reshape(16 * RZ, 2 * length)
-    ha = hidden_pair[:, :, RZ : RZ + RA].reshape(16 * RA, 2 * length)
-    hb = hidden_pair[:, :, RZ + RA :].reshape(2, 8 * RA, 2 * length)
-
-    hidden, hz, ha, hb = barrier((hidden, hz, ha, hb))
+    ha = hidden_pair[:, :, RZ:].reshape(16 * (rows - RZ), 2 * length)
+    hidden, hz, ha = barrier((hidden, hz, ha))
 
     kv_pre = jnp.dot(hidden, full_weight, preferred_element_type=F32)
     query_grad, kv_grad = attention_backward(kv_pre, queries, upstream, pos, weight)
@@ -264,44 +245,28 @@
 
     place = jnp.stack([x, y])
 
-    def block_y(v, k):
-        there = lax.rem(y + k, 4)
-        v = v.reshape(2, -1, 2 * HD)
-        at = (lax.rem(there, 2), 0, there // 2 * HD)
-        return lax.dynamic_slice(v, at, (1, v.shape[1], HD))[0]
-
-    def block_x(v, k, width):
-        return lax.dynamic_slice_in_dim(v, lax.rem(x + k, 4) * width, width, axis=1)
-
-    out = barrier(tuple(terms(place, ha, hb, pair)) + (kv_grad,))
+    out = barrier(tuple(terms(place, ha, pair)) + (kv_grad,))
     sent = tuple(shift(out[k], "x", 4, k) for k in (1, 2, 3))
-    sent += tuple(shift(out[4 + k], Y, 4, k) for k in (1, 2, 3))
-    hidden_grad = hidden_gradient(out[8], full_weight)
+    hidden_grad = hidden_gradient(out[4], full_weight)
     arrived = barrier(sent + (hidden_grad,))
-    hidden_grad = arrived[6]
-    out = turn(place, (out[0], *arrived[:3]), (out[4], *arrived[3:6]))
-    arrived = barrier(
-        tuple(shift(out[k], Y, 4, k) for k in (1, 2, 3))
-        + tuple(shift(out[4 + k], "x", 4, k) for k in (1, 2, 3))
-    )
-    a = add_up([out[0], *arrived[:3]]).reshape(8, RA, HD)
-    b = add_up([out[4], *arrived[3:]]).reshape(8, RA, HD)
-    ab = jnp.concatenate([a, b], axis=1).astype(BF16).reshape(2, 4, 2 * RA, HD)
-
-    ab, sum_z = barrier((ab, sum_z))
-    arrived = barrier(
-        (swap(pick(ab, 1 - z // 4, 0), "z", 8, 4),)
-        + tuple(shift(block_x(sum_z, k, 2 * HD), "x", 4, k) for k in (1, 2, 3))
-    )
-    ab = add_up([pick(ab, z // 4, 0), arrived[0]]).astype(BF16)
-    s = add_up([block_x(sum_z, 0, 2 * HD), *arrived[1:]]).astype(BF16)
-    arrived = barrier(
-        tuple(swap(pick(ab, lax.rem(z, 4) ^ k, 0), "z", 8, k) for k in (1, 2, 3))
-        + tuple(shift(block_y(s, k), Y, 4, k) for k in (1, 2, 3))
-    )
-    ab = add_up([pick(ab, lax.rem(z, 4), 0), *arrived[:3]])
-    s = add_up([block_y(s, 0), *arrived[3:]])
-    summed = jnp.concatenate([s, ab], axis=0)
+    hidden_grad = arrived[3]
+    out = turn(place, (out[0], *arrived[:3]))
+    arrived = barrier(tuple(shift(out[k], Y, 4, k) for k in (1, 2, 3)))
+    a = add_up([out[0], *arrived]).astype(BF16).reshape(2, 4, rows - RZ, HD)
+    a = add_up([pick(a, z // 4, 0), swap(pick(a, 1 - z // 4, 0), "z", 8, 4)]).astype(BF16)
+    sent = tuple(swap(pick(a, lax.rem(z, 4) ^ k, 0), "z", 8, k) for k in (1, 2, 3))
+
+    blocks = jnp.stack([sum_z[:, j * HD : (j + 1) * HD] for j in range(8)]).reshape(16, RZ, HD)
+    blocks, a = barrier((blocks, a))
+    arrived = lax.all_to_all(blocks, ("x", *Y), 0, 0, tiled=True)
+    arrived = barrier((arrived, *sent))
+    summed = jnp.concatenate(
+        [
+            jnp.sum(arrived[0].astype(F32), axis=0),
+            add_up([pick(a, lax.rem(z, 4), 0), *arrived[1:]]),
+        ],
+        axis=0,
+    )
     weight_grad = summed / F32(total_tokens)
     new_moment_one = 0.9 * moment_one + 0.1 * weight_grad
     new_moment_two = 0.999 * moment_two + 0.001 * weight_grad * weight_grad

time: 191 us -> 197 us (1.031)
  starting transfers between devices: 53.4 us -> 37.9 us
  waiting for transfers between devices: 66.8 us -> 77.5 us
  local copies, waits for them, and re-layouts: 13.5 us -> 23.2 us
    ppermute x20 -> x8, starting transfers between devices: 35.6 us -> 11.2 us  [shift(): return lax.ppermute(v, axis, [(i, (i + k) % n) for i in range(n)])]
    unnamed x20 -> x25, local copies, waits for them, and re-layouts: 5.4 us -> 14.4 us
    all_to_all x0 -> x1, starting transfers between devices: none -> 7.28 us  [body(): arrived = lax.all_to_all(blocks, ('x', *Y), 0, 0, tiled=True)]
    ppermute x20 -> x8, waiting for transfers between devices: 8.44 us -> 15.3 us  [shift(): return lax.ppermute(v, axis, [(i, (i + k) % n) for i in range(n)])]
    reduce_scatter x1, waiting for transfers between devices: 0.02 us -> 2.3 us  [body(): sum_z = lax.psum_scatter(part_z, 'z', scatter_dimension=0, tiled=True)]
  transfers between devices with their start and end apart: 34 -> 23, of which waited for: 14 -> 17; matrix products, arithmetic and copies ran while one was open for 9% -> 10% of each run, Pallas kernels for 7% -> 6%
where the time goes in v4:
time: 197 us; the launch traced here: 196 us
  waiting for transfers between devices  77.5 us (39%)
  starting transfers between devices  37.9 us (19%)
  local copies, waits for them, and re-layouts  23.2 us (12%)
  Pallas kernels  22.9 us (12%)
  between operations  15.7 us (8%)
  matrix products  10.3 us (5%)
  other arithmetic  8.13 us (4%)
    ppermute x12, waiting for transfers between devices, swap(): return lax.ppermute(v, axis, [(i, i ^ bit) for i in range(n)])  31.1 us
    all_gather x1, waiting for transfers between devices, body(): lax.all_gather(kv_weight, ('yl', 'z', 'c'), axis=0, tiled=True)  28.1 us
    ppermute x12, starting transfers between devices, swap(): return lax.ppermute(v, axis, [(i, i ^ bit) for i in range(n)])  19.4 us
    ppermute x8, waiting for transfers between devices, shift(): return lax.ppermute(v, axis, [(i, (i + k) % n) for i in range(n)])  15.3 us
    unnamed x25, local copies, waits for them, and re-layouts  14.4 us
    ppermute x8, starting transfers between devices, shift(): return lax.ppermute(v, axis, [(i, (i + k) % n) for i in range(n)])  11.2 us
    pallas_call x1, Pallas kernels, attention_backward(): pl.pallas_call(attention_kernel, grid=(KVH,), in_specs=[pl.BlockSpec((len...  10.4 us
    pallas_call x1, Pallas kernels, hidden_gradient(): pl.pallas_call(hidden_grad_kernel, grid=(8,), in_specs=[pl.BlockSpec((len...  9.83 us
  transfers between devices with their start and end apart: 23, of which 17 were waited for; matrix products, arithmetic and copies ran while one was open for 10% of the time, Pallas kernels for 6%

profile of v4, /device:TPU:2, one launch (start us, length us, event | category | flops | bytes accessed | tf_op | source)
XLA Modules:
  0.0 195.7 jit_solution(10098386591836295675)
XLA Ops:
  13.3 4.4 %copy.27 = bf16[256,5120]{0,1:T(8,128)(2,1)} copy(bf16[256,5120]{1,0:T(8,128)(2,1)} %param.10) | data formatting | bytes 5242880 | tf_op args[0]
  18.4 2.4 %collective-permute-start.2 = (f32[8,128]{1,0:T(8,128)S(1)}, f32[8,128]{1,0:T(8,128)S(1)}, u32[]{:S(2)}, u32[]{:S(2)}) collective-permute-start(f32[8,128]{1,0:T(8,128)S(1)} %broadcast_add_fusion), channel_id=1, source_target_pairs={{0,64},{64,0},{128,192},{192,128},{1,65},{65,1},{129,193},{193,129... | collective-permute-start | bytes 12296 | tf_op jit(solution)/shard_map/ppermute | solution.py:43
  20.7 3.0 %dynamic-slice_bitcast_fusion = (bf16[16,160,256]{2,1,0:T(8,128)(2,1)}, bf16[16,1,160,256]{3,2,1,0:T(8,128)(2,1)S(1)}) fusion(bf16[16,2,160,256]{3,2,1,0:T(8,128)(2,1)} %bitcast.93, s32[]{:T(128)S(6)} %select_n.58, s32[]{:T(128)S(6)} %select_n.57), kind=kLoop, calls=%fused_computation.5 | loop fusion | bytes 5242888 | tf_op jit(solution)/shard_map/jit(dynamic_index_in_dim)/squeeze | solution.py:194
  25.4 4.4 %collective-permute-done.3 = f32[8,128]{1,0:T(8,128)S(1)} collective-permute-done((f32[8,128]{1,0:T(8,128)S(1)}, f32[8,128]{1,0:T(8,128)S(1)}, u32[]{:S(2)}, u32[]{:S(2)}) %collective-permute-start.3) | collective-permute-done | bytes 4128 | tf_op jit(solution)/shard_map/ppermute | solution.py:43
  29.8 3.6 %collective-permute-done.4 = f32[8,128]{1,0:T(8,128)S(1)} collective-permute-done((f32[8,128]{1,0:T(8,128)S(1)}, f32[8,128]{1,0:T(8,128)S(1)}, u32[]{:S(2)}, u32[]{:S(2)}) %collective-permute-start.4) | collective-permute-done | bytes 4128 | tf_op jit(solution)/shard_map/ppermute | solution.py:43
  33.4 1.5 collective-permute-start.5
  35.4 3.2 %collective-permute-done.5 = f32[8,128]{1,0:T(8,128)S(1)} collective-permute-done((f32[8,128]{1,0:T(8,128)S(1)}, f32[8,128]{1,0:T(8,128)S(1)}, u32[]{:S(2)}, u32[]{:S(2)}) %collective-permute-start.5) | collective-permute-done | bytes 4128 | tf_op jit(solution)/shard_map/ppermute | solution.py:43
  38.7 3.5 %collective-permute-done.6 = f32[8,128]{1,0:T(8,128)S(1)} collective-permute-done((f32[8,128]{1,0:T(8,128)S(1)}, f32[8,128]{1,0:T(8,128)S(1)}, u32[]{:S(2)}, u32[]{:S(2)}) %collective-permute-start.6) | collective-permute-done | bytes 4128 | tf_op jit(solution)/shard_map/ppermute | solution.py:43
  42.2 1.5 collective-permute-start.7
  43.8 3.0 %collective-permute-done.7 = f32[8,128]{1,0:T(8,128)S(1)} collective-permute-done((f32[8,128]{1,0:T(8,128)S(1)}, f32[8,128]{1,0:T(8,128)S(1)}, u32[]{:S(2)}, u32[]{:S(2)}) %collective-permute-start.7) | collective-permute-done | bytes 4128 | tf_op jit(solution)/shard_map/ppermute | solution.py:43
  46.8 5.4 %collective-permute-start.8 = (f32[8,128]{1,0:T(8,128)S(1)}, f32[8,128]{1,0:T(8,128)S(1)}, u32[]{:S(2)}, u32[]{:S(2)}) collective-permute-start(f32[8,128]{1,0:T(8,128)S(1)} %add.111), channel_id=1, source_target_pairs={{0,8},{2,10},{4,12},{6,14},{8,0},{10,2},{12,4},{14,6},{1,9},{3,11}... | collective-permute-start | bytes 12296 | tf_op jit(solution)/shard_map/ppermute | solution.py:43
  52.6 1.8 collective-permute-done.8
  59.6 28.1 %all-gather.2.cloned.1.call-done.w = bf16[5120,1024]{1,0:T(8,128)(2,1)} async-done(((bf16[160,1024]{1,0:T(8,128)(2,1)}), bf16[5120,1024]{1,0:T(8,128)(2,1)}) %all-gather.2.cloned.1.call-update) | async-done | bytes 10485776 | tf_op jit(solution)/shard_map/all_gather | solution.py:223
  87.7 6.5 %fusion.17.kpre.vpre = f32[256,1024]{1,0:T(8,128)S(1)} fusion(bf16[256,5120]{1,0:T(8,128)(2,1)} %param.10, bf16[5120,1024]{1,0:T(8,128)(2,1)} %all-gather.2.cloned.1.call-done.w), kind=kOutput, calls=%fused_computation.66 | convolution fusion | flops 2684354560 | bytes 14155776 | tf_op jit(solution)/shard_map/dot_general | solution.py:239
  94.3 10.4 %shard_map.137 = (bf16[256,2560]{1,0:T(8,128)(2,1)}, bf16[256,1024]{1,0:T(8,128)(2,1)S(1)}) custom-call(f32[256,1024]{1,0:T(8,128)S(1)} %fusion.17.kpre.vpre, f32[256,1024]{1,0:T(8,128)S(1)} %fusion.17.kpre.vpre, bf16[256,2560]{1,0:T(8,128)(2,1)S(1)} %copy-done, bf16[256,2560]{1,0:T(8,128)(2,1)S(1)} %copy-done.1, f32[256,128]{1,0:T(8,128)S(1)} %get-tuple-element.80.cos, ...), custom_call_target="tpu_custom_call" | custom-call | tf_op jit(solution)/shard_map/pallas_call | solution.py:103
  104.9 1.6 collective-permute-done.9
  106.6 3.8 %convolution_convert_fusion = bf16[1664,1024]{1,0:T(8,128)(2,1)} fusion(bf16[1664,512]{1,0:T(8,128)(2,1)S(1)} %bitcast.94, bf16[512,1024]{1,0:T(8,128)(2,1)S(1)} %constant_dynamic-update-slice_fusion.pair), kind=kOutput, calls=%fused_computation | convolution fusion | flops 1746534400 | bytes 6160384 | tf_op jit(solution)/shard_map/dot_general | solution.py:243
  110.5 1.7 shard_map.138
  112.2 1.9 collective-permute-start.10
  114.9 2.4 %collective-permute-start.12 = (bf16[896,256]{1,0:T(8,128)(2,1)S(1)}, bf16[896,256]{1,0:T(8,128)(2,1)S(1)}, u32[]{:S(2)}, u32[]{:S(2)}) collective-permute-start(bf16[896,256]{1,0:T(8,128)(2,1)S(1)} %get-tuple-element.46), channel_id=1, source_target_pairs={{0,192},{64,0},{128,64},{192,128},{1,193},{65,1},{129,65},{193,129... | collective-permute-start | bytes 1376264 | tf_op jit(solution)/shard_map/ppermute | solution.py:39
  117.3 9.8 %shard_map.139 = bf16[256,5120]{1,0:T(8,128)(2,1)} custom-call(bf16[256,1024]{1,0:T(8,128)(2,1)S(1)} %get-tuple-element.47.kv, bf16[5120,1024]{1,0:T(8,128)(2,1)} %all-gather.2.cloned.1.call-done.w), custom_call_target="tpu_custom_call" | custom-call | tf_op jit(solution)/shard_map/pallas_call | solution.py:136
  127.2 6.9 %collective-permute-done.10.refs_1_ = bf16[896,256]{1,0:T(8,128)(2,1)S(1)} collective-permute-done((bf16[896,256]{1,0:T(8,128)(2,1)S(1)}, bf16[896,256]{1,0:T(8,128)(2,1)S(1)}, u32[]{:S(2)}, u32[]{:S(2)}) %collective-permute-start.10) | collective-permute-done | bytes 458784 | tf_op jit(solution)/shard_map/ppermute | solution.py:39
  134.1 2.9 %collective-permute-done.12.refs_3_ = bf16[896,256]{1,0:T(8,128)(2,1)S(1)} collective-permute-done((bf16[896,256]{1,0:T(8,128)(2,1)S(1)}, bf16[896,256]{1,0:T(8,128)(2,1)S(1)}, u32[]{:S(2)}, u32[]{:S(2)}) %collective-permute-start.12) | collective-permute-done | bytes 458784 | tf_op jit(solution)/shard_map/ppermute | solution.py:39
  139.5 2.7 %collective-permute-start.14 = (bf16[448,128]{1,0:T(8,128)(2,1)S(1)}, bf16[448,128]{1,0:T(8,128)(2,1)S(1)}, u32[]{:S(2)}, u32[]{:S(2)}) collective-permute-start(bf16[448,128]{1,0:T(8,128)(2,1)S(1)} %get-tuple-element.56), channel_id=1, source_target_pairs={{0,32},{16,48},{32,0},{48,16},{1,33},{17,49},{33,1},{49,17},{2,34}... | collective-permute-start | bytes 344072 | tf_op jit(solution)/shard_map/ppermute | solution.py:39
  142.2 1.5 collective-permute-start.15
  145.0 2.3 %collective-permute-done.14 = bf16[448,128]{1,0:T(8,128)(2,1)S(1)} collective-permute-done((bf16[448,128]{1,0:T(8,128)(2,1)S(1)}, bf16[448,128]{1,0:T(8,128)(2,1)S(1)}, u32[]{:S(2)}, u32[]{:S(2)}) %collective-permute-start.14) | collective-permute-done | bytes 114720 | tf_op jit(solution)/shard_map/ppermute | solution.py:39
  147.6 3.2 %collective-permute-start.16 = (bf16[4,56,128]{2,1,0:T(8,128)(2,1)S(1)}, bf16[4,56,128]{2,1,0:T(8,128)(2,1)S(1)}, u32[]{:S(2)}, u32[]{:S(2)}) collective-permute-start(bf16[4,56,128]{2,1,0:T(8,128)(2,1)S(1)} %dynamic-slice_bitcast_fusion.1), channel_id=1, source_target_pairs={{0,8},{2,10},{4,12},{6,14},{8,0},{10,2},{12,4},{14,6},{1,9},{3,11}... | collective-permute-start | bytes 172040 | tf_op jit(solution)/shard_map/ppermute | solution.py:43
  150.8 7.0 %collective-permute-done.16 = bf16[4,56,128]{2,1,0:T(8,128)(2,1)S(1)} collective-permute-done((bf16[4,56,128]{2,1,0:T(8,128)(2,1)S(1)}, bf16[4,56,128]{2,1,0:T(8,128)(2,1)S(1)}, u32[]{:S(2)}, u32[]{:S(2)}) %collective-permute-start.16) | collective-permute-done | bytes 57376 | tf_op jit(solution)/shard_map/ppermute | solution.py:43
  157.8 2.3 %reduce-scatter.2.cloned.1.call-done = bf16[208,1024]{1,0:T(8,128)(2,1)} async-done(((bf16[1664,1024]{1,0:T(8,128)(2,1)}), bf16[208,1024]{1,0:T(8,128)(2,1)}) %reduce-scatter.2.cloned.1.call-update) | async-done | bytes 426000 | tf_op jit(solution)/shard_map/reduce_scatter | solution.py:244
  171.5 7.3 %all-to-all-start = ((bf16[16,104,128]{2,1,0:T(8,128)(2,1)}), bf16[16,104,128]{2,1,0:T(8,128)(2,1)S(1)}, u32[]{:S(2)}, u32[]{:S(2)}) async-start(bf16[16,104,128]{2,1,0:T(8,128)(2,1)} %bitcast.33), calls=%async_computation.1 | async-start | bytes 851968 | tf_op jit(solution)/shard_map/all_to_all | solution.py:261
  179.5 3.0 %collective-permute-start.18 = (bf16[56,128]{1,0:T(8,128)(2,1)S(1)}, bf16[56,128]{1,0:T(8,128)(2,1)S(1)}, u32[]{:S(2)}, u32[]{:S(2)}) collective-permute-start(bf16[56,128]{1,0:T(8,128)(2,1)S(1)} %get-tuple-element.75), channel_id=1, source_target_pairs={{0,4},{2,6},{4,0},{6,2},{8,12},{10,14},{12,8},{14,10},{1,5},{3,7},... | collective-permute-start | bytes 43016 | tf_op jit(solution)/shard_map/ppermute | solution.py:43
  184.1 3.8 %collective-permute-done.19 = bf16[56,128]{1,0:T(8,128)(2,1)S(1)} collective-permute-done((bf16[56,128]{1,0:T(8,128)(2,1)S(1)}, bf16[56,128]{1,0:T(8,128)(2,1)S(1)}, u32[]{:S(2)}, u32[]{:S(2)}) %collective-permute-start.19) | collective-permute-done | bytes 14368 | tf_op jit(solution)/shard_map/ppermute | solution.py:43
  (90 shorter events, 33.3 us)
Async XLA Ops:
  7.2 80.6 %all-gather.2.cloned.1.call-start = ((), (), s32[]{:S(2)}) async-start(), calls=%async_computation.2 | async-start | bytes 10813440 | tf_op jit(solution)/shard_map/all_gather | solution.py:223
  7.9 152.2 %reduce-scatter.2.cloned.1.call-start = ((), (), s32[]{:S(2)}) async-start(), calls=%async_computation.3 | async-start | bytes 3833856 | tf_op jit(solution)/shard_map/reduce_scatter | solution.py:244
  13.2 4.5 %collective-permute-start.1 = (f32[8,128]{1,0:T(8,128)S(1)}, f32[8,128]{1,0:T(8,128)S(1)}, u32[]{:S(2)}, u32[]{:S(2)}) collective-permute-start(f32[8,128]{1,0:T(8,128)S(1)} %broadcast_in_dim.57), channel_id=1, source_target_pairs={{0,1},{1,0},{2,3},{3,2},{4,5},{5,4},{6,7},{7,6},{8,9},{9,8},{10,11... | collective-permute-start | bytes 12296 | tf_op jit(solution)/shard_map/ppermute | solution.py:43
  18.4 5.5 %collective-permute-start.2 = (f32[8,128]{1,0:T(8,128)S(1)}, f32[8,128]{1,0:T(8,128)S(1)}, u32[]{:S(2)}, u32[]{:S(2)}) collective-permute-start(f32[8,128]{1,0:T(8,128)S(1)} %broadcast_add_fusion), channel_id=1, source_target_pairs={{0,64},{64,0},{128,192},{192,128},{1,65},{65,1},{129,193},{193,129... | collective-permute-start | bytes 12296 | tf_op jit(solution)/shard_map/ppermute | solution.py:43
  20.7 31.5 %copy-start.6 = (s32[1,256]{1,0:T(1,128)S(1)}, s32[1,256]{1,0:T(1,128)}, u32[]{:S(2)}) copy-start(s32[1,256]{1,0:T(1,128)} %param.13) | copy-start | bytes 3076
  20.7 31.5 %copy-start.7 = (f32[1,4]{1,0:T(1,128)S(1)}, f32[1,4]{1,0:T(1,128)}, u32[]{:S(2)}) copy-start(f32[1,4]{1,0:T(1,128)} %param.15) | copy-start | bytes 52
  23.7 32.1 %collective-permute-start = (bf16[16,160,256]{2,1,0:T(8,128)(2,1)}, bf16[16,160,256]{2,1,0:T(8,128)(2,1)}, u32[]{:S(2)}, u32[]{:S(2)}) collective-permute-start(bf16[16,160,256]{2,1,0:T(8,128)(2,1)} %get-tuple-element.72), channel_id=1, source_target_pairs={{0,1},{1,0},{2,3},{3,2},{4,5},{5,4},{6,7},{7,6},{8,9},{9,8},{10,11... | collective-permute-start | bytes 3932168 | tf_op jit(solution)/shard_map/ppermute | solution.py:39
  24.6 5.2 %collective-permute-start.3 = (f32[8,128]{1,0:T(8,128)S(1)}, f32[8,128]{1,0:T(8,128)S(1)}, u32[]{:S(2)}, u32[]{:S(2)}) collective-permute-start(f32[8,128]{1,0:T(8,128)S(1)} %fusion.22), channel_id=1, source_target_pairs={{0,128},{64,192},{128,0},{192,64},{1,129},{65,193},{129,1},{193,65... | collective-permute-start | bytes 12296 | tf_op jit(solution)/shard_map/ppermute | solution.py:43
  29.8 3.6 %collective-permute-start.4 = (f32[8,128]{1,0:T(8,128)S(1)}, f32[8,128]{1,0:T(8,128)S(1)}, u32[]{:S(2)}, u32[]{:S(2)}) collective-permute-start(f32[8,128]{1,0:T(8,128)S(1)} %add.107), channel_id=1, source_target_pairs={{0,16},{16,0},{1,17},{17,1},{2,18},{18,2},{3,19},{19,3},{4,20},{20... | collective-permute-start | bytes 12296 | tf_op jit(solution)/shard_map/ppermute | solution.py:43
  33.4 5.2 %collective-permute-start.5 = (f32[8,128]{1,0:T(8,128)S(1)}, f32[8,128]{1,0:T(8,128)S(1)}, u32[]{:S(2)}, u32[]{:S(2)}) collective-permute-start(f32[8,128]{1,0:T(8,128)S(1)} %add.108), channel_id=1, source_target_pairs={{0,32},{32,0},{1,33},{33,1},{2,34},{34,2},{3,35},{35,3},{4,36},{36... | collective-permute-start | bytes 12296 | tf_op jit(solution)/shard_map/ppermute | solution.py:43
  38.6 3.6 %collective-permute-start.6 = (f32[8,128]{1,0:T(8,128)S(1)}, f32[8,128]{1,0:T(8,128)S(1)}, u32[]{:S(2)}, u32[]{:S(2)}) collective-permute-start(f32[8,128]{1,0:T(8,128)S(1)} %add.109), channel_id=1, source_target_pairs={{0,2},{2,0},{4,6},{6,4},{8,10},{10,8},{12,14},{14,12},{1,3},{3,1},... | collective-permute-start | bytes 12296 | tf_op jit(solution)/shard_map/ppermute | solution.py:43
  42.2 4.6 %collective-permute-start.7 = (f32[8,128]{1,0:T(8,128)S(1)}, f32[8,128]{1,0:T(8,128)S(1)}, u32[]{:S(2)}, u32[]{:S(2)}) collective-permute-start(f32[8,128]{1,0:T(8,128)S(1)} %add.110), channel_id=1, source_target_pairs={{0,4},{2,6},{4,0},{6,2},{8,12},{10,14},{12,8},{14,10},{1,5},{3,7},... | collective-permute-start | bytes 12296 | tf_op jit(solution)/shard_map/ppermute | solution.py:43
  46.8 7.6 %collective-permute-start.8 = (f32[8,128]{1,0:T(8,128)S(1)}, f32[8,128]{1,0:T(8,128)S(1)}, u32[]{:S(2)}, u32[]{:S(2)}) collective-permute-start(f32[8,128]{1,0:T(8,128)S(1)} %add.111), channel_id=1, source_target_pairs={{0,8},{2,10},{4,12},{6,14},{8,0},{10,2},{12,4},{14,6},{1,9},{3,11}... | collective-permute-start | bytes 12296 | tf_op jit(solution)/shard_map/ppermute | solution.py:43
  87.7 6.5 %copy-start = (bf16[256,2560]{1,0:T(8,128)(2,1)S(1)}, bf16[256,2560]{1,0:T(8,128)(2,1)}, u32[]{:S(2)}) copy-start(bf16[256,2560]{1,0:T(8,128)(2,1)} %q.1) | copy-start | bytes 3932164
  87.7 6.5 %copy-start.1 = (bf16[256,2560]{1,0:T(8,128)(2,1)S(1)}, bf16[256,2560]{1,0:T(8,128)(2,1)}, u32[]{:S(2)}) copy-start(bf16[256,2560]{1,0:T(8,128)(2,1)} %up.1) | copy-start | bytes 3932164
  104.6 2.0 copy-start.2
  104.6 1.9 collective-permute-start.9
  112.2 21.9 %collective-permute-start.10 = (bf16[896,256]{1,0:T(8,128)(2,1)S(1)}, bf16[896,256]{1,0:T(8,128)(2,1)S(1)}, u32[]{:S(2)}, u32[]{:S(2)}) collective-permute-start(bf16[896,256]{1,0:T(8,128)(2,1)S(1)} %get-tuple-element.44), channel_id=1, source_target_pairs={{0,64},{64,128},{128,192},{192,0},{1,65},{65,129},{129,193},{193,1... | collective-permute-start | bytes 1376264 | tf_op jit(solution)/shard_map/ppermute | solution.py:39
  114.1 20.0 %collective-permute-start.11 = (bf16[896,256]{1,0:T(8,128)(2,1)S(1)}, bf16[896,256]{1,0:T(8,128)(2,1)S(1)}, u32[]{:S(2)}, u32[]{:S(2)}) collective-permute-start(bf16[896,256]{1,0:T(8,128)(2,1)S(1)} %get-tuple-element.45), channel_id=1, source_target_pairs={{0,128},{64,192},{128,0},{192,64},{1,129},{65,193},{129,1},{193,65... | collective-permute-start | bytes 1376264 | tf_op jit(solution)/shard_map/ppermute | solution.py:39
  114.9 22.1 %collective-permute-start.12 = (bf16[896,256]{1,0:T(8,128)(2,1)S(1)}, bf16[896,256]{1,0:T(8,128)(2,1)S(1)}, u32[]{:S(2)}, u32[]{:S(2)}) collective-permute-start(bf16[896,256]{1,0:T(8,128)(2,1)S(1)} %get-tuple-element.46), channel_id=1, source_target_pairs={{0,192},{64,0},{128,64},{192,128},{1,193},{65,1},{129,65},{193,129... | collective-permute-start | bytes 1376264 | tf_op jit(solution)/shard_map/ppermute | solution.py:39
  138.1 50.0 %copy-start.3 = (f32[160,128]{1,0:T(8,128)S(1)}, f32[160,128]{1,0:T(8,128)}, u32[]{:S(2)}) copy-start(f32[160,128]{1,0:T(8,128)} %param.17) | copy-start | bytes 245764
  138.1 50.0 %copy-start.4 = (f32[160,128]{1,0:T(8,128)S(1)}, f32[160,128]{1,0:T(8,128)}, u32[]{:S(2)}) copy-start(f32[160,128]{1,0:T(8,128)} %param.18) | copy-start | bytes 245764
  138.1 50.0 %copy-start.5 = (f32[160,128]{1,0:T(8,128)S(1)}, f32[160,128]{1,0:T(8,128)}, u32[]{:S(2)}) copy-start(f32[160,128]{1,0:T(8,128)} %param.19) | copy-start | bytes 245764
  138.1 6.9 %collective-permute-start.13 = (bf16[448,128]{1,0:T(8,128)(2,1)S(1)}, bf16[448,128]{1,0:T(8,128)(2,1)S(1)}, u32[]{:S(2)}, u32[]{:S(2)}) collective-permute-start(bf16[448,128]{1,0:T(8,128)(2,1)S(1)} %get-tuple-element.55), channel_id=1, source_target_pairs={{0,16},{16,32},{32,48},{48,0},{1,17},{17,33},{33,49},{49,1},{2,18}... | collective-permute-start | bytes 344072 | tf_op jit(solution)/shard_map/ppermute | solution.py:39
  139.5 7.8 %collective-permute-start.14 = (bf16[448,128]{1,0:T(8,128)(2,1)S(1)}, bf16[448,128]{1,0:T(8,128)(2,1)S(1)}, u32[]{:S(2)}, u32[]{:S(2)}) collective-permute-start(bf16[448,128]{1,0:T(8,128)(2,1)S(1)} %get-tuple-element.56), channel_id=1, source_target_pairs={{0,32},{16,48},{32,0},{48,16},{1,33},{17,49},{33,1},{49,17},{2,34}... | collective-permute-start | bytes 344072 | tf_op jit(solution)/shard_map/ppermute | solution.py:39
  142.2 5.3 %collective-permute-start.15 = (bf16[448,128]{1,0:T(8,128)(2,1)S(1)}, bf16[448,128]{1,0:T(8,128)(2,1)S(1)}, u32[]{:S(2)}, u32[]{:S(2)}) collective-permute-start(bf16[448,128]{1,0:T(8,128)(2,1)S(1)} %get-tuple-element.57), channel_id=1, source_target_pairs={{0,48},{16,0},{32,16},{48,32},{1,49},{17,1},{33,17},{49,33},{2,50}... | collective-permute-start | bytes 344072 | tf_op jit(solution)/shard_map/ppermute | solution.py:39
  147.6 10.2 %collective-permute-start.16 = (bf16[4,56,128]{2,1,0:T(8,128)(2,1)S(1)}, bf16[4,56,128]{2,1,0:T(8,128)(2,1)S(1)}, u32[]{:S(2)}, u32[]{:S(2)}) collective-permute-start(bf16[4,56,128]{2,1,0:T(8,128)(2,1)S(1)} %dynamic-slice_bitcast_fusion.1), channel_id=1, source_target_pairs={{0,8},{2,10},{4,12},{6,14},{8,0},{10,2},{12,4},{14,6},{1,9},{3,11}... | collective-permute-start | bytes 172040 | tf_op jit(solution)/shard_map/ppermute | solution.py:43
  171.5 16.4 %all-to-all-start = ((bf16[16,104,128]{2,1,0:T(8,128)(2,1)}), bf16[16,104,128]{2,1,0:T(8,128)(2,1)S(1)}, u32[]{:S(2)}, u32[]{:S(2)}) async-start(bf16[16,104,128]{2,1,0:T(8,128)(2,1)} %bitcast.33), calls=%async_computation.1 | async-start | bytes 851968 | tf_op jit(solution)/shard_map/all_to_all | solution.py:261
  178.8 4.5 %collective-permute-start.17 = (bf16[56,128]{1,0:T(8,128)(2,1)S(1)}, bf16[56,128]{1,0:T(8,128)(2,1)S(1)}, u32[]{:S(2)}, u32[]{:S(2)}) collective-permute-start(bf16[56,128]{1,0:T(8,128)(2,1)S(1)} %get-tuple-element.76), channel_id=1, source_target_pairs={{0,2},{2,0},{4,6},{6,4},{8,10},{10,8},{12,14},{14,12},{1,3},{3,1},... | collective-permute-start | bytes 43016 | tf_op jit(solution)/shard_map/ppermute | solution.py:43
  179.5 4.7 %collective-permute-start.18 = (bf16[56,128]{1,0:T(8,128)(2,1)S(1)}, bf16[56,128]{1,0:T(8,128)(2,1)S(1)}, u32[]{:S(2)}, u32[]{:S(2)}) collective-permute-start(bf16[56,128]{1,0:T(8,128)(2,1)S(1)} %get-tuple-element.75), channel_id=1, source_target_pairs={{0,4},{2,6},{4,0},{6,2},{8,12},{10,14},{12,8},{14,10},{1,5},{3,7},... | collective-permute-start | bytes 43016 | tf_op jit(solution)/shard_map/ppermute | solution.py:43
  182.5 5.5 %collective-permute-start.19 = (bf16[56,128]{1,0:T(8,128)(2,1)S(1)}, bf16[56,128]{1,0:T(8,128)(2,1)S(1)}, u32[]{:S(2)}, u32[]{:S(2)}) collective-permute-start(bf16[56,128]{1,0:T(8,128)(2,1)S(1)} %get-tuple-element.74), channel_id=1, source_target_pairs={{0,6},{2,4},{4,2},{6,0},{8,14},{10,12},{12,10},{14,8},{1,7},{3,5},... | collective-permute-start | bytes 43016 | tf_op jit(solution)/shard_map/ppermute | solution.py:43
Sparse Core Ops, SparseCore 0:
  9.9 77.8 all-gather.1
  110.5 49.5 reduce-scatter.1

commit v5 on v4

--- a/solution.py
+++ b/solution.py
@@ -11,7 +11,7 @@
 GROUP = 5
 KVH = 4
 SCALE = HD**-0.5
-RZ = 104
+RZ = 96
 Y = ("yh", "yl")
 F32 = jnp.float32
 BF16 = jnp.bfloat16
@@ -146,6 +146,28 @@
     )(kv_grad, full_weight)
 
 
+def first_terms_kernel(h, pair, out):
+    term = jnp.dot(h[0], pair[...], preferred_element_type=F32).astype(BF16)
+    rows = h.shape[1]
+    for j in range(8):
+        out[j * rows : (j + 1) * rows, :] = term[:, j * HD : (j + 1) * HD]
+
+
+def first_terms(hz, pair):
+    planes, rows, depth = hz.shape
+    return pl.pallas_call(
+        first_terms_kernel,
+        grid=(planes,),
+        in_specs=[
+            pl.BlockSpec((1, rows, depth), lambda i: (i, 0, 0)),
+            pl.BlockSpec(pair.shape, lambda i: (0, 0)),
+        ],
+        out_specs=pl.BlockSpec((8 * rows, HD), lambda i: (i, 0)),
+        out_shape=jax.ShapeDtypeStruct((planes * 8 * rows, HD), BF16),
+        compiler_params=pltpu.CompilerParams(vmem_limit_bytes=24 * 2**20),
+    )(hz, pair)
+
+
 def terms_kernel(place, ha, pair, *outs):
     for k in range(4):
         at = pl.multiple_of(lax.rem(place[0] + k, 4) * 2 * HD, 2 * HD)
@@ -232,7 +254,7 @@
     mine = pick(hidden_t, c, 1)
     theirs = shift(pick(hidden_t, 1 - c, 1), "c", 2, 1)
     hidden_pair = jnp.concatenate([mine, theirs], axis=-1).reshape(2, 8, rows, 2 * length)
-    hz = jnp.transpose(hidden_pair[:, :, :RZ], (1, 0, 2, 3)).reshape(16 * RZ, 2 * length)
+    hz = jnp.transpose(hidden_pair[:, :, :RZ], (1, 0, 2, 3)).reshape(8, 2 * RZ, 2 * length)
     ha = hidden_pair[:, :, RZ:].reshape(16 * (rows - RZ), 2 * length)
     hidden, hz, ha = barrier((hidden, hz, ha))
 
@@ -240,8 +262,7 @@
     query_grad, kv_grad = attention_backward(kv_pre, queries, upstream, pos, weight)
     pair = jnp.concatenate([kv_grad, shift(kv_grad, "c", 2, 1)], axis=0)
 
-    part_z = jnp.dot(hz, pair, preferred_element_type=F32).astype(BF16)
-    sum_z = lax.psum_scatter(part_z, "z", scatter_dimension=0, tiled=True)
+    sum_z = lax.psum_scatter(first_terms(hz, pair), "z", scatter_dimension=0, tiled=True)
 
     place = jnp.stack([x, y])
 
@@ -256,7 +277,7 @@
     a = add_up([pick(a, z // 4, 0), swap(pick(a, 1 - z // 4, 0), "z", 8, 4)]).astype(BF16)
     sent = tuple(swap(pick(a, lax.rem(z, 4) ^ k, 0), "z", 8, k) for k in (1, 2, 3))
 
-    blocks = jnp.stack([sum_z[:, j * HD : (j + 1) * HD] for j in range(8)]).reshape(16, RZ, HD)
+    blocks = sum_z.reshape(16, RZ, HD)
     blocks, a = barrier((blocks, a))
     arrived = lax.all_to_all(blocks, ("x", *Y), 0, 0, tiled=True)
     arrived = barrier((arrived, *sent))

time: 197 us -> 186 us (0.944)
  local copies, waits for them, and re-layouts: 23.2 us -> 14.3 us
  Pallas kernels: 22.9 us -> 28.1 us
  matrix products: 10.3 us -> 6.5 us
    unnamed x25 -> x26, local copies, waits for them, and re-layouts: 14.4 us -> 8.22 us
    pallas_call x0 -> x1, Pallas kernels: none -> 5 us  [first_terms(): pl.pallas_call(first_terms_kernel, grid=(planes,), in_specs=[pl.BlockSpec...]
    dot_general x1 -> x0, matrix products: 3.81 us -> none  [body(): part_z = jnp.dot(hz, pair, preferred_element_type=F32).astype(BF16)]
    ppermute x8, waiting for transfers between devices: 15.3 us -> 18.7 us  [shift(): return lax.ppermute(v, axis, [(i, (i + k) % n) for i in range(n)])]
    ppermute x12, waiting for transfers between devices: 31.1 us -> 28.5 us  [swap(): return lax.ppermute(v, axis, [(i, i ^ bit) for i in range(n)])]
    reduce_scatter x1, waiting for transfers between devices: 2.3 us -> 0.02 us  [body(): lax.psum_scatter(first_terms(hz, pair), 'z', scatter_dimension=0, tiled=T...]
  transfers between devices with their start and end apart: 23 -> 23, of which waited for: 17 -> 16; matrix products, arithmetic and copies ran while one was open for 10% -> 9% of each run, Pallas kernels for 6% -> 7%
where the time goes in v5:
time: 186 us; the launch traced here: 185 us
  waiting for transfers between devices  75.9 us (41%)
  starting transfers between devices  37.9 us (20%)
  Pallas kernels  28.1 us (15%)
  between operations  15.7 us (8%)
  local copies, waits for them, and re-layouts  14.3 us (8%)
  other arithmetic  6.91 us (4%)
  matrix products  6.5 us (3%)
    ppermute x12, waiting for transfers between devices, swap(): return lax.ppermute(v, axis, [(i, i ^ bit) for i in range(n)])  28.5 us
    all_gather x1, waiting for transfers between devices, body(): lax.all_gather(kv_weight, ('yl', 'z', 'c'), axis=0, tiled=True)  28 us
    ppermute x12, starting transfers between devices, swap(): return lax.ppermute(v, axis, [(i, i ^ bit) for i in range(n)])  19.6 us
    ppermute x8, waiting for transfers between devices, shift(): return lax.ppermute(v, axis, [(i, (i + k) % n) for i in range(n)])  18.7 us
    ppermute x8, starting transfers between devices, shift(): return lax.ppermute(v, axis, [(i, (i + k) % n) for i in range(n)])  10.6 us
    pallas_call x1, Pallas kernels, attention_backward(): pl.pallas_call(attention_kernel, grid=(KVH,), in_specs=[pl.BlockSpec((len...  10.4 us
    pallas_call x1, Pallas kernels, hidden_gradient(): pl.pallas_call(hidden_grad_kernel, grid=(8,), in_specs=[pl.BlockSpec((len...  9.77 us
    unnamed x26, local copies, waits for them, and re-layouts  8.22 us
  transfers between devices with their start and end apart: 23, of which 16 were waited for; matrix products, arithmetic and copies ran while one was open for 9% of the time, Pallas kernels for 7%

profile of v5, /device:TPU:2, one launch (start us, length us, event | category | flops | bytes accessed | tf_op | source)
XLA Modules:
  0.0 185.3 jit_solution(4195534633993224737)
XLA Ops:
  13.3 4.4 %copy.21 = bf16[256,5120]{0,1:T(8,128)(2,1)} copy(bf16[256,5120]{1,0:T(8,128)(2,1)} %param.10) | data formatting | bytes 5242880 | tf_op args[0]
  18.4 2.4 %collective-permute-start.2 = (f32[8,128]{1,0:T(8,128)S(1)}, f32[8,128]{1,0:T(8,128)S(1)}, u32[]{:S(2)}, u32[]{:S(2)}) collective-permute-start(f32[8,128]{1,0:T(8,128)S(1)} %broadcast_add_fusion), channel_id=1, source_target_pairs={{0,64},{64,0},{128,192},{192,128},{1,65},{65,1},{129,193},{193,129... | collective-permute-start | bytes 12296 | tf_op jit(solution)/shard_map/ppermute | solution.py:43
  20.7 3.0 %dynamic-slice_bitcast_fusion = (bf16[16,160,256]{2,1,0:T(8,128)(2,1)}, bf16[16,1,160,256]{3,2,1,0:T(8,128)(2,1)S(1)}) fusion(bf16[16,2,160,256]{3,2,1,0:T(8,128)(2,1)} %bitcast.60, s32[]{:T(128)S(6)} %select_n.58, s32[]{:T(128)S(6)} %select_n.57), kind=kLoop, calls=%fused_computation.4 | loop fusion | bytes 5242888 | tf_op jit(solution)/shard_map/jit(dynamic_index_in_dim)/squeeze | solution.py:216
  25.4 4.4 %collective-permute-done.3 = f32[8,128]{1,0:T(8,128)S(1)} collective-permute-done((f32[8,128]{1,0:T(8,128)S(1)}, f32[8,128]{1,0:T(8,128)S(1)}, u32[]{:S(2)}, u32[]{:S(2)}) %collective-permute-start.3) | collective-permute-done | bytes 4128 | tf_op jit(solution)/shard_map/ppermute | solution.py:43
  29.8 3.6 %collective-permute-done.4 = f32[8,128]{1,0:T(8,128)S(1)} collective-permute-done((f32[8,128]{1,0:T(8,128)S(1)}, f32[8,128]{1,0:T(8,128)S(1)}, u32[]{:S(2)}, u32[]{:S(2)}) %collective-permute-start.4) | collective-permute-done | bytes 4128 | tf_op jit(solution)/shard_map/ppermute | solution.py:43
  35.4 3.1 %collective-permute-done.5 = f32[8,128]{1,0:T(8,128)S(1)} collective-permute-done((f32[8,128]{1,0:T(8,128)S(1)}, f32[8,128]{1,0:T(8,128)S(1)}, u32[]{:S(2)}, u32[]{:S(2)}) %collective-permute-start.5) | collective-permute-done | bytes 4128 | tf_op jit(solution)/shard_map/ppermute | solution.py:43
  38.7 3.5 %collective-permute-done.6 = f32[8,128]{1,0:T(8,128)S(1)} collective-permute-done((f32[8,128]{1,0:T(8,128)S(1)}, f32[8,128]{1,0:T(8,128)S(1)}, u32[]{:S(2)}, u32[]{:S(2)}) %collective-permute-start.6) | collective-permute-done | bytes 4128 | tf_op jit(solution)/shard_map/ppermute | solution.py:43
  42.2 1.5 collective-permute-start.7
  43.8 3.0 %collective-permute-done.7 = f32[8,128]{1,0:T(8,128)S(1)} collective-permute-done((f32[8,128]{1,0:T(8,128)S(1)}, f32[8,128]{1,0:T(8,128)S(1)}, u32[]{:S(2)}, u32[]{:S(2)}) %collective-permute-start.7) | collective-permute-done | bytes 4128 | tf_op jit(solution)/shard_map/ppermute | solution.py:43
  46.8 5.4 %collective-permute-start.8 = (f32[8,128]{1,0:T(8,128)S(1)}, f32[8,128]{1,0:T(8,128)S(1)}, u32[]{:S(2)}, u32[]{:S(2)}) collective-permute-start(f32[8,128]{1,0:T(8,128)S(1)} %add.111), channel_id=1, source_target_pairs={{0,8},{2,10},{4,12},{6,14},{8,0},{10,2},{12,4},{14,6},{1,9},{3,11}... | collective-permute-start | bytes 12296 | tf_op jit(solution)/shard_map/ppermute | solution.py:43
  52.6 1.8 collective-permute-done.8
  59.8 28.0 %all-gather.2.cloned.1.call-done.w = bf16[5120,1024]{1,0:T(8,128)(2,1)} async-done(((bf16[160,1024]{1,0:T(8,128)(2,1)}), bf16[5120,1024]{1,0:T(8,128)(2,1)}) %all-gather.2.cloned.1.call-update) | async-done | bytes 10485776 | tf_op jit(solution)/shard_map/all_gather | solution.py:245
  87.9 6.5 %fusion.9.kpre.vpre = f32[256,1024]{1,0:T(8,128)S(1)} fusion(bf16[256,5120]{1,0:T(8,128)(2,1)} %param.10, bf16[5120,1024]{1,0:T(8,128)(2,1)} %all-gather.2.cloned.1.call-done.w), kind=kOutput, calls=%fused_computation.49 | convolution fusion | flops 2684354560 | bytes 14155776 | tf_op jit(solution)/shard_map/dot_general | solution.py:261
  94.4 10.4 %shard_map.137 = (bf16[256,2560]{1,0:T(8,128)(2,1)}, bf16[256,1024]{1,0:T(8,128)(2,1)S(1)}) custom-call(f32[256,1024]{1,0:T(8,128)S(1)} %fusion.9.kpre.vpre, f32[256,1024]{1,0:T(8,128)S(1)} %fusion.9.kpre.vpre, bf16[256,2560]{1,0:T(8,128)(2,1)S(1)} %copy-done.1, bf16[256,2560]{1,0:T(8,128)(2,1)S(1)} %copy-done.2, f32[256,128]{1,0:T(8,128)S(1)} %get-tuple-element.80.cos, ...), custom_call_target="tpu_custom_call" | custom-call | tf_op jit(solution)/shard_map/pallas_call | solution.py:103
  105.0 1.6 collective-permute-done.9
  106.7 5.0 %shard_map.140 = bf16[12288,128]{1,0:T(8,128)(2,1)} custom-call(bf16[8,192,512]{2,1,0:T(8,128)(2,1)S(1)} %bitcast.56, bf16[512,1024]{1,0:T(8,128)(2,1)S(1)} %constant_dynamic-update-slice_fusion.pair), custom_call_target="tpu_custom_call" | custom-call | tf_op jit(solution)/shard_map/pallas_call | solution.py:158
  112.9 1.8 shard_map.138
  114.7 1.9 %collective-permute-start.10 = (bf16[1024,256]{1,0:T(8,128)(2,1)S(1)}, bf16[1024,256]{1,0:T(8,128)(2,1)S(1)}, u32[]{:S(2)}, u32[]{:S(2)}) collective-permute-start(bf16[1024,256]{1,0:T(8,128)(2,1)S(1)} %get-tuple-element.44), channel_id=1, source_target_pairs={{0,64},{64,128},{128,192},{192,0},{1,65},{65,129},{129,193},{193,1... | collective-permute-start | bytes 1572872 | tf_op jit(solution)/shard_map/ppermute | solution.py:39
  117.6 2.0 %collective-permute-start.12 = (bf16[1024,256]{1,0:T(8,128)(2,1)S(1)}, bf16[1024,256]{1,0:T(8,128)(2,1)S(1)}, u32[]{:S(2)}, u32[]{:S(2)}) collective-permute-start(bf16[1024,256]{1,0:T(8,128)(2,1)S(1)} %get-tuple-element.46), channel_id=1, source_target_pairs={{0,192},{64,0},{128,64},{192,128},{1,193},{65,1},{129,65},{193,129... | collective-permute-start | bytes 1572872 | tf_op jit(solution)/shard_map/ppermute | solution.py:39
  119.6 9.8 %shard_map.139 = bf16[256,5120]{1,0:T(8,128)(2,1)} custom-call(bf16[256,1024]{1,0:T(8,128)(2,1)S(1)} %get-tuple-element.47.kv, bf16[5120,1024]{1,0:T(8,128)(2,1)} %all-gather.2.cloned.1.call-done.w), custom_call_target="tpu_custom_call" | custom-call | tf_op jit(solution)/shard_map/pallas_call | solution.py:136
  129.4 10.1 %collective-permute-done.10.refs_1_ = bf16[1024,256]{1,0:T(8,128)(2,1)S(1)} collective-permute-done((bf16[1024,256]{1,0:T(8,128)(2,1)S(1)}, bf16[1024,256]{1,0:T(8,128)(2,1)S(1)}, u32[]{:S(2)}, u32[]{:S(2)}) %collective-permute-start.10) | collective-permute-done | bytes 524320 | tf_op jit(solution)/shard_map/ppermute | solution.py:39
  139.4 2.9 %collective-permute-done.12.refs_3_ = bf16[1024,256]{1,0:T(8,128)(2,1)S(1)} collective-permute-done((bf16[1024,256]{1,0:T(8,128)(2,1)S(1)}, bf16[1024,256]{1,0:T(8,128)(2,1)S(1)}, u32[]{:S(2)}, u32[]{:S(2)}) %collective-permute-start.12) | collective-permute-done | bytes 524320 | tf_op jit(solution)/shard_map/ppermute | solution.py:39
  144.6 2.6 %collective-permute-start.14 = (bf16[512,128]{1,0:T(8,128)(2,1)S(1)}, bf16[512,128]{1,0:T(8,128)(2,1)S(1)}, u32[]{:S(2)}, u32[]{:S(2)}) collective-permute-start(bf16[512,128]{1,0:T(8,128)(2,1)S(1)} %get-tuple-element.56), channel_id=1, source_target_pairs={{0,32},{16,48},{32,0},{48,16},{1,33},{17,49},{33,1},{49,17},{2,34}... | collective-permute-start | bytes 393224 | tf_op jit(solution)/shard_map/ppermute | solution.py:39
  147.2 1.6 collective-permute-start.15
  148.8 2.3 %collective-permute-done.13 = bf16[512,128]{1,0:T(8,128)(2,1)S(1)} collective-permute-done((bf16[512,128]{1,0:T(8,128)(2,1)S(1)}, bf16[512,128]{1,0:T(8,128)(2,1)S(1)}, u32[]{:S(2)}, u32[]{:S(2)}) %collective-permute-start.13) | collective-permute-done | bytes 131104 | tf_op jit(solution)/shard_map/ppermute | solution.py:39
  151.2 1.5 collective-permute-done.14
  153.0 3.4 %collective-permute-start.16 = (bf16[4,64,128]{2,1,0:T(8,128)(2,1)S(1)}, bf16[4,64,128]{2,1,0:T(8,128)(2,1)S(1)}, u32[]{:S(2)}, u32[]{:S(2)}) collective-permute-start(bf16[4,64,128]{2,1,0:T(8,128)(2,1)S(1)} %dynamic-slice_bitcast_fusion.1), channel_id=1, source_target_pairs={{0,8},{2,10},{4,12},{6,14},{8,0},{10,2},{12,4},{14,6},{1,9},{3,11}... | collective-permute-start | bytes 196616 | tf_op jit(solution)/shard_map/ppermute | solution.py:43
  156.4 5.1 %collective-permute-done.16 = bf16[4,64,128]{2,1,0:T(8,128)(2,1)S(1)} collective-permute-done((bf16[4,64,128]{2,1,0:T(8,128)(2,1)S(1)}, bf16[4,64,128]{2,1,0:T(8,128)(2,1)S(1)}, u32[]{:S(2)}, u32[]{:S(2)}) %collective-permute-start.16) | collective-permute-done | bytes 65568 | tf_op jit(solution)/shard_map/ppermute | solution.py:43
  161.5 7.6 %all-to-all-start = ((bf16[16,96,128]{2,1,0:T(8,128)(2,1)}), bf16[16,96,128]{2,1,0:T(8,128)(2,1)S(1)}, u32[]{:S(2)}, u32[]{:S(2)}) async-start(bf16[16,96,128]{2,1,0:T(8,128)(2,1)} %bitcast.65), calls=%async_computation.1 | async-start | bytes 786432 | tf_op jit(solution)/shard_map/all_to_all | solution.py:282
  170.0 2.0 %collective-permute-start.18 = (bf16[64,128]{1,0:T(8,128)(2,1)S(1)}, bf16[64,128]{1,0:T(8,128)(2,1)S(1)}, u32[]{:S(2)}, u32[]{:S(2)}) collective-permute-start(bf16[64,128]{1,0:T(8,128)(2,1)S(1)} %get-tuple-element.75), channel_id=1, source_target_pairs={{0,4},{2,6},{4,0},{6,2},{8,12},{10,14},{12,8},{14,10},{1,5},{3,7},... | collective-permute-start | bytes 49160 | tf_op jit(solution)/shard_map/ppermute | solution.py:43
  172.1 1.6 collective-permute-start.19
  174.7 2.9 %collective-permute-done.19 = bf16[64,128]{1,0:T(8,128)(2,1)S(1)} collective-permute-done((bf16[64,128]{1,0:T(8,128)(2,1)S(1)}, bf16[64,128]{1,0:T(8,128)(2,1)S(1)}, u32[]{:S(2)}, u32[]{:S(2)}) %collective-permute-start.19) | collective-permute-done | bytes 16416 | tf_op jit(solution)/shard_map/ppermute | solution.py:43
  (90 shorter events, 23.0 us)
Async XLA Ops:
  7.2 80.7 %all-gather.2.cloned.1.call-start = ((), (), s32[]{:S(2)}) async-start(), calls=%async_computation.2 | async-start | bytes 10813440 | tf_op jit(solution)/shard_map/all_gather | solution.py:245
  7.9 153.6 %reduce-scatter.2.cloned.1.call-start = ((), (), s32[]{:S(2)}) async-start(), calls=%async_computation.3 | async-start | bytes 3538944 | tf_op jit(solution)/shard_map/reduce_scatter | solution.py:265
  13.2 4.5 %collective-permute-start.1 = (f32[8,128]{1,0:T(8,128)S(1)}, f32[8,128]{1,0:T(8,128)S(1)}, u32[]{:S(2)}, u32[]{:S(2)}) collective-permute-start(f32[8,128]{1,0:T(8,128)S(1)} %broadcast_in_dim.57), channel_id=1, source_target_pairs={{0,1},{1,0},{2,3},{3,2},{4,5},{5,4},{6,7},{7,6},{8,9},{9,8},{10,11... | collective-permute-start | bytes 12296 | tf_op jit(solution)/shard_map/ppermute | solution.py:43
  18.4 5.5 %collective-permute-start.2 = (f32[8,128]{1,0:T(8,128)S(1)}, f32[8,128]{1,0:T(8,128)S(1)}, u32[]{:S(2)}, u32[]{:S(2)}) collective-permute-start(f32[8,128]{1,0:T(8,128)S(1)} %broadcast_add_fusion), channel_id=1, source_target_pairs={{0,64},{64,0},{128,192},{192,128},{1,65},{65,1},{129,193},{193,129... | collective-permute-start | bytes 12296 | tf_op jit(solution)/shard_map/ppermute | solution.py:43
  20.7 31.5 %copy-start.10 = (s32[1,256]{1,0:T(1,128)S(1)}, s32[1,256]{1,0:T(1,128)}, u32[]{:S(2)}) copy-start(s32[1,256]{1,0:T(1,128)} %param.13) | copy-start | bytes 3076
  20.7 31.5 %copy-start.11 = (f32[1,4]{1,0:T(1,128)S(1)}, f32[1,4]{1,0:T(1,128)}, u32[]{:S(2)}) copy-start(f32[1,4]{1,0:T(1,128)} %param.15) | copy-start | bytes 52
  23.7 32.1 %copy-start.3 = (bf16[16,1,160,256]{3,2,1,0:T(8,128)(2,1)}, bf16[16,1,160,256]{3,2,1,0:T(8,128)(2,1)S(1)}, u32[]{:S(2)}) copy-start(bf16[16,1,160,256]{3,2,1,0:T(8,128)(2,1)S(1)} %get-tuple-element.73) | copy-start | bytes 3932164
  23.7 32.1 %collective-permute-start = (bf16[16,160,256]{2,1,0:T(8,128)(2,1)}, bf16[16,160,256]{2,1,0:T(8,128)(2,1)S(1)}, u32[]{:S(2)}, u32[]{:S(2)}) collective-permute-start(bf16[16,160,256]{2,1,0:T(8,128)(2,1)} %get-tuple-element.72), channel_id=1, source_target_pairs={{0,1},{1,0},{2,3},{3,2},{4,5},{5,4},{6,7},{7,6},{8,9},{9,8},{10,11... | collective-permute-start | bytes 3932168 | tf_op jit(solution)/shard_map/ppermute | solution.py:39
  24.6 5.2 %collective-permute-start.3 = (f32[8,128]{1,0:T(8,128)S(1)}, f32[8,128]{1,0:T(8,128)S(1)}, u32[]{:S(2)}, u32[]{:S(2)}) collective-permute-start(f32[8,128]{1,0:T(8,128)S(1)} %fusion.12), channel_id=1, source_target_pairs={{0,128},{64,192},{128,0},{192,64},{1,129},{65,193},{129,1},{193,65... | collective-permute-start | bytes 12296 | tf_op jit(solution)/shard_map/ppermute | solution.py:43
  29.8 3.6 %collective-permute-start.4 = (f32[8,128]{1,0:T(8,128)S(1)}, f32[8,128]{1,0:T(8,128)S(1)}, u32[]{:S(2)}, u32[]{:S(2)}) collective-permute-start(f32[8,128]{1,0:T(8,128)S(1)} %add.107), channel_id=1, source_target_pairs={{0,16},{16,0},{1,17},{17,1},{2,18},{18,2},{3,19},{19,3},{4,20},{20... | collective-permute-start | bytes 12296 | tf_op jit(solution)/shard_map/ppermute | solution.py:43
  33.4 5.1 %collective-permute-start.5 = (f32[8,128]{1,0:T(8,128)S(1)}, f32[8,128]{1,0:T(8,128)S(1)}, u32[]{:S(2)}, u32[]{:S(2)}) collective-permute-start(f32[8,128]{1,0:T(8,128)S(1)} %add.108), channel_id=1, source_target_pairs={{0,32},{32,0},{1,33},{33,1},{2,34},{34,2},{3,35},{35,3},{4,36},{36... | collective-permute-start | bytes 12296 | tf_op jit(solution)/shard_map/ppermute | solution.py:43
  38.6 3.6 %collective-permute-start.6 = (f32[8,128]{1,0:T(8,128)S(1)}, f32[8,128]{1,0:T(8,128)S(1)}, u32[]{:S(2)}, u32[]{:S(2)}) collective-permute-start(f32[8,128]{1,0:T(8,128)S(1)} %add.109), channel_id=1, source_target_pairs={{0,2},{2,0},{4,6},{6,4},{8,10},{10,8},{12,14},{14,12},{1,3},{3,1},... | collective-permute-start | bytes 12296 | tf_op jit(solution)/shard_map/ppermute | solution.py:43
  42.2 4.6 %collective-permute-start.7 = (f32[8,128]{1,0:T(8,128)S(1)}, f32[8,128]{1,0:T(8,128)S(1)}, u32[]{:S(2)}, u32[]{:S(2)}) collective-permute-start(f32[8,128]{1,0:T(8,128)S(1)} %add.110), channel_id=1, source_target_pairs={{0,4},{2,6},{4,0},{6,2},{8,12},{10,14},{12,8},{14,10},{1,5},{3,7},... | collective-permute-start | bytes 12296 | tf_op jit(solution)/shard_map/ppermute | solution.py:43
  46.8 7.6 %collective-permute-start.8 = (f32[8,128]{1,0:T(8,128)S(1)}, f32[8,128]{1,0:T(8,128)S(1)}, u32[]{:S(2)}, u32[]{:S(2)}) collective-permute-start(f32[8,128]{1,0:T(8,128)S(1)} %add.111), channel_id=1, source_target_pairs={{0,8},{2,10},{4,12},{6,14},{8,0},{10,2},{12,4},{14,6},{1,9},{3,11}... | collective-permute-start | bytes 12296 | tf_op jit(solution)/shard_map/ppermute | solution.py:43
  57.0 1.7 copy-start.6
  87.9 6.5 %copy-start.1 = (bf16[256,2560]{1,0:T(8,128)(2,1)S(1)}, bf16[256,2560]{1,0:T(8,128)(2,1)}, u32[]{:S(2)}) copy-start(bf16[256,2560]{1,0:T(8,128)(2,1)} %q.1) | copy-start | bytes 3932164
  87.9 6.5 %copy-start.2 = (bf16[256,2560]{1,0:T(8,128)(2,1)S(1)}, bf16[256,2560]{1,0:T(8,128)(2,1)}, u32[]{:S(2)}) copy-start(bf16[256,2560]{1,0:T(8,128)(2,1)} %up.1) | copy-start | bytes 3932164
  104.7 1.9 %collective-permute-start.9 = (bf16[256,1024]{1,0:T(8,128)(2,1)S(1)}, bf16[256,1024]{1,0:T(8,128)(2,1)S(1)}, u32[]{:S(2)}, u32[]{:S(2)}) collective-permute-start(bf16[256,1024]{1,0:T(8,128)(2,1)S(1)} %get-tuple-element.47.kv), channel_id=1, source_target_pairs={{0,1},{1,0},{2,3},{3,2},{4,5},{5,4},{6,7},{7,6},{8,9},{9,8},{10,11... | collective-permute-start | bytes 1572872 | tf_op jit(solution)/shard_map/ppermute | solution.py:39
  114.7 24.7 %collective-permute-start.10 = (bf16[1024,256]{1,0:T(8,128)(2,1)S(1)}, bf16[1024,256]{1,0:T(8,128)(2,1)S(1)}, u32[]{:S(2)}, u32[]{:S(2)}) collective-permute-start(bf16[1024,256]{1,0:T(8,128)(2,1)S(1)} %get-tuple-element.44), channel_id=1, source_target_pairs={{0,64},{64,128},{128,192},{192,0},{1,65},{65,129},{129,193},{193,1... | collective-permute-start | bytes 1572872 | tf_op jit(solution)/shard_map/ppermute | solution.py:39
  116.6 22.9 %collective-permute-start.11 = (bf16[1024,256]{1,0:T(8,128)(2,1)S(1)}, bf16[1024,256]{1,0:T(8,128)(2,1)S(1)}, u32[]{:S(2)}, u32[]{:S(2)}) collective-permute-start(bf16[1024,256]{1,0:T(8,128)(2,1)S(1)} %get-tuple-element.45), channel_id=1, source_target_pairs={{0,128},{64,192},{128,0},{192,64},{1,129},{65,193},{129,1},{193,65... | collective-permute-start | bytes 1572872 | tf_op jit(solution)/shard_map/ppermute | solution.py:39
  117.6 24.7 %collective-permute-start.12 = (bf16[1024,256]{1,0:T(8,128)(2,1)S(1)}, bf16[1024,256]{1,0:T(8,128)(2,1)S(1)}, u32[]{:S(2)}, u32[]{:S(2)}) collective-permute-start(bf16[1024,256]{1,0:T(8,128)(2,1)S(1)} %get-tuple-element.46), channel_id=1, source_target_pairs={{0,192},{64,0},{128,64},{192,128},{1,193},{65,1},{129,65},{193,129... | collective-permute-start | bytes 1572872 | tf_op jit(solution)/shard_map/ppermute | solution.py:39
  129.4 48.3 %copy-start.7 = (f32[160,128]{1,0:T(8,128)S(1)}, f32[160,128]{1,0:T(8,128)}, u32[]{:S(2)}) copy-start(f32[160,128]{1,0:T(8,128)} %param.17) | copy-start | bytes 245764
  129.4 48.3 %copy-start.8 = (f32[160,128]{1,0:T(8,128)S(1)}, f32[160,128]{1,0:T(8,128)}, u32[]{:S(2)}) copy-start(f32[160,128]{1,0:T(8,128)} %param.18) | copy-start | bytes 245764
  129.4 48.3 %copy-start.9 = (f32[160,128]{1,0:T(8,128)S(1)}, f32[160,128]{1,0:T(8,128)}, u32[]{:S(2)}) copy-start(f32[160,128]{1,0:T(8,128)} %param.19) | copy-start | bytes 245764
  143.5 7.7 %collective-permute-start.13 = (bf16[512,128]{1,0:T(8,128)(2,1)S(1)}, bf16[512,128]{1,0:T(8,128)(2,1)S(1)}, u32[]{:S(2)}, u32[]{:S(2)}) collective-permute-start(bf16[512,128]{1,0:T(8,128)(2,1)S(1)} %get-tuple-element.55), channel_id=1, source_target_pairs={{0,16},{16,32},{32,48},{48,0},{1,17},{17,33},{33,49},{49,1},{2,18}... | collective-permute-start | bytes 393224 | tf_op jit(solution)/shard_map/ppermute | solution.py:39
  144.6 8.1 %collective-permute-start.14 = (bf16[512,128]{1,0:T(8,128)(2,1)S(1)}, bf16[512,128]{1,0:T(8,128)(2,1)S(1)}, u32[]{:S(2)}, u32[]{:S(2)}) collective-permute-start(bf16[512,128]{1,0:T(8,128)(2,1)S(1)} %get-tuple-element.56), channel_id=1, source_target_pairs={{0,32},{16,48},{32,0},{48,16},{1,33},{17,49},{33,1},{49,17},{2,34}... | collective-permute-start | bytes 393224 | tf_op jit(solution)/shard_map/ppermute | solution.py:39
  147.2 5.7 %collective-permute-start.15 = (bf16[512,128]{1,0:T(8,128)(2,1)S(1)}, bf16[512,128]{1,0:T(8,128)(2,1)S(1)}, u32[]{:S(2)}, u32[]{:S(2)}) collective-permute-start(bf16[512,128]{1,0:T(8,128)(2,1)S(1)} %get-tuple-element.57), channel_id=1, source_target_pairs={{0,48},{16,0},{32,16},{48,32},{1,49},{17,1},{33,17},{49,33},{2,50}... | collective-permute-start | bytes 393224 | tf_op jit(solution)/shard_map/ppermute | solution.py:39
  153.0 8.5 %collective-permute-start.16 = (bf16[4,64,128]{2,1,0:T(8,128)(2,1)S(1)}, bf16[4,64,128]{2,1,0:T(8,128)(2,1)S(1)}, u32[]{:S(2)}, u32[]{:S(2)}) collective-permute-start(bf16[4,64,128]{2,1,0:T(8,128)(2,1)S(1)} %dynamic-slice_bitcast_fusion.1), channel_id=1, source_target_pairs={{0,8},{2,10},{4,12},{6,14},{8,0},{10,2},{12,4},{14,6},{1,9},{3,11}... | collective-permute-start | bytes 196616 | tf_op jit(solution)/shard_map/ppermute | solution.py:43
  161.5 16.0 %all-to-all-start = ((bf16[16,96,128]{2,1,0:T(8,128)(2,1)}), bf16[16,96,128]{2,1,0:T(8,128)(2,1)S(1)}, u32[]{:S(2)}, u32[]{:S(2)}) async-start(bf16[16,96,128]{2,1,0:T(8,128)(2,1)} %bitcast.65), calls=%async_computation.1 | async-start | bytes 786432 | tf_op jit(solution)/shard_map/all_to_all | solution.py:282
  169.1 4.5 %collective-permute-start.17 = (bf16[64,128]{1,0:T(8,128)(2,1)S(1)}, bf16[64,128]{1,0:T(8,128)(2,1)S(1)}, u32[]{:S(2)}, u32[]{:S(2)}) collective-permute-start(bf16[64,128]{1,0:T(8,128)(2,1)S(1)} %get-tuple-element.76), channel_id=1, source_target_pairs={{0,2},{2,0},{4,6},{6,4},{8,10},{10,8},{12,14},{14,12},{1,3},{3,1},... | collective-permute-start | bytes 49160 | tf_op jit(solution)/shard_map/ppermute | solution.py:43
  170.0 4.6 %collective-permute-start.18 = (bf16[64,128]{1,0:T(8,128)(2,1)S(1)}, bf16[64,128]{1,0:T(8,128)(2,1)S(1)}, u32[]{:S(2)}, u32[]{:S(2)}) collective-permute-start(bf16[64,128]{1,0:T(8,128)(2,1)S(1)} %get-tuple-element.75), channel_id=1, source_target_pairs={{0,4},{2,6},{4,0},{6,2},{8,12},{10,14},{12,8},{14,10},{1,5},{3,7},... | collective-permute-start | bytes 49160 | tf_op jit(solution)/shard_map/ppermute | solution.py:43
  172.1 5.5 %collective-permute-start.19 = (bf16[64,128]{1,0:T(8,128)(2,1)S(1)}, bf16[64,128]{1,0:T(8,128)(2,1)S(1)}, u32[]{:S(2)}, u32[]{:S(2)}) collective-permute-start(bf16[64,128]{1,0:T(8,128)(2,1)S(1)} %get-tuple-element.74), channel_id=1, source_target_pairs={{0,6},{2,4},{4,2},{6,0},{8,14},{10,12},{12,10},{14,8},{1,7},{3,5},... | collective-permute-start | bytes 49160 | tf_op jit(solution)/shard_map/ppermute | solution.py:43
  (3 other events, 3.6 us)
Sparse Core Ops, SparseCore 0:
  9.9 77.9 all-gather.1
  111.8 45.7 reduce-scatter.1

commit v6 on v5

--- a/solution.py
+++ b/solution.py
@@ -147,22 +147,25 @@
 
 
 def first_terms_kernel(h, pair, out):
-    term = jnp.dot(h[0], pair[...], preferred_element_type=F32).astype(BF16)
-    rows = h.shape[1]
-    for j in range(8):
-        out[j * rows : (j + 1) * rows, :] = term[:, j * HD : (j + 1) * HD]
+    planes, rows, depth = h.shape
+    block = h[...].reshape(planes * rows, depth)
+    term = jnp.dot(block, pair[...], preferred_element_type=F32).astype(BF16)
+    for p in range(planes):
+        for j in range(8):
+            at = (8 * p + j) * rows
+            out[at : at + rows, :] = term[p * rows : (p + 1) * rows, j * HD : (j + 1) * HD]
 
 
 def first_terms(hz, pair):
     planes, rows, depth = hz.shape
     return pl.pallas_call(
         first_terms_kernel,
-        grid=(planes,),
+        grid=(planes // 2,),
         in_specs=[
-            pl.BlockSpec((1, rows, depth), lambda i: (i, 0, 0)),
+            pl.BlockSpec((2, rows, depth), lambda i: (i, 0, 0)),
             pl.BlockSpec(pair.shape, lambda i: (0, 0)),
         ],
-        out_specs=pl.BlockSpec((8 * rows, HD), lambda i: (i, 0)),
+        out_specs=pl.BlockSpec((16 * rows, HD), lambda i: (i, 0)),
         out_shape=jax.ShapeDtypeStruct((planes * 8 * rows, HD), BF16),
         compiler_params=pltpu.CompilerParams(vmem_limit_bytes=24 * 2**20),
     )(hz, pair)
@@ -274,13 +277,12 @@
     out = turn(place, (out[0], *arrived[:3]))
     arrived = barrier(tuple(shift(out[k], Y, 4, k) for k in (1, 2, 3)))
     a = add_up([out[0], *arrived]).astype(BF16).reshape(2, 4, rows - RZ, HD)
-    a = add_up([pick(a, z // 4, 0), swap(pick(a, 1 - z // 4, 0), "z", 8, 4)]).astype(BF16)
+    blocks = lax.all_to_all(sum_z.reshape(16, RZ, HD), ("x", *Y), 0, 0, tiled=True)
+    theirs = swap(pick(a, 1 - z // 4, 0), "z", 8, 4)
+    theirs, a, _ = barrier((theirs, a, sum_z))
+    a = add_up([pick(a, z // 4, 0), theirs]).astype(BF16)
     sent = tuple(swap(pick(a, lax.rem(z, 4) ^ k, 0), "z", 8, k) for k in (1, 2, 3))
-
-    blocks = sum_z.reshape(16, RZ, HD)
-    blocks, a = barrier((blocks, a))
-    arrived = lax.all_to_all(blocks, ("x", *Y), 0, 0, tiled=True)
-    arrived = barrier((arrived, *sent))
+    arrived = barrier((blocks, *sent))
     summed = jnp.concatenate(
         [
             jnp.sum(arrived[0].astype(F32), axis=0),

time: 186 us -> 182 us (0.978)
  waiting for transfers between devices: 75.9 us -> 73.7 us
    ppermute x12, waiting for transfers between devices: 28.5 us -> 25 us  [swap(): return lax.ppermute(v, axis, [(i, i ^ bit) for i in range(n)])]
where the time goes in v6:
time: 182 us
  waiting for transfers between devices  73.7 us (40%)
  starting transfers between devices  37.9 us (21%)
  Pallas kernels  26.6 us (15%)
  between operations  15.7 us (9%)
  local copies, waits for them, and re-layouts  14.3 us (8%)
  other arithmetic  6.91 us (4%)
  matrix products  6.5 us (4%)
    all_gather x1, waiting for transfers between devices, body(): lax.all_gather(kv_weight, ('yl', 'z', 'c'), axis=0, tiled=True)  28 us
    ppermute x12, waiting for transfers between devices, swap(): return lax.ppermute(v, axis, [(i, i ^ bit) for i in range(n)])  25 us
    ppermute x12, starting transfers between devices, swap(): return lax.ppermute(v, axis, [(i, i ^ bit) for i in range(n)])  19.6 us
    ppermute x8, waiting for transfers between devices, shift(): return lax.ppermute(v, axis, [(i, (i + k) % n) for i in range(n)])  18.7 us
    ppermute x8, starting transfers between devices, shift(): return lax.ppermute(v, axis, [(i, (i + k) % n) for i in range(n)])  10.6 us
    pallas_call x1, Pallas kernels, attention_backward(): pl.pallas_call(attention_kernel, grid=(KVH,), in_specs=[pl.BlockSpec((len...  10.4 us
    pallas_call x1, Pallas kernels, hidden_gradient(): pl.pallas_call(hidden_grad_kernel, grid=(8,), in_specs=[pl.BlockSpec((len...  9.76 us
    unnamed x26, local copies, waits for them, and re-layouts  8.22 us
  transfers between devices with their start and end apart: 23, of which 16 were waited for; matrix products, arithmetic and copies ran while one was open for 9% of the time, Pallas kernels for 7%

profile of v6, /device:TPU:2, one launch (start us, length us, event | category | flops | bytes accessed | tf_op | source)
XLA Modules:
  0.0 181.6 jit_solution(6307834256320051103)
XLA Ops:
  13.3 4.4 %copy.21 = bf16[256,5120]{0,1:T(8,128)(2,1)} copy(bf16[256,5120]{1,0:T(8,128)(2,1)} %param.10) | data formatting | bytes 5242880 | tf_op args[0]
  18.4 2.4 %collective-permute-start.2 = (f32[8,128]{1,0:T(8,128)S(1)}, f32[8,128]{1,0:T(8,128)S(1)}, u32[]{:S(2)}, u32[]{:S(2)}) collective-permute-start(f32[8,128]{1,0:T(8,128)S(1)} %broadcast_add_fusion), channel_id=1, source_target_pairs={{0,64},{64,0},{128,192},{192,128},{1,65},{65,1},{129,193},{193,129... | collective-permute-start | bytes 12296 | tf_op jit(solution)/shard_map/ppermute | solution.py:43
  20.7 3.0 %dynamic-slice_bitcast_fusion = (bf16[16,160,256]{2,1,0:T(8,128)(2,1)}, bf16[16,1,160,256]{3,2,1,0:T(8,128)(2,1)S(1)}) fusion(bf16[16,2,160,256]{3,2,1,0:T(8,128)(2,1)} %bitcast.60, s32[]{:T(128)S(6)} %select_n.58, s32[]{:T(128)S(6)} %select_n.57), kind=kLoop, calls=%fused_computation.4 | loop fusion | bytes 5242888 | tf_op jit(solution)/shard_map/jit(dynamic_index_in_dim)/squeeze | solution.py:219
  25.4 4.4 %collective-permute-done.3 = f32[8,128]{1,0:T(8,128)S(1)} collective-permute-done((f32[8,128]{1,0:T(8,128)S(1)}, f32[8,128]{1,0:T(8,128)S(1)}, u32[]{:S(2)}, u32[]{:S(2)}) %collective-permute-start.3) | collective-permute-done | bytes 4128 | tf_op jit(solution)/shard_map/ppermute | solution.py:43
  29.8 3.6 %collective-permute-done.4 = f32[8,128]{1,0:T(8,128)S(1)} collective-permute-done((f32[8,128]{1,0:T(8,128)S(1)}, f32[8,128]{1,0:T(8,128)S(1)}, u32[]{:S(2)}, u32[]{:S(2)}) %collective-permute-start.4) | collective-permute-done | bytes 4128 | tf_op jit(solution)/shard_map/ppermute | solution.py:43
  33.4 1.5 collective-permute-start.5
  35.4 3.1 %collective-permute-done.5 = f32[8,128]{1,0:T(8,128)S(1)} collective-permute-done((f32[8,128]{1,0:T(8,128)S(1)}, f32[8,128]{1,0:T(8,128)S(1)}, u32[]{:S(2)}, u32[]{:S(2)}) %collective-permute-start.5) | collective-permute-done | bytes 4128 | tf_op jit(solution)/shard_map/ppermute | solution.py:43
  38.7 3.5 %collective-permute-done.6 = f32[8,128]{1,0:T(8,128)S(1)} collective-permute-done((f32[8,128]{1,0:T(8,128)S(1)}, f32[8,128]{1,0:T(8,128)S(1)}, u32[]{:S(2)}, u32[]{:S(2)}) %collective-permute-start.6) | collective-permute-done | bytes 4128 | tf_op jit(solution)/shard_map/ppermute | solution.py:43
  42.2 1.5 collective-permute-start.7
  43.8 3.0 %collective-permute-done.7 = f32[8,128]{1,0:T(8,128)S(1)} collective-permute-done((f32[8,128]{1,0:T(8,128)S(1)}, f32[8,128]{1,0:T(8,128)S(1)}, u32[]{:S(2)}, u32[]{:S(2)}) %collective-permute-start.7) | collective-permute-done | bytes 4128 | tf_op jit(solution)/shard_map/ppermute | solution.py:43
  46.8 5.4 %collective-permute-start.8 = (f32[8,128]{1,0:T(8,128)S(1)}, f32[8,128]{1,0:T(8,128)S(1)}, u32[]{:S(2)}, u32[]{:S(2)}) collective-permute-start(f32[8,128]{1,0:T(8,128)S(1)} %add.111), channel_id=1, source_target_pairs={{0,8},{2,10},{4,12},{6,14},{8,0},{10,2},{12,4},{14,6},{1,9},{3,11}... | collective-permute-start | bytes 12296 | tf_op jit(solution)/shard_map/ppermute | solution.py:43
  52.6 1.8 %collective-permute-done.8 = f32[8,128]{1,0:T(8,128)S(1)} collective-permute-done((f32[8,128]{1,0:T(8,128)S(1)}, f32[8,128]{1,0:T(8,128)S(1)}, u32[]{:S(2)}, u32[]{:S(2)}) %collective-permute-start.8) | collective-permute-done | bytes 4128 | tf_op jit(solution)/shard_map/ppermute | solution.py:43
  59.8 28.0 %all-gather.2.cloned.1.call-done.w = bf16[5120,1024]{1,0:T(8,128)(2,1)} async-done(((bf16[160,1024]{1,0:T(8,128)(2,1)}), bf16[5120,1024]{1,0:T(8,128)(2,1)}) %all-gather.2.cloned.1.call-update) | async-done | bytes 10485776 | tf_op jit(solution)/shard_map/all_gather | solution.py:248
  87.9 6.5 %fusion.9.kpre.vpre = f32[256,1024]{1,0:T(8,128)S(1)} fusion(bf16[256,5120]{1,0:T(8,128)(2,1)} %param.10, bf16[5120,1024]{1,0:T(8,128)(2,1)} %all-gather.2.cloned.1.call-done.w), kind=kOutput, calls=%fused_computation.49 | convolution fusion | flops 2684354560 | bytes 14155776 | tf_op jit(solution)/shard_map/dot_general | solution.py:264
  94.4 10.4 %shard_map.137 = (bf16[256,2560]{1,0:T(8,128)(2,1)}, bf16[256,1024]{1,0:T(8,128)(2,1)S(1)}) custom-call(f32[256,1024]{1,0:T(8,128)S(1)} %fusion.9.kpre.vpre, f32[256,1024]{1,0:T(8,128)S(1)} %fusion.9.kpre.vpre, bf16[256,2560]{1,0:T(8,128)(2,1)S(1)} %copy-done.1, bf16[256,2560]{1,0:T(8,128)(2,1)S(1)} %copy-done.2, f32[256,128]{1,0:T(8,128)S(1)} %get-tuple-element.80.cos, ...), custom_call_target="tpu_custom_call" | custom-call | tf_op jit(solution)/shard_map/pallas_call | solution.py:103
  105.0 1.6 collective-permute-done.9
  106.7 3.6 %shard_map.140 = bf16[12288,128]{1,0:T(8,128)(2,1)} custom-call(bf16[8,192,512]{2,1,0:T(8,128)(2,1)S(1)} %bitcast.56, bf16[512,1024]{1,0:T(8,128)(2,1)S(1)} %constant_dynamic-update-slice_fusion.pair), custom_call_target="tpu_custom_call" | custom-call | tf_op jit(solution)/shard_map/pallas_call | solution.py:161
  111.5 1.8 shard_map.138
  113.3 1.9 %collective-permute-start.10 = (bf16[1024,256]{1,0:T(8,128)(2,1)S(1)}, bf16[1024,256]{1,0:T(8,128)(2,1)S(1)}, u32[]{:S(2)}, u32[]{:S(2)}) collective-permute-start(bf16[1024,256]{1,0:T(8,128)(2,1)S(1)} %get-tuple-element.44), channel_id=1, source_target_pairs={{0,64},{64,128},{128,192},{192,0},{1,65},{65,129},{129,193},{193,1... | collective-permute-start | bytes 1572872 | tf_op jit(solution)/shard_map/ppermute | solution.py:39
  116.2 2.0 %collective-permute-start.12 = (bf16[1024,256]{1,0:T(8,128)(2,1)S(1)}, bf16[1024,256]{1,0:T(8,128)(2,1)S(1)}, u32[]{:S(2)}, u32[]{:S(2)}) collective-permute-start(bf16[1024,256]{1,0:T(8,128)(2,1)S(1)} %get-tuple-element.46), channel_id=1, source_target_pairs={{0,192},{64,0},{128,64},{192,128},{1,193},{65,1},{129,65},{193,129... | collective-permute-start | bytes 1572872 | tf_op jit(solution)/shard_map/ppermute | solution.py:39
  118.2 9.8 %shard_map.139 = bf16[256,5120]{1,0:T(8,128)(2,1)} custom-call(bf16[256,1024]{1,0:T(8,128)(2,1)S(1)} %get-tuple-element.47.kv, bf16[5120,1024]{1,0:T(8,128)(2,1)} %all-gather.2.cloned.1.call-done.w), custom_call_target="tpu_custom_call" | custom-call | tf_op jit(solution)/shard_map/pallas_call | solution.py:136
  127.9 10.1 %collective-permute-done.10.refs_1_ = bf16[1024,256]{1,0:T(8,128)(2,1)S(1)} collective-permute-done((bf16[1024,256]{1,0:T(8,128)(2,1)S(1)}, bf16[1024,256]{1,0:T(8,128)(2,1)S(1)}, u32[]{:S(2)}, u32[]{:S(2)}) %collective-permute-start.10) | collective-permute-done | bytes 524320 | tf_op jit(solution)/shard_map/ppermute | solution.py:39
  138.0 2.9 %collective-permute-done.12.refs_3_ = bf16[1024,256]{1,0:T(8,128)(2,1)S(1)} collective-permute-done((bf16[1024,256]{1,0:T(8,128)(2,1)S(1)}, bf16[1024,256]{1,0:T(8,128)(2,1)S(1)}, u32[]{:S(2)}, u32[]{:S(2)}) %collective-permute-start.12) | collective-permute-done | bytes 524320 | tf_op jit(solution)/shard_map/ppermute | solution.py:39
  143.1 2.6 %collective-permute-start.14 = (bf16[512,128]{1,0:T(8,128)(2,1)S(1)}, bf16[512,128]{1,0:T(8,128)(2,1)S(1)}, u32[]{:S(2)}, u32[]{:S(2)}) collective-permute-start(bf16[512,128]{1,0:T(8,128)(2,1)S(1)} %get-tuple-element.56), channel_id=1, source_target_pairs={{0,32},{16,48},{32,0},{48,16},{1,33},{17,49},{33,1},{49,17},{2,34}... | collective-permute-start | bytes 393224 | tf_op jit(solution)/shard_map/ppermute | solution.py:39
  145.8 1.6 collective-permute-start.15
  147.4 2.3 %collective-permute-done.13 = bf16[512,128]{1,0:T(8,128)(2,1)S(1)} collective-permute-done((bf16[512,128]{1,0:T(8,128)(2,1)S(1)}, bf16[512,128]{1,0:T(8,128)(2,1)S(1)}, u32[]{:S(2)}, u32[]{:S(2)}) %collective-permute-start.13) | collective-permute-done | bytes 131104 | tf_op jit(solution)/shard_map/ppermute | solution.py:39
  149.7 1.4 collective-permute-done.14
  151.6 3.4 %collective-permute-start.16 = (bf16[4,64,128]{2,1,0:T(8,128)(2,1)S(1)}, bf16[4,64,128]{2,1,0:T(8,128)(2,1)S(1)}, u32[]{:S(2)}, u32[]{:S(2)}) collective-permute-start(bf16[4,64,128]{2,1,0:T(8,128)(2,1)S(1)} %dynamic-slice_bitcast_fusion.1), channel_id=1, source_target_pairs={{0,8},{2,10},{4,12},{6,14},{8,0},{10,2},{12,4},{14,6},{1,9},{3,11}... | collective-permute-start | bytes 196616 | tf_op jit(solution)/shard_map/ppermute | solution.py:43
  156.3 7.5 %all-to-all-start = ((bf16[16,96,128]{2,1,0:T(8,128)(2,1)}), bf16[16,96,128]{2,1,0:T(8,128)(2,1)S(1)}, u32[]{:S(2)}, u32[]{:S(2)}) async-start(bf16[16,96,128]{2,1,0:T(8,128)(2,1)} %bitcast.65), calls=%async_computation.1 | async-start | bytes 786432 | tf_op jit(solution)/shard_map/all_to_all | solution.py:280
  165.1 3.3 %collective-permute-start.18 = (bf16[64,128]{1,0:T(8,128)(2,1)S(1)}, bf16[64,128]{1,0:T(8,128)(2,1)S(1)}, u32[]{:S(2)}, u32[]{:S(2)}) collective-permute-start(bf16[64,128]{1,0:T(8,128)(2,1)S(1)} %get-tuple-element.75), channel_id=1, source_target_pairs={{0,4},{2,6},{4,0},{6,2},{8,12},{10,14},{12,8},{14,10},{1,5},{3,7},... | collective-permute-start | bytes 49160 | tf_op jit(solution)/shard_map/ppermute | solution.py:43
  168.4 1.9 %collective-permute-done.18 = bf16[64,128]{1,0:T(8,128)(2,1)S(1)} collective-permute-done((bf16[64,128]{1,0:T(8,128)(2,1)S(1)}, bf16[64,128]{1,0:T(8,128)(2,1)S(1)}, u32[]{:S(2)}, u32[]{:S(2)}) %collective-permute-start.18) | collective-permute-done | bytes 16416 | tf_op jit(solution)/shard_map/ppermute | solution.py:43
  170.3 3.6 %collective-permute-done.19 = bf16[64,128]{1,0:T(8,128)(2,1)S(1)} collective-permute-done((bf16[64,128]{1,0:T(8,128)(2,1)S(1)}, bf16[64,128]{1,0:T(8,128)(2,1)S(1)}, u32[]{:S(2)}, u32[]{:S(2)}) %collective-permute-start.19) | collective-permute-done | bytes 16416 | tf_op jit(solution)/shard_map/ppermute | solution.py:43
  (90 shorter events, 22.1 us)
Async XLA Ops:
  7.2 80.7 %all-gather.2.cloned.1.call-start = ((), (), s32[]{:S(2)}) async-start(), calls=%async_computation.2 | async-start | bytes 10813440 | tf_op jit(solution)/shard_map/all_gather | solution.py:248
  7.9 148.4 %reduce-scatter.2.cloned.1.call-start = ((), (), s32[]{:S(2)}) async-start(), calls=%async_computation.3 | async-start | bytes 3538944 | tf_op jit(solution)/shard_map/reduce_scatter | solution.py:268
  13.2 4.5 %collective-permute-start.1 = (f32[8,128]{1,0:T(8,128)S(1)}, f32[8,128]{1,0:T(8,128)S(1)}, u32[]{:S(2)}, u32[]{:S(2)}) collective-permute-start(f32[8,128]{1,0:T(8,128)S(1)} %broadcast_in_dim.57), channel_id=1, source_target_pairs={{0,1},{1,0},{2,3},{3,2},{4,5},{5,4},{6,7},{7,6},{8,9},{9,8},{10,11... | collective-permute-start | bytes 12296 | tf_op jit(solution)/shard_map/ppermute | solution.py:43
  18.4 5.5 %collective-permute-start.2 = (f32[8,128]{1,0:T(8,128)S(1)}, f32[8,128]{1,0:T(8,128)S(1)}, u32[]{:S(2)}, u32[]{:S(2)}) collective-permute-start(f32[8,128]{1,0:T(8,128)S(1)} %broadcast_add_fusion), channel_id=1, source_target_pairs={{0,64},{64,0},{128,192},{192,128},{1,65},{65,1},{129,193},{193,129... | collective-permute-start | bytes 12296 | tf_op jit(solution)/shard_map/ppermute | solution.py:43
  20.7 31.5 %copy-start.10 = (s32[1,256]{1,0:T(1,128)S(1)}, s32[1,256]{1,0:T(1,128)}, u32[]{:S(2)}) copy-start(s32[1,256]{1,0:T(1,128)} %param.13) | copy-start | bytes 3076
  20.7 31.5 %copy-start.11 = (f32[1,4]{1,0:T(1,128)S(1)}, f32[1,4]{1,0:T(1,128)}, u32[]{:S(2)}) copy-start(f32[1,4]{1,0:T(1,128)} %param.15) | copy-start | bytes 52
  23.7 32.1 %copy-start.3 = (bf16[16,1,160,256]{3,2,1,0:T(8,128)(2,1)}, bf16[16,1,160,256]{3,2,1,0:T(8,128)(2,1)S(1)}, u32[]{:S(2)}) copy-start(bf16[16,1,160,256]{3,2,1,0:T(8,128)(2,1)S(1)} %get-tuple-element.73) | copy-start | bytes 3932164
  23.7 32.1 %collective-permute-start = (bf16[16,160,256]{2,1,0:T(8,128)(2,1)}, bf16[16,160,256]{2,1,0:T(8,128)(2,1)S(1)}, u32[]{:S(2)}, u32[]{:S(2)}) collective-permute-start(bf16[16,160,256]{2,1,0:T(8,128)(2,1)} %get-tuple-element.72), channel_id=1, source_target_pairs={{0,1},{1,0},{2,3},{3,2},{4,5},{5,4},{6,7},{7,6},{8,9},{9,8},{10,11... | collective-permute-start | bytes 3932168 | tf_op jit(solution)/shard_map/ppermute | solution.py:39
  24.6 5.2 %collective-permute-start.3 = (f32[8,128]{1,0:T(8,128)S(1)}, f32[8,128]{1,0:T(8,128)S(1)}, u32[]{:S(2)}, u32[]{:S(2)}) collective-permute-start(f32[8,128]{1,0:T(8,128)S(1)} %fusion.12), channel_id=1, source_target_pairs={{0,128},{64,192},{128,0},{192,64},{1,129},{65,193},{129,1},{193,65... | collective-permute-start | bytes 12296 | tf_op jit(solution)/shard_map/ppermute | solution.py:43
  29.8 3.6 %collective-permute-start.4 = (f32[8,128]{1,0:T(8,128)S(1)}, f32[8,128]{1,0:T(8,128)S(1)}, u32[]{:S(2)}, u32[]{:S(2)}) collective-permute-start(f32[8,128]{1,0:T(8,128)S(1)} %add.107), channel_id=1, source_target_pairs={{0,16},{16,0},{1,17},{17,1},{2,18},{18,2},{3,19},{19,3},{4,20},{20... | collective-permute-start | bytes 12296 | tf_op jit(solution)/shard_map/ppermute | solution.py:43
  33.4 5.1 %collective-permute-start.5 = (f32[8,128]{1,0:T(8,128)S(1)}, f32[8,128]{1,0:T(8,128)S(1)}, u32[]{:S(2)}, u32[]{:S(2)}) collective-permute-start(f32[8,128]{1,0:T(8,128)S(1)} %add.108), channel_id=1, source_target_pairs={{0,32},{32,0},{1,33},{33,1},{2,34},{34,2},{3,35},{35,3},{4,36},{36... | collective-permute-start | bytes 12296 | tf_op jit(solution)/shard_map/ppermute | solution.py:43
  38.6 3.6 %collective-permute-start.6 = (f32[8,128]{1,0:T(8,128)S(1)}, f32[8,128]{1,0:T(8,128)S(1)}, u32[]{:S(2)}, u32[]{:S(2)}) collective-permute-start(f32[8,128]{1,0:T(8,128)S(1)} %add.109), channel_id=1, source_target_pairs={{0,2},{2,0},{4,6},{6,4},{8,10},{10,8},{12,14},{14,12},{1,3},{3,1},... | collective-permute-start | bytes 12296 | tf_op jit(solution)/shard_map/ppermute | solution.py:43
  42.2 4.6 %collective-permute-start.7 = (f32[8,128]{1,0:T(8,128)S(1)}, f32[8,128]{1,0:T(8,128)S(1)}, u32[]{:S(2)}, u32[]{:S(2)}) collective-permute-start(f32[8,128]{1,0:T(8,128)S(1)} %add.110), channel_id=1, source_target_pairs={{0,4},{2,6},{4,0},{6,2},{8,12},{10,14},{12,8},{14,10},{1,5},{3,7},... | collective-permute-start | bytes 12296 | tf_op jit(solution)/shard_map/ppermute | solution.py:43
  46.8 7.6 %collective-permute-start.8 = (f32[8,128]{1,0:T(8,128)S(1)}, f32[8,128]{1,0:T(8,128)S(1)}, u32[]{:S(2)}, u32[]{:S(2)}) collective-permute-start(f32[8,128]{1,0:T(8,128)S(1)} %add.111), channel_id=1, source_target_pairs={{0,8},{2,10},{4,12},{6,14},{8,0},{10,2},{12,4},{14,6},{1,9},{3,11}... | collective-permute-start | bytes 12296 | tf_op jit(solution)/shard_map/ppermute | solution.py:43
  57.0 1.7 copy-start.6
  87.9 6.5 %copy-start.1 = (bf16[256,2560]{1,0:T(8,128)(2,1)S(1)}, bf16[256,2560]{1,0:T(8,128)(2,1)}, u32[]{:S(2)}) copy-start(bf16[256,2560]{1,0:T(8,128)(2,1)} %q.1) | copy-start | bytes 3932164
  87.9 6.5 %copy-start.2 = (bf16[256,2560]{1,0:T(8,128)(2,1)S(1)}, bf16[256,2560]{1,0:T(8,128)(2,1)}, u32[]{:S(2)}) copy-start(bf16[256,2560]{1,0:T(8,128)(2,1)} %up.1) | copy-start | bytes 3932164
  104.7 1.9 %collective-permute-start.9 = (bf16[256,1024]{1,0:T(8,128)(2,1)S(1)}, bf16[256,1024]{1,0:T(8,128)(2,1)S(1)}, u32[]{:S(2)}, u32[]{:S(2)}) collective-permute-start(bf16[256,1024]{1,0:T(8,128)(2,1)S(1)} %get-tuple-element.47.kv), channel_id=1, source_target_pairs={{0,1},{1,0},{2,3},{3,2},{4,5},{5,4},{6,7},{7,6},{8,9},{9,8},{10,11... | collective-permute-start | bytes 1572872 | tf_op jit(solution)/shard_map/ppermute | solution.py:39
  113.3 24.7 %collective-permute-start.10 = (bf16[1024,256]{1,0:T(8,128)(2,1)S(1)}, bf16[1024,256]{1,0:T(8,128)(2,1)S(1)}, u32[]{:S(2)}, u32[]{:S(2)}) collective-permute-start(bf16[1024,256]{1,0:T(8,128)(2,1)S(1)} %get-tuple-element.44), channel_id=1, source_target_pairs={{0,64},{64,128},{128,192},{192,0},{1,65},{65,129},{129,193},{193,1... | collective-permute-start | bytes 1572872 | tf_op jit(solution)/shard_map/ppermute | solution.py:39
  115.2 22.9 %collective-permute-start.11 = (bf16[1024,256]{1,0:T(8,128)(2,1)S(1)}, bf16[1024,256]{1,0:T(8,128)(2,1)S(1)}, u32[]{:S(2)}, u32[]{:S(2)}) collective-permute-start(bf16[1024,256]{1,0:T(8,128)(2,1)S(1)} %get-tuple-element.45), channel_id=1, source_target_pairs={{0,128},{64,192},{128,0},{192,64},{1,129},{65,193},{129,1},{193,65... | collective-permute-start | bytes 1572872 | tf_op jit(solution)/shard_map/ppermute | solution.py:39
  116.2 24.7 %collective-permute-start.12 = (bf16[1024,256]{1,0:T(8,128)(2,1)S(1)}, bf16[1024,256]{1,0:T(8,128)(2,1)S(1)}, u32[]{:S(2)}, u32[]{:S(2)}) collective-permute-start(bf16[1024,256]{1,0:T(8,128)(2,1)S(1)} %get-tuple-element.46), channel_id=1, source_target_pairs={{0,192},{64,0},{128,64},{192,128},{1,193},{65,1},{129,65},{193,129... | collective-permute-start | bytes 1572872 | tf_op jit(solution)/shard_map/ppermute | solution.py:39
  127.9 46.1 %copy-start.7 = (f32[160,128]{1,0:T(8,128)S(1)}, f32[160,128]{1,0:T(8,128)}, u32[]{:S(2)}) copy-start(f32[160,128]{1,0:T(8,128)} %param.17) | copy-start | bytes 245764
  127.9 46.1 %copy-start.8 = (f32[160,128]{1,0:T(8,128)S(1)}, f32[160,128]{1,0:T(8,128)}, u32[]{:S(2)}) copy-start(f32[160,128]{1,0:T(8,128)} %param.18) | copy-start | bytes 245764
  127.9 46.1 %copy-start.9 = (f32[160,128]{1,0:T(8,128)S(1)}, f32[160,128]{1,0:T(8,128)}, u32[]{:S(2)}) copy-start(f32[160,128]{1,0:T(8,128)} %param.19) | copy-start | bytes 245764
  142.1 7.7 %collective-permute-start.13 = (bf16[512,128]{1,0:T(8,128)(2,1)S(1)}, bf16[512,128]{1,0:T(8,128)(2,1)S(1)}, u32[]{:S(2)}, u32[]{:S(2)}) collective-permute-start(bf16[512,128]{1,0:T(8,128)(2,1)S(1)} %get-tuple-element.55), channel_id=1, source_target_pairs={{0,16},{16,32},{32,48},{48,0},{1,17},{17,33},{33,49},{49,1},{2,18}... | collective-permute-start | bytes 393224 | tf_op jit(solution)/shard_map/ppermute | solution.py:39
  143.1 8.1 %collective-permute-start.14 = (bf16[512,128]{1,0:T(8,128)(2,1)S(1)}, bf16[512,128]{1,0:T(8,128)(2,1)S(1)}, u32[]{:S(2)}, u32[]{:S(2)}) collective-permute-start(bf16[512,128]{1,0:T(8,128)(2,1)S(1)} %get-tuple-element.56), channel_id=1, source_target_pairs={{0,32},{16,48},{32,0},{48,16},{1,33},{17,49},{33,1},{49,17},{2,34}... | collective-permute-start | bytes 393224 | tf_op jit(solution)/shard_map/ppermute | solution.py:39
  145.8 5.7 %collective-permute-start.15 = (bf16[512,128]{1,0:T(8,128)(2,1)S(1)}, bf16[512,128]{1,0:T(8,128)(2,1)S(1)}, u32[]{:S(2)}, u32[]{:S(2)}) collective-permute-start(bf16[512,128]{1,0:T(8,128)(2,1)S(1)} %get-tuple-element.57), channel_id=1, source_target_pairs={{0,48},{16,0},{32,16},{48,32},{1,49},{17,1},{33,17},{49,33},{2,50}... | collective-permute-start | bytes 393224 | tf_op jit(solution)/shard_map/ppermute | solution.py:39
  151.6 12.3 %collective-permute-start.16 = (bf16[4,64,128]{2,1,0:T(8,128)(2,1)S(1)}, bf16[4,64,128]{2,1,0:T(8,128)(2,1)S(1)}, u32[]{:S(2)}, u32[]{:S(2)}) collective-permute-start(bf16[4,64,128]{2,1,0:T(8,128)(2,1)S(1)} %dynamic-slice_bitcast_fusion.1), channel_id=1, source_target_pairs={{0,8},{2,10},{4,12},{6,14},{8,0},{10,2},{12,4},{14,6},{1,9},{3,11}... | collective-permute-start | bytes 196616 | tf_op jit(solution)/shard_map/ppermute | solution.py:43
  156.3 17.6 %all-to-all-start = ((bf16[16,96,128]{2,1,0:T(8,128)(2,1)}), bf16[16,96,128]{2,1,0:T(8,128)(2,1)S(1)}, u32[]{:S(2)}, u32[]{:S(2)}) async-start(bf16[16,96,128]{2,1,0:T(8,128)(2,1)} %bitcast.65), calls=%async_computation.1 | async-start | bytes 786432 | tf_op jit(solution)/shard_map/all_to_all | solution.py:280
  163.9 4.5 %collective-permute-start.17 = (bf16[64,128]{1,0:T(8,128)(2,1)S(1)}, bf16[64,128]{1,0:T(8,128)(2,1)S(1)}, u32[]{:S(2)}, u32[]{:S(2)}) collective-permute-start(bf16[64,128]{1,0:T(8,128)(2,1)S(1)} %get-tuple-element.76), channel_id=1, source_target_pairs={{0,2},{2,0},{4,6},{6,4},{8,10},{10,8},{12,14},{14,12},{1,3},{3,1},... | collective-permute-start | bytes 49160 | tf_op jit(solution)/shard_map/ppermute | solution.py:43
  165.1 5.2 %collective-permute-start.18 = (bf16[64,128]{1,0:T(8,128)(2,1)S(1)}, bf16[64,128]{1,0:T(8,128)(2,1)S(1)}, u32[]{:S(2)}, u32[]{:S(2)}) collective-permute-start(bf16[64,128]{1,0:T(8,128)(2,1)S(1)} %get-tuple-element.75), channel_id=1, source_target_pairs={{0,4},{2,6},{4,0},{6,2},{8,12},{10,14},{12,8},{14,10},{1,5},{3,7},... | collective-permute-start | bytes 49160 | tf_op jit(solution)/shard_map/ppermute | solution.py:43
  168.4 5.5 %collective-permute-start.19 = (bf16[64,128]{1,0:T(8,128)(2,1)S(1)}, bf16[64,128]{1,0:T(8,128)(2,1)S(1)}, u32[]{:S(2)}, u32[]{:S(2)}) collective-permute-start(bf16[64,128]{1,0:T(8,128)(2,1)S(1)} %get-tuple-element.74), channel_id=1, source_target_pairs={{0,6},{2,4},{4,2},{6,0},{8,14},{10,12},{12,10},{14,8},{1,7},{3,5},... | collective-permute-start | bytes 49160 | tf_op jit(solution)/shard_map/ppermute | solution.py:43
  (3 other events, 3.6 us)
Sparse Core Ops, SparseCore 0:
  9.9 77.9 all-gather.1
  110.4 45.8 reduce-scatter.1

commit v7 on v6

--- a/solution.py
+++ b/solution.py
@@ -62,31 +62,37 @@
 
 def attention_kernel(kpre, vpre, q, up, cos, sin, start, weight, qg, kvg):
     length = kpre.shape[0]
+    half = length // 2
     cosine, sine = cos[...], sin[...]
     kp = kpre[...]
     k = (kp * cosine + pltpu.roll(kp, HD // 2, 1) * sine).astype(BF16)
     v = vpre[...].astype(BF16)
-    key_index = lax.broadcasted_iota(jnp.int32, (length, length), 0)
-    query_index = lax.broadcasted_iota(jnp.int32, (length, length), 1)
-    allowed = (key_index >= start[...]) & (key_index <= query_index)
-    w = weight[...]
-    dk = jnp.zeros((length, HD), F32)
-    dv = jnp.zeros((length, HD), F32)
-    for g in range(GROUP):
-        cols = slice(g * HD, (g + 1) * HD)
-        qh = q[:, cols]
-        do = (up[:, cols].astype(F32) * w).astype(BF16)
-        s = jnp.where(allowed, dot_nt(k, qh) * SCALE, F32(-1e30))
+    dk, dv = [], []
+    for part in range(2):
+        rows, keys = slice(part * half, (part + 1) * half), (part + 1) * half
+        kh, vh = k[:keys], v[:keys]
+        key_index = lax.broadcasted_iota(jnp.int32, (keys, half), 0)
+        query_index = lax.broadcasted_iota(jnp.int32, (keys, half), 1) + part * half
+        allowed = (key_index >= start[:, rows]) & (key_index <= query_index)
+        allowed = jnp.concatenate([allowed.astype(F32)] * GROUP, axis=1) > 0
+        w = weight[rows, :]
+        cols = [slice(g * HD, (g + 1) * HD) for g in range(GROUP)]
+        qh = jnp.concatenate([q[rows, c] for c in cols], axis=0)
+        do = jnp.concatenate([(up[rows, c].astype(F32) * w).astype(BF16) for c in cols], axis=0)
+        s = jnp.where(allowed, dot_nt(kh, qh) * SCALE, F32(-1e30))
         e = jnp.exp(s - jnp.max(s, axis=0, keepdims=True))
         p = e * (1.0 / jnp.sum(e, axis=0, keepdims=True))
         low = p.astype(BF16)
-        dp = dot_nt(v, do)
+        dp = dot_nt(vh, do)
         delta = jnp.sum(low.astype(F32) * dp, axis=0, keepdims=True)
         ds = (p * (dp - delta)).astype(BF16)
-        qg[:, cols] = (dot_tn(ds, k) * SCALE).astype(BF16)
-        dk = dk + jnp.dot(ds, qh, preferred_element_type=F32)
-        dv = dv + jnp.dot(low, do, preferred_element_type=F32)
-    dk = dk * SCALE
+        dq = (dot_tn(ds, kh) * SCALE).astype(BF16)
+        for g in range(GROUP):
+            qg[rows, cols[g]] = dq[g * half : (g + 1) * half]
+        dk.append(jnp.dot(ds, qh, preferred_element_type=F32))
+        dv.append(jnp.dot(low, do, preferred_element_type=F32))
+    dk = jnp.concatenate([dk[0] + dk[1][:half], dk[1][half:]], axis=0) * SCALE
+    dv = jnp.concatenate([dv[0] + dv[1][:half], dv[1][half:]], axis=0)
     at = pl.multiple_of(pl.program_id(0) * HD, HD)
     kvg[:, pl.ds(at, HD)] = (dk * cosine - pltpu.roll(dk, HD // 2, 1) * sine).astype(BF16)
     kvg[:, pl.ds(at + KVH * HD, HD)] = dv.astype(BF16)

time: 182 us -> 179 us (0.984)
  Pallas kernels: 26.6 us -> 23.6 us
    pallas_call x1, Pallas kernels: 10.4 us -> 7.29 us  [attention_backward(): pl.pallas_call(attention_kernel, grid=(KVH,), in_specs=[pl.BlockSpec((len...]
where the time goes in v7:
time: 179 us; the launch traced here: 178 us
  waiting for transfers between devices  73.3 us (41%)
  starting transfers between devices  38.3 us (21%)
  Pallas kernels  23.6 us (13%)
  between operations  15.7 us (9%)
  local copies, waits for them, and re-layouts  14.3 us (8%)
  other arithmetic  6.91 us (4%)
  matrix products  6.5 us (4%)
    all_gather x1, waiting for transfers between devices, body(): lax.all_gather(kv_weight, ('yl', 'z', 'c'), axis=0, tiled=True)  28 us
    ppermute x12, waiting for transfers between devices, swap(): return lax.ppermute(v, axis, [(i, i ^ bit) for i in range(n)])  24.9 us
    ppermute x12, starting transfers between devices, swap(): return lax.ppermute(v, axis, [(i, i ^ bit) for i in range(n)])  19.6 us
    ppermute x8, waiting for transfers between devices, shift(): return lax.ppermute(v, axis, [(i, (i + k) % n) for i in range(n)])  18.7 us
    ppermute x8, starting transfers between devices, shift(): return lax.ppermute(v, axis, [(i, (i + k) % n) for i in range(n)])  10.8 us
    pallas_call x1, Pallas kernels, hidden_gradient(): pl.pallas_call(hidden_grad_kernel, grid=(8,), in_specs=[pl.BlockSpec((len...  9.75 us
    unnamed x26, local copies, waits for them, and re-layouts  8.22 us
    all_to_all x1, starting transfers between devices, body(): lax.all_to_all(sum_z.reshape(16, RZ, HD), ('x', *Y), 0, 0, tiled=True)  7.77 us
  transfers between devices with their start and end apart: 23, of which 16 were waited for; matrix products, arithmetic and copies ran while one was open for 9% of the time, Pallas kernels for 7%

profile of v7, /device:TPU:2, one launch (start us, length us, event | category | flops | bytes accessed | tf_op | source)
XLA Modules:
  0.0 178.5 jit_solution(7243875419021788720)
XLA Ops:
  13.3 4.4 %copy.21 = bf16[256,5120]{0,1:T(8,128)(2,1)} copy(bf16[256,5120]{1,0:T(8,128)(2,1)} %param.10) | data formatting | bytes 5242880 | tf_op args[0]
  18.4 2.4 %collective-permute-start.2 = (f32[8,128]{1,0:T(8,128)S(1)}, f32[8,128]{1,0:T(8,128)S(1)}, u32[]{:S(2)}, u32[]{:S(2)}) collective-permute-start(f32[8,128]{1,0:T(8,128)S(1)} %broadcast_add_fusion), channel_id=1, source_target_pairs={{0,64},{64,0},{128,192},{192,128},{1,65},{65,1},{129,193},{193,129... | collective-permute-start | bytes 12296 | tf_op jit(solution)/shard_map/ppermute | solution.py:43
  20.7 3.0 %dynamic-slice_bitcast_fusion = (bf16[16,160,256]{2,1,0:T(8,128)(2,1)}, bf16[16,1,160,256]{3,2,1,0:T(8,128)(2,1)S(1)}) fusion(bf16[16,2,160,256]{3,2,1,0:T(8,128)(2,1)} %bitcast.60, s32[]{:T(128)S(6)} %select_n.58, s32[]{:T(128)S(6)} %select_n.57), kind=kLoop, calls=%fused_computation.4 | loop fusion | bytes 5242888 | tf_op jit(solution)/shard_map/jit(dynamic_index_in_dim)/squeeze | solution.py:225
  25.4 4.4 %collective-permute-done.3 = f32[8,128]{1,0:T(8,128)S(1)} collective-permute-done((f32[8,128]{1,0:T(8,128)S(1)}, f32[8,128]{1,0:T(8,128)S(1)}, u32[]{:S(2)}, u32[]{:S(2)}) %collective-permute-start.3) | collective-permute-done | bytes 4128 | tf_op jit(solution)/shard_map/ppermute | solution.py:43
  29.8 3.6 %collective-permute-done.4 = f32[8,128]{1,0:T(8,128)S(1)} collective-permute-done((f32[8,128]{1,0:T(8,128)S(1)}, f32[8,128]{1,0:T(8,128)S(1)}, u32[]{:S(2)}, u32[]{:S(2)}) %collective-permute-start.4) | collective-permute-done | bytes 4128 | tf_op jit(solution)/shard_map/ppermute | solution.py:43
  33.4 1.5 collective-permute-start.5
  35.4 3.1 %collective-permute-done.5 = f32[8,128]{1,0:T(8,128)S(1)} collective-permute-done((f32[8,128]{1,0:T(8,128)S(1)}, f32[8,128]{1,0:T(8,128)S(1)}, u32[]{:S(2)}, u32[]{:S(2)}) %collective-permute-start.5) | collective-permute-done | bytes 4128 | tf_op jit(solution)/shard_map/ppermute | solution.py:43
  38.7 3.5 %collective-permute-done.6 = f32[8,128]{1,0:T(8,128)S(1)} collective-permute-done((f32[8,128]{1,0:T(8,128)S(1)}, f32[8,128]{1,0:T(8,128)S(1)}, u32[]{:S(2)}, u32[]{:S(2)}) %collective-permute-start.6) | collective-permute-done | bytes 4128 | tf_op jit(solution)/shard_map/ppermute | solution.py:43
  42.2 1.5 collective-permute-start.7
  43.8 3.0 %collective-permute-done.7 = f32[8,128]{1,0:T(8,128)S(1)} collective-permute-done((f32[8,128]{1,0:T(8,128)S(1)}, f32[8,128]{1,0:T(8,128)S(1)}, u32[]{:S(2)}, u32[]{:S(2)}) %collective-permute-start.7) | collective-permute-done | bytes 4128 | tf_op jit(solution)/shard_map/ppermute | solution.py:43
  46.8 5.4 %collective-permute-start.8 = (f32[8,128]{1,0:T(8,128)S(1)}, f32[8,128]{1,0:T(8,128)S(1)}, u32[]{:S(2)}, u32[]{:S(2)}) collective-permute-start(f32[8,128]{1,0:T(8,128)S(1)} %add.111), channel_id=1, source_target_pairs={{0,8},{2,10},{4,12},{6,14},{8,0},{10,2},{12,4},{14,6},{1,9},{3,11}... | collective-permute-start | bytes 12296 | tf_op jit(solution)/shard_map/ppermute | solution.py:43
  52.6 1.8 %collective-permute-done.8 = f32[8,128]{1,0:T(8,128)S(1)} collective-permute-done((f32[8,128]{1,0:T(8,128)S(1)}, f32[8,128]{1,0:T(8,128)S(1)}, u32[]{:S(2)}, u32[]{:S(2)}) %collective-permute-start.8) | collective-permute-done | bytes 4128 | tf_op jit(solution)/shard_map/ppermute | solution.py:43
  59.8 28.0 %all-gather.2.cloned.1.call-done.w = bf16[5120,1024]{1,0:T(8,128)(2,1)} async-done(((bf16[160,1024]{1,0:T(8,128)(2,1)}), bf16[5120,1024]{1,0:T(8,128)(2,1)}) %all-gather.2.cloned.1.call-update) | async-done | bytes 10485776 | tf_op jit(solution)/shard_map/all_gather | solution.py:254
  87.9 6.5 %fusion.9.kpre.vpre = f32[256,1024]{1,0:T(8,128)S(1)} fusion(bf16[256,5120]{1,0:T(8,128)(2,1)} %param.10, bf16[5120,1024]{1,0:T(8,128)(2,1)} %all-gather.2.cloned.1.call-done.w), kind=kOutput, calls=%fused_computation.49 | convolution fusion | flops 2684354560 | bytes 14155776 | tf_op jit(solution)/shard_map/dot_general | solution.py:270
  94.4 7.3 %shard_map.137 = (bf16[256,2560]{1,0:T(8,128)(2,1)}, bf16[256,1024]{1,0:T(8,128)(2,1)S(1)}) custom-call(f32[256,1024]{1,0:T(8,128)S(1)} %fusion.9.kpre.vpre, f32[256,1024]{1,0:T(8,128)S(1)} %fusion.9.kpre.vpre, bf16[256,2560]{1,0:T(8,128)(2,1)S(1)} %copy-done.1, bf16[256,2560]{1,0:T(8,128)(2,1)S(1)} %copy-done.2, f32[256,128]{1,0:T(8,128)S(1)} %get-tuple-element.80.cos, ...), custom_call_target="tpu_custom_call" | custom-call | tf_op jit(solution)/shard_map/pallas_call | solution.py:109
  102.0 1.6 collective-permute-done.9
  103.6 3.6 %shard_map.140 = bf16[12288,128]{1,0:T(8,128)(2,1)} custom-call(bf16[8,192,512]{2,1,0:T(8,128)(2,1)S(1)} %bitcast.56, bf16[512,1024]{1,0:T(8,128)(2,1)S(1)} %constant_dynamic-update-slice_fusion.pair), custom_call_target="tpu_custom_call" | custom-call | tf_op jit(solution)/shard_map/pallas_call | solution.py:167
  108.4 1.8 %shard_map.138 = (bf16[1024,256]{1,0:T(8,128)(2,1)S(1)}, bf16[1024,256]{1,0:T(8,128)(2,1)S(1)}, bf16[1024,256]{1,0:T(8,128)(2,1)S(1)}, bf16[1024,256]{1,0:T(8,128)(2,1)S(1)}) custom-call(s32[2]{0:T(128)S(1)} %pad_add_fusion.place, bf16[1024,512]{1,0:T(8,128)(2,1)S(1)} %bitcast.57, bf16[512,1024]{1,0:T(8,128)(2,1)S(1)} %constant_dynamic-update-slice_fusion.pair), custom_call_target="tpu_custom_call" | custom-call | tf_op jit(solution)/shard_map/pallas_call | solution.py:192
  110.2 2.0 %collective-permute-start.10 = (bf16[1024,256]{1,0:T(8,128)(2,1)S(1)}, bf16[1024,256]{1,0:T(8,128)(2,1)S(1)}, u32[]{:S(2)}, u32[]{:S(2)}) collective-permute-start(bf16[1024,256]{1,0:T(8,128)(2,1)S(1)} %get-tuple-element.44), channel_id=1, source_target_pairs={{0,64},{64,128},{128,192},{192,0},{1,65},{65,129},{129,193},{193,1... | collective-permute-start | bytes 1572872 | tf_op jit(solution)/shard_map/ppermute | solution.py:39
  113.3 2.0 %collective-permute-start.12 = (bf16[1024,256]{1,0:T(8,128)(2,1)S(1)}, bf16[1024,256]{1,0:T(8,128)(2,1)S(1)}, u32[]{:S(2)}, u32[]{:S(2)}) collective-permute-start(bf16[1024,256]{1,0:T(8,128)(2,1)S(1)} %get-tuple-element.46), channel_id=1, source_target_pairs={{0,192},{64,0},{128,64},{192,128},{1,193},{65,1},{129,65},{193,129... | collective-permute-start | bytes 1572872 | tf_op jit(solution)/shard_map/ppermute | solution.py:39
  115.3 9.8 %shard_map.139 = bf16[256,5120]{1,0:T(8,128)(2,1)} custom-call(bf16[256,1024]{1,0:T(8,128)(2,1)S(1)} %get-tuple-element.47.kv, bf16[5120,1024]{1,0:T(8,128)(2,1)} %all-gather.2.cloned.1.call-done.w), custom_call_target="tpu_custom_call" | custom-call | tf_op jit(solution)/shard_map/pallas_call | solution.py:142
  125.1 10.1 %collective-permute-done.10.refs_1_ = bf16[1024,256]{1,0:T(8,128)(2,1)S(1)} collective-permute-done((bf16[1024,256]{1,0:T(8,128)(2,1)S(1)}, bf16[1024,256]{1,0:T(8,128)(2,1)S(1)}, u32[]{:S(2)}, u32[]{:S(2)}) %collective-permute-start.10) | collective-permute-done | bytes 524320 | tf_op jit(solution)/shard_map/ppermute | solution.py:39
  135.1 2.9 %collective-permute-done.12.refs_3_ = bf16[1024,256]{1,0:T(8,128)(2,1)S(1)} collective-permute-done((bf16[1024,256]{1,0:T(8,128)(2,1)S(1)}, bf16[1024,256]{1,0:T(8,128)(2,1)S(1)}, u32[]{:S(2)}, u32[]{:S(2)}) %collective-permute-start.12) | collective-permute-done | bytes 524320 | tf_op jit(solution)/shard_map/ppermute | solution.py:39
  140.3 2.6 %collective-permute-start.14 = (bf16[512,128]{1,0:T(8,128)(2,1)S(1)}, bf16[512,128]{1,0:T(8,128)(2,1)S(1)}, u32[]{:S(2)}, u32[]{:S(2)}) collective-permute-start(bf16[512,128]{1,0:T(8,128)(2,1)S(1)} %get-tuple-element.56), channel_id=1, source_target_pairs={{0,32},{16,48},{32,0},{48,16},{1,33},{17,49},{33,1},{49,17},{2,34}... | collective-permute-start | bytes 393224 | tf_op jit(solution)/shard_map/ppermute | solution.py:39
  142.9 1.6 collective-permute-start.15
  144.5 2.3 %collective-permute-done.13 = bf16[512,128]{1,0:T(8,128)(2,1)S(1)} collective-permute-done((bf16[512,128]{1,0:T(8,128)(2,1)S(1)}, bf16[512,128]{1,0:T(8,128)(2,1)S(1)}, u32[]{:S(2)}, u32[]{:S(2)}) %collective-permute-start.13) | collective-permute-done | bytes 131104 | tf_op jit(solution)/shard_map/ppermute | solution.py:39
  146.9 1.4 collective-permute-done.14
  148.7 3.4 %collective-permute-start.16 = (bf16[4,64,128]{2,1,0:T(8,128)(2,1)S(1)}, bf16[4,64,128]{2,1,0:T(8,128)(2,1)S(1)}, u32[]{:S(2)}, u32[]{:S(2)}) collective-permute-start(bf16[4,64,128]{2,1,0:T(8,128)(2,1)S(1)} %dynamic-slice_bitcast_fusion.1), channel_id=1, source_target_pairs={{0,8},{2,10},{4,12},{6,14},{8,0},{10,2},{12,4},{14,6},{1,9},{3,11}... | collective-permute-start | bytes 196616 | tf_op jit(solution)/shard_map/ppermute | solution.py:43
  153.0 7.8 %all-to-all-start = ((bf16[16,96,128]{2,1,0:T(8,128)(2,1)}), bf16[16,96,128]{2,1,0:T(8,128)(2,1)S(1)}, u32[]{:S(2)}, u32[]{:S(2)}) async-start(bf16[16,96,128]{2,1,0:T(8,128)(2,1)} %bitcast.65), calls=%async_computation.1 | async-start | bytes 786432 | tf_op jit(solution)/shard_map/all_to_all | solution.py:286
  161.5 3.8 %collective-permute-start.18 = (bf16[64,128]{1,0:T(8,128)(2,1)S(1)}, bf16[64,128]{1,0:T(8,128)(2,1)S(1)}, u32[]{:S(2)}, u32[]{:S(2)}) collective-permute-start(bf16[64,128]{1,0:T(8,128)(2,1)S(1)} %get-tuple-element.75), channel_id=1, source_target_pairs={{0,4},{2,6},{4,0},{6,2},{8,12},{10,14},{12,8},{14,10},{1,5},{3,7},... | collective-permute-start | bytes 49160 | tf_op jit(solution)/shard_map/ppermute | solution.py:43
  165.4 1.6 collective-permute-done.18
  167.0 3.8 %collective-permute-done.19 = bf16[64,128]{1,0:T(8,128)(2,1)S(1)} collective-permute-done((bf16[64,128]{1,0:T(8,128)(2,1)S(1)}, bf16[64,128]{1,0:T(8,128)(2,1)S(1)}, u32[]{:S(2)}, u32[]{:S(2)}) %collective-permute-start.19) | collective-permute-done | bytes 16416 | tf_op jit(solution)/shard_map/ppermute | solution.py:43
  (90 shorter events, 21.2 us)
Async XLA Ops:
  7.2 80.7 %all-gather.2.cloned.1.call-start = ((), (), s32[]{:S(2)}) async-start(), calls=%async_computation.2 | async-start | bytes 10813440 | tf_op jit(solution)/shard_map/all_gather | solution.py:254
  7.9 145.1 %reduce-scatter.2.cloned.1.call-start = ((), (), s32[]{:S(2)}) async-start(), calls=%async_computation.3 | async-start | bytes 3538944 | tf_op jit(solution)/shard_map/reduce_scatter | solution.py:274
  13.2 4.5 %collective-permute-start.1 = (f32[8,128]{1,0:T(8,128)S(1)}, f32[8,128]{1,0:T(8,128)S(1)}, u32[]{:S(2)}, u32[]{:S(2)}) collective-permute-start(f32[8,128]{1,0:T(8,128)S(1)} %broadcast_in_dim.57), channel_id=1, source_target_pairs={{0,1},{1,0},{2,3},{3,2},{4,5},{5,4},{6,7},{7,6},{8,9},{9,8},{10,11... | collective-permute-start | bytes 12296 | tf_op jit(solution)/shard_map/ppermute | solution.py:43
  18.4 5.5 %collective-permute-start.2 = (f32[8,128]{1,0:T(8,128)S(1)}, f32[8,128]{1,0:T(8,128)S(1)}, u32[]{:S(2)}, u32[]{:S(2)}) collective-permute-start(f32[8,128]{1,0:T(8,128)S(1)} %broadcast_add_fusion), channel_id=1, source_target_pairs={{0,64},{64,0},{128,192},{192,128},{1,65},{65,1},{129,193},{193,129... | collective-permute-start | bytes 12296 | tf_op jit(solution)/shard_map/ppermute | solution.py:43
  20.7 31.5 %copy-start.10 = (s32[1,256]{1,0:T(1,128)S(1)}, s32[1,256]{1,0:T(1,128)}, u32[]{:S(2)}) copy-start(s32[1,256]{1,0:T(1,128)} %param.13) | copy-start | bytes 3076
  20.7 31.5 %copy-start.11 = (f32[1,4]{1,0:T(1,128)S(1)}, f32[1,4]{1,0:T(1,128)}, u32[]{:S(2)}) copy-start(f32[1,4]{1,0:T(1,128)} %param.15) | copy-start | bytes 52
  23.7 32.1 %copy-start.3 = (bf16[16,1,160,256]{3,2,1,0:T(8,128)(2,1)}, bf16[16,1,160,256]{3,2,1,0:T(8,128)(2,1)S(1)}, u32[]{:S(2)}) copy-start(bf16[16,1,160,256]{3,2,1,0:T(8,128)(2,1)S(1)} %get-tuple-element.73) | copy-start | bytes 3932164
  23.7 32.1 %collective-permute-start = (bf16[16,160,256]{2,1,0:T(8,128)(2,1)}, bf16[16,160,256]{2,1,0:T(8,128)(2,1)S(1)}, u32[]{:S(2)}, u32[]{:S(2)}) collective-permute-start(bf16[16,160,256]{2,1,0:T(8,128)(2,1)} %get-tuple-element.72), channel_id=1, source_target_pairs={{0,1},{1,0},{2,3},{3,2},{4,5},{5,4},{6,7},{7,6},{8,9},{9,8},{10,11... | collective-permute-start | bytes 3932168 | tf_op jit(solution)/shard_map/ppermute | solution.py:39
  24.6 5.2 %collective-permute-start.3 = (f32[8,128]{1,0:T(8,128)S(1)}, f32[8,128]{1,0:T(8,128)S(1)}, u32[]{:S(2)}, u32[]{:S(2)}) collective-permute-start(f32[8,128]{1,0:T(8,128)S(1)} %fusion.12), channel_id=1, source_target_pairs={{0,128},{64,192},{128,0},{192,64},{1,129},{65,193},{129,1},{193,65... | collective-permute-start | bytes 12296 | tf_op jit(solution)/shard_map/ppermute | solution.py:43
  29.8 3.6 %collective-permute-start.4 = (f32[8,128]{1,0:T(8,128)S(1)}, f32[8,128]{1,0:T(8,128)S(1)}, u32[]{:S(2)}, u32[]{:S(2)}) collective-permute-start(f32[8,128]{1,0:T(8,128)S(1)} %add.107), channel_id=1, source_target_pairs={{0,16},{16,0},{1,17},{17,1},{2,18},{18,2},{3,19},{19,3},{4,20},{20... | collective-permute-start | bytes 12296 | tf_op jit(solution)/shard_map/ppermute | solution.py:43
  33.4 5.1 %collective-permute-start.5 = (f32[8,128]{1,0:T(8,128)S(1)}, f32[8,128]{1,0:T(8,128)S(1)}, u32[]{:S(2)}, u32[]{:S(2)}) collective-permute-start(f32[8,128]{1,0:T(8,128)S(1)} %add.108), channel_id=1, source_target_pairs={{0,32},{32,0},{1,33},{33,1},{2,34},{34,2},{3,35},{35,3},{4,36},{36... | collective-permute-start | bytes 12296 | tf_op jit(solution)/shard_map/ppermute | solution.py:43
  38.6 3.6 %collective-permute-start.6 = (f32[8,128]{1,0:T(8,128)S(1)}, f32[8,128]{1,0:T(8,128)S(1)}, u32[]{:S(2)}, u32[]{:S(2)}) collective-permute-start(f32[8,128]{1,0:T(8,128)S(1)} %add.109), channel_id=1, source_target_pairs={{0,2},{2,0},{4,6},{6,4},{8,10},{10,8},{12,14},{14,12},{1,3},{3,1},... | collective-permute-start | bytes 12296 | tf_op jit(solution)/shard_map/ppermute | solution.py:43
  42.2 4.6 %collective-permute-start.7 = (f32[8,128]{1,0:T(8,128)S(1)}, f32[8,128]{1,0:T(8,128)S(1)}, u32[]{:S(2)}, u32[]{:S(2)}) collective-permute-start(f32[8,128]{1,0:T(8,128)S(1)} %add.110), channel_id=1, source_target_pairs={{0,4},{2,6},{4,0},{6,2},{8,12},{10,14},{12,8},{14,10},{1,5},{3,7},... | collective-permute-start | bytes 12296 | tf_op jit(solution)/shard_map/ppermute | solution.py:43
  46.8 7.6 %collective-permute-start.8 = (f32[8,128]{1,0:T(8,128)S(1)}, f32[8,128]{1,0:T(8,128)S(1)}, u32[]{:S(2)}, u32[]{:S(2)}) collective-permute-start(f32[8,128]{1,0:T(8,128)S(1)} %add.111), channel_id=1, source_target_pairs={{0,8},{2,10},{4,12},{6,14},{8,0},{10,2},{12,4},{14,6},{1,9},{3,11}... | collective-permute-start | bytes 12296 | tf_op jit(solution)/shard_map/ppermute | solution.py:43
  57.0 1.7 copy-start.6
  87.9 6.5 %copy-start.1 = (bf16[256,2560]{1,0:T(8,128)(2,1)S(1)}, bf16[256,2560]{1,0:T(8,128)(2,1)}, u32[]{:S(2)}) copy-start(bf16[256,2560]{1,0:T(8,128)(2,1)} %q.1) | copy-start | bytes 3932164
  87.9 6.5 %copy-start.2 = (bf16[256,2560]{1,0:T(8,128)(2,1)S(1)}, bf16[256,2560]{1,0:T(8,128)(2,1)}, u32[]{:S(2)}) copy-start(bf16[256,2560]{1,0:T(8,128)(2,1)} %up.1) | copy-start | bytes 3932164
  101.7 1.9 %collective-permute-start.9 = (bf16[256,1024]{1,0:T(8,128)(2,1)S(1)}, bf16[256,1024]{1,0:T(8,128)(2,1)S(1)}, u32[]{:S(2)}, u32[]{:S(2)}) collective-permute-start(bf16[256,1024]{1,0:T(8,128)(2,1)S(1)} %get-tuple-element.47.kv), channel_id=1, source_target_pairs={{0,1},{1,0},{2,3},{3,2},{4,5},{5,4},{6,7},{7,6},{8,9},{9,8},{10,11... | collective-permute-start | bytes 1572872 | tf_op jit(solution)/shard_map/ppermute | solution.py:39
  110.2 24.9 %collective-permute-start.10 = (bf16[1024,256]{1,0:T(8,128)(2,1)S(1)}, bf16[1024,256]{1,0:T(8,128)(2,1)S(1)}, u32[]{:S(2)}, u32[]{:S(2)}) collective-permute-start(bf16[1024,256]{1,0:T(8,128)(2,1)S(1)} %get-tuple-element.44), channel_id=1, source_target_pairs={{0,64},{64,128},{128,192},{192,0},{1,65},{65,129},{129,193},{193,1... | collective-permute-start | bytes 1572872 | tf_op jit(solution)/shard_map/ppermute | solution.py:39
  112.3 22.9 %collective-permute-start.11 = (bf16[1024,256]{1,0:T(8,128)(2,1)S(1)}, bf16[1024,256]{1,0:T(8,128)(2,1)S(1)}, u32[]{:S(2)}, u32[]{:S(2)}) collective-permute-start(bf16[1024,256]{1,0:T(8,128)(2,1)S(1)} %get-tuple-element.45), channel_id=1, source_target_pairs={{0,128},{64,192},{128,0},{192,64},{1,129},{65,193},{129,1},{193,65... | collective-permute-start | bytes 1572872 | tf_op jit(solution)/shard_map/ppermute | solution.py:39
  113.3 24.7 %collective-permute-start.12 = (bf16[1024,256]{1,0:T(8,128)(2,1)S(1)}, bf16[1024,256]{1,0:T(8,128)(2,1)S(1)}, u32[]{:S(2)}, u32[]{:S(2)}) collective-permute-start(bf16[1024,256]{1,0:T(8,128)(2,1)S(1)} %get-tuple-element.46), channel_id=1, source_target_pairs={{0,192},{64,0},{128,64},{192,128},{1,193},{65,1},{129,65},{193,129... | collective-permute-start | bytes 1572872 | tf_op jit(solution)/shard_map/ppermute | solution.py:39
  125.1 45.8 %copy-start.7 = (f32[160,128]{1,0:T(8,128)S(1)}, f32[160,128]{1,0:T(8,128)}, u32[]{:S(2)}) copy-start(f32[160,128]{1,0:T(8,128)} %param.17) | copy-start | bytes 245764
  125.1 45.9 %copy-start.8 = (f32[160,128]{1,0:T(8,128)S(1)}, f32[160,128]{1,0:T(8,128)}, u32[]{:S(2)}) copy-start(f32[160,128]{1,0:T(8,128)} %param.18) | copy-start | bytes 245764
  125.1 45.9 %copy-start.9 = (f32[160,128]{1,0:T(8,128)S(1)}, f32[160,128]{1,0:T(8,128)}, u32[]{:S(2)}) copy-start(f32[160,128]{1,0:T(8,128)} %param.19) | copy-start | bytes 245764
  139.2 7.7 %collective-permute-start.13 = (bf16[512,128]{1,0:T(8,128)(2,1)S(1)}, bf16[512,128]{1,0:T(8,128)(2,1)S(1)}, u32[]{:S(2)}, u32[]{:S(2)}) collective-permute-start(bf16[512,128]{1,0:T(8,128)(2,1)S(1)} %get-tuple-element.55), channel_id=1, source_target_pairs={{0,16},{16,32},{32,48},{48,0},{1,17},{17,33},{33,49},{49,1},{2,18}... | collective-permute-start | bytes 393224 | tf_op jit(solution)/shard_map/ppermute | solution.py:39
  140.3 8.1 %collective-permute-start.14 = (bf16[512,128]{1,0:T(8,128)(2,1)S(1)}, bf16[512,128]{1,0:T(8,128)(2,1)S(1)}, u32[]{:S(2)}, u32[]{:S(2)}) collective-permute-start(bf16[512,128]{1,0:T(8,128)(2,1)S(1)} %get-tuple-element.56), channel_id=1, source_target_pairs={{0,32},{16,48},{32,0},{48,16},{1,33},{17,49},{33,1},{49,17},{2,34}... | collective-permute-start | bytes 393224 | tf_op jit(solution)/shard_map/ppermute | solution.py:39
  142.9 5.7 %collective-permute-start.15 = (bf16[512,128]{1,0:T(8,128)(2,1)S(1)}, bf16[512,128]{1,0:T(8,128)(2,1)S(1)}, u32[]{:S(2)}, u32[]{:S(2)}) collective-permute-start(bf16[512,128]{1,0:T(8,128)(2,1)S(1)} %get-tuple-element.57), channel_id=1, source_target_pairs={{0,48},{16,0},{32,16},{48,32},{1,49},{17,1},{33,17},{49,33},{2,50}... | collective-permute-start | bytes 393224 | tf_op jit(solution)/shard_map/ppermute | solution.py:39
  148.7 12.1 %collective-permute-start.16 = (bf16[4,64,128]{2,1,0:T(8,128)(2,1)S(1)}, bf16[4,64,128]{2,1,0:T(8,128)(2,1)S(1)}, u32[]{:S(2)}, u32[]{:S(2)}) collective-permute-start(bf16[4,64,128]{2,1,0:T(8,128)(2,1)S(1)} %dynamic-slice_bitcast_fusion.1), channel_id=1, source_target_pairs={{0,8},{2,10},{4,12},{6,14},{8,0},{10,2},{12,4},{14,6},{1,9},{3,11}... | collective-permute-start | bytes 196616 | tf_op jit(solution)/shard_map/ppermute | solution.py:43
  153.0 17.8 %all-to-all-start = ((bf16[16,96,128]{2,1,0:T(8,128)(2,1)}), bf16[16,96,128]{2,1,0:T(8,128)(2,1)S(1)}, u32[]{:S(2)}, u32[]{:S(2)}) async-start(bf16[16,96,128]{2,1,0:T(8,128)(2,1)} %bitcast.65), calls=%async_computation.1 | async-start | bytes 786432 | tf_op jit(solution)/shard_map/all_to_all | solution.py:286
  160.9 4.5 %collective-permute-start.17 = (bf16[64,128]{1,0:T(8,128)(2,1)S(1)}, bf16[64,128]{1,0:T(8,128)(2,1)S(1)}, u32[]{:S(2)}, u32[]{:S(2)}) collective-permute-start(bf16[64,128]{1,0:T(8,128)(2,1)S(1)} %get-tuple-element.76), channel_id=1, source_target_pairs={{0,2},{2,0},{4,6},{6,4},{8,10},{10,8},{12,14},{14,12},{1,3},{3,1},... | collective-permute-start | bytes 49160 | tf_op jit(solution)/shard_map/ppermute | solution.py:43
  161.5 5.5 %collective-permute-start.18 = (bf16[64,128]{1,0:T(8,128)(2,1)S(1)}, bf16[64,128]{1,0:T(8,128)(2,1)S(1)}, u32[]{:S(2)}, u32[]{:S(2)}) collective-permute-start(bf16[64,128]{1,0:T(8,128)(2,1)S(1)} %get-tuple-element.75), channel_id=1, source_target_pairs={{0,4},{2,6},{4,0},{6,2},{8,12},{10,14},{12,8},{14,10},{1,5},{3,7},... | collective-permute-start | bytes 49160 | tf_op jit(solution)/shard_map/ppermute | solution.py:43
  165.3 5.5 %collective-permute-start.19 = (bf16[64,128]{1,0:T(8,128)(2,1)S(1)}, bf16[64,128]{1,0:T(8,128)(2,1)S(1)}, u32[]{:S(2)}, u32[]{:S(2)}) collective-permute-start(bf16[64,128]{1,0:T(8,128)(2,1)S(1)} %get-tuple-element.74), channel_id=1, source_target_pairs={{0,6},{2,4},{4,2},{6,0},{8,14},{10,12},{12,10},{14,8},{1,7},{3,5},... | collective-permute-start | bytes 49160 | tf_op jit(solution)/shard_map/ppermute | solution.py:43
  (3 other events, 3.6 us)
Sparse Core Ops, SparseCore 0:
  9.9 77.9 all-gather.1
  107.4 45.6 reduce-scatter.1

commit v8 on v7

--- a/solution.py
+++ b/solution.py
@@ -15,6 +15,8 @@
 Y = ("yh", "yl")
 F32 = jnp.float32
 BF16 = jnp.bfloat16
+VMEM = pl.BlockSpec(memory_space=pltpu.VMEM)
+SMEM = pl.BlockSpec(memory_space=pltpu.SMEM)
 
 
 def positions_in_row(segs):
@@ -153,8 +155,8 @@
 
 
 def first_terms_kernel(h, pair, out):
-    planes, rows, depth = h.shape
-    block = h[...].reshape(planes * rows, depth)
+    planes, rows, depth = 2, h.shape[1], h.shape[2]
+    block = h[pl.ds(planes * pl.program_id(0), planes)].reshape(planes * rows, depth)
     term = jnp.dot(block, pair[...], preferred_element_type=F32).astype(BF16)
     for p in range(planes):
         for j in range(8):
@@ -167,10 +169,7 @@
     return pl.pallas_call(
         first_terms_kernel,
         grid=(planes // 2,),
-        in_specs=[
-            pl.BlockSpec((2, rows, depth), lambda i: (i, 0, 0)),
-            pl.BlockSpec(pair.shape, lambda i: (0, 0)),
-        ],
+        in_specs=[VMEM, VMEM],
         out_specs=pl.BlockSpec((16 * rows, HD), lambda i: (i, 0)),
         out_shape=jax.ShapeDtypeStruct((planes * 8 * rows, HD), BF16),
         compiler_params=pltpu.CompilerParams(vmem_limit_bytes=24 * 2**20),
@@ -182,10 +181,6 @@
         at = pl.multiple_of(lax.rem(place[0] + k, 4) * 2 * HD, 2 * HD)
         cols = pair[:, pl.ds(at, 2 * HD)]
         outs[k][...] = jnp.dot(ha[...], cols, preferred_element_type=F32).astype(BF16)
-
-
-VMEM = pl.BlockSpec(memory_space=pltpu.VMEM)
-SMEM = pl.BlockSpec(memory_space=pltpu.SMEM)
 
 
 def terms(place, ha, pair):
@@ -284,17 +279,13 @@
     arrived = barrier(tuple(shift(out[k], Y, 4, k) for k in (1, 2, 3)))
     a = add_up([out[0], *arrived]).astype(BF16).reshape(2, 4, rows - RZ, HD)
     blocks = lax.all_to_all(sum_z.reshape(16, RZ, HD), ("x", *Y), 0, 0, tiled=True)
-    theirs = swap(pick(a, 1 - z // 4, 0), "z", 8, 4)
+    near = lax.rem(z, 4)
+    theirs = tuple(swap(pick(a, near ^ k, 1), "z", 8, k) for k in (1, 2, 3))
     theirs, a, _ = barrier((theirs, a, sum_z))
-    a = add_up([pick(a, z // 4, 0), theirs]).astype(BF16)
-    sent = tuple(swap(pick(a, lax.rem(z, 4) ^ k, 0), "z", 8, k) for k in (1, 2, 3))
-    arrived = barrier((blocks, *sent))
+    a = add_up([pick(a, near, 1), *theirs]).astype(BF16)
+    blocks, far = barrier((blocks, swap(pick(a, 1 - z // 4, 0), "z", 8, 4)))
     summed = jnp.concatenate(
-        [
-            jnp.sum(arrived[0].astype(F32), axis=0),
-            add_up([pick(a, lax.rem(z, 4), 0), *arrived[1:]]),
-        ],
-        axis=0,
+        [jnp.sum(blocks.astype(F32), axis=0), add_up([pick(a, z // 4, 0), far])], axis=0
     )
     weight_grad = summed / F32(total_tokens)
     new_moment_one = 0.9 * moment_one + 0.1 * weight_grad

time: 179 us -> 177 us (0.989)
  waiting for transfers between devices: 73.3 us -> 70.9 us
  transfers between devices with their start and end apart: 23 -> 23, of which waited for: 16 -> 14; matrix products, arithmetic and copies ran while one was open for 9% -> 9% of each run, Pallas kernels for 7% -> 7%
where the time goes in v8:
time: 177 us; the launch traced here: 176 us
  waiting for transfers between devices  70.9 us (40%)
  starting transfers between devices  38.1 us (22%)
  Pallas kernels  23.6 us (13%)
  between operations  15.7 us (9%)
  local copies, waits for them, and re-layouts  14.3 us (8%)
  other arithmetic  6.91 us (4%)
  matrix products  6.5 us (4%)
    all_gather x1, waiting for transfers between devices, body(): lax.all_gather(kv_weight, ('yl', 'z', 'c'), axis=0, tiled=True)  28 us
    ppermute x12, waiting for transfers between devices, swap(): return lax.ppermute(v, axis, [(i, i ^ bit) for i in range(n)])  23.5 us
    ppermute x12, starting transfers between devices, swap(): return lax.ppermute(v, axis, [(i, i ^ bit) for i in range(n)])  19.9 us
    ppermute x8, waiting for transfers between devices, shift(): return lax.ppermute(v, axis, [(i, (i + k) % n) for i in range(n)])  18.7 us
    ppermute x8, starting transfers between devices, shift(): return lax.ppermute(v, axis, [(i, (i + k) % n) for i in range(n)])  10.8 us
    pallas_call x1, Pallas kernels, hidden_gradient(): pl.pallas_call(hidden_grad_kernel, grid=(8,), in_specs=[pl.BlockSpec((len...  9.75 us
    unnamed x26, local copies, waits for them, and re-layouts  8.22 us
    all_to_all x1, starting transfers between devices, body(): lax.all_to_all(sum_z.reshape(16, RZ, HD), ('x', *Y), 0, 0, tiled=True)  7.33 us
  transfers between devices with their start and end apart: 23, of which 14 were waited for; matrix products, arithmetic and copies ran while one was open for 9% of the time, Pallas kernels for 7%

profile of v8, /device:TPU:2, one launch (start us, length us, event | category | flops | bytes accessed | tf_op | source)
XLA Modules:
  0.0 176.0 jit_solution(4874694910118565649)
XLA Ops:
  13.3 4.4 %copy.23 = bf16[256,5120]{0,1:T(8,128)(2,1)} copy(bf16[256,5120]{1,0:T(8,128)(2,1)} %param.10) | data formatting | bytes 5242880 | tf_op args[0]
  18.4 2.4 %collective-permute-start.2 = (f32[8,128]{1,0:T(8,128)S(1)}, f32[8,128]{1,0:T(8,128)S(1)}, u32[]{:S(2)}, u32[]{:S(2)}) collective-permute-start(f32[8,128]{1,0:T(8,128)S(1)} %broadcast_add_fusion), channel_id=1, source_target_pairs={{0,64},{64,0},{128,192},{192,128},{1,65},{65,1},{129,193},{193,129... | collective-permute-start | bytes 12296 | tf_op jit(solution)/shard_map/ppermute | solution.py:45
  20.7 3.0 %dynamic-slice_bitcast_fusion = (bf16[16,160,256]{2,1,0:T(8,128)(2,1)}, bf16[16,1,160,256]{3,2,1,0:T(8,128)(2,1)S(1)}) fusion(bf16[16,2,160,256]{3,2,1,0:T(8,128)(2,1)} %bitcast.60, s32[]{:T(128)S(6)} %select_n.58, s32[]{:T(128)S(6)} %select_n.57), kind=kLoop, calls=%fused_computation.4 | loop fusion | bytes 5242888 | tf_op jit(solution)/shard_map/jit(dynamic_index_in_dim)/squeeze | solution.py:220
  25.4 4.4 %collective-permute-done.3 = f32[8,128]{1,0:T(8,128)S(1)} collective-permute-done((f32[8,128]{1,0:T(8,128)S(1)}, f32[8,128]{1,0:T(8,128)S(1)}, u32[]{:S(2)}, u32[]{:S(2)}) %collective-permute-start.3) | collective-permute-done | bytes 4128 | tf_op jit(solution)/shard_map/ppermute | solution.py:45
  29.8 3.6 %collective-permute-done.4 = f32[8,128]{1,0:T(8,128)S(1)} collective-permute-done((f32[8,128]{1,0:T(8,128)S(1)}, f32[8,128]{1,0:T(8,128)S(1)}, u32[]{:S(2)}, u32[]{:S(2)}) %collective-permute-start.4) | collective-permute-done | bytes 4128 | tf_op jit(solution)/shard_map/ppermute | solution.py:45
  33.4 1.5 collective-permute-start.5
  35.4 3.1 %collective-permute-done.5 = f32[8,128]{1,0:T(8,128)S(1)} collective-permute-done((f32[8,128]{1,0:T(8,128)S(1)}, f32[8,128]{1,0:T(8,128)S(1)}, u32[]{:S(2)}, u32[]{:S(2)}) %collective-permute-start.5) | collective-permute-done | bytes 4128 | tf_op jit(solution)/shard_map/ppermute | solution.py:45
  38.7 3.5 %collective-permute-done.6 = f32[8,128]{1,0:T(8,128)S(1)} collective-permute-done((f32[8,128]{1,0:T(8,128)S(1)}, f32[8,128]{1,0:T(8,128)S(1)}, u32[]{:S(2)}, u32[]{:S(2)}) %collective-permute-start.6) | collective-permute-done | bytes 4128 | tf_op jit(solution)/shard_map/ppermute | solution.py:45
  42.2 1.5 collective-permute-start.7
  43.8 3.0 %collective-permute-done.7 = f32[8,128]{1,0:T(8,128)S(1)} collective-permute-done((f32[8,128]{1,0:T(8,128)S(1)}, f32[8,128]{1,0:T(8,128)S(1)}, u32[]{:S(2)}, u32[]{:S(2)}) %collective-permute-start.7) | collective-permute-done | bytes 4128 | tf_op jit(solution)/shard_map/ppermute | solution.py:45
  46.8 5.4 %collective-permute-start.8 = (f32[8,128]{1,0:T(8,128)S(1)}, f32[8,128]{1,0:T(8,128)S(1)}, u32[]{:S(2)}, u32[]{:S(2)}) collective-permute-start(f32[8,128]{1,0:T(8,128)S(1)} %add.111), channel_id=1, source_target_pairs={{0,8},{2,10},{4,12},{6,14},{8,0},{10,2},{12,4},{14,6},{1,9},{3,11}... | collective-permute-start | bytes 12296 | tf_op jit(solution)/shard_map/ppermute | solution.py:45
  52.6 1.8 %collective-permute-done.8 = f32[8,128]{1,0:T(8,128)S(1)} collective-permute-done((f32[8,128]{1,0:T(8,128)S(1)}, f32[8,128]{1,0:T(8,128)S(1)}, u32[]{:S(2)}, u32[]{:S(2)}) %collective-permute-start.8) | collective-permute-done | bytes 4128 | tf_op jit(solution)/shard_map/ppermute | solution.py:45
  59.8 28.0 %all-gather.2.cloned.1.call-done.w = bf16[5120,1024]{1,0:T(8,128)(2,1)} async-done(((bf16[160,1024]{1,0:T(8,128)(2,1)}), bf16[5120,1024]{1,0:T(8,128)(2,1)}) %all-gather.2.cloned.1.call-update) | async-done | bytes 10485776 | tf_op jit(solution)/shard_map/all_gather | solution.py:249
  87.9 6.5 %fusion.9.kpre.vpre = f32[256,1024]{1,0:T(8,128)S(1)} fusion(bf16[256,5120]{1,0:T(8,128)(2,1)} %param.10, bf16[5120,1024]{1,0:T(8,128)(2,1)} %all-gather.2.cloned.1.call-done.w), kind=kOutput, calls=%fused_computation.49 | convolution fusion | flops 2684354560 | bytes 14155776 | tf_op jit(solution)/shard_map/dot_general | solution.py:265
  94.4 7.3 %shard_map.137 = (bf16[256,2560]{1,0:T(8,128)(2,1)}, bf16[256,1024]{1,0:T(8,128)(2,1)S(1)}) custom-call(f32[256,1024]{1,0:T(8,128)S(1)} %fusion.9.kpre.vpre, f32[256,1024]{1,0:T(8,128)S(1)} %fusion.9.kpre.vpre, bf16[256,2560]{1,0:T(8,128)(2,1)S(1)} %copy-done.1, bf16[256,2560]{1,0:T(8,128)(2,1)S(1)} %copy-done.2, f32[256,128]{1,0:T(8,128)S(1)} %get-tuple-element.80.cos, ...), custom_call_target="tpu_custom_call" | custom-call | tf_op jit(solution)/shard_map/pallas_call | solution.py:111
  102.0 1.6 collective-permute-done.9
  103.6 3.6 %shard_map.140 = bf16[12288,128]{1,0:T(8,128)(2,1)} custom-call(bf16[8,192,512]{2,1,0:T(8,128)(2,1)S(1)} %bitcast.56, bf16[512,1024]{1,0:T(8,128)(2,1)S(1)} %constant_dynamic-update-slice_fusion.pair), custom_call_target="tpu_custom_call" | custom-call | tf_op jit(solution)/shard_map/pallas_call | solution.py:169
  108.4 1.8 %shard_map.138 = (bf16[1024,256]{1,0:T(8,128)(2,1)S(1)}, bf16[1024,256]{1,0:T(8,128)(2,1)S(1)}, bf16[1024,256]{1,0:T(8,128)(2,1)S(1)}, bf16[1024,256]{1,0:T(8,128)(2,1)S(1)}) custom-call(s32[2]{0:T(128)S(1)} %pad_add_fusion.place, bf16[1024,512]{1,0:T(8,128)(2,1)S(1)} %bitcast.57, bf16[512,1024]{1,0:T(8,128)(2,1)S(1)} %constant_dynamic-update-slice_fusion.pair), custom_call_target="tpu_custom_call" | custom-call | tf_op jit(solution)/shard_map/pallas_call | solution.py:187
  110.2 2.0 %collective-permute-start.10 = (bf16[1024,256]{1,0:T(8,128)(2,1)S(1)}, bf16[1024,256]{1,0:T(8,128)(2,1)S(1)}, u32[]{:S(2)}, u32[]{:S(2)}) collective-permute-start(bf16[1024,256]{1,0:T(8,128)(2,1)S(1)} %get-tuple-element.44), channel_id=1, source_target_pairs={{0,64},{64,128},{128,192},{192,0},{1,65},{65,129},{129,193},{193,1... | collective-permute-start | bytes 1572872 | tf_op jit(solution)/shard_map/ppermute | solution.py:41
  113.3 2.0 %collective-permute-start.12 = (bf16[1024,256]{1,0:T(8,128)(2,1)S(1)}, bf16[1024,256]{1,0:T(8,128)(2,1)S(1)}, u32[]{:S(2)}, u32[]{:S(2)}) collective-permute-start(bf16[1024,256]{1,0:T(8,128)(2,1)S(1)} %get-tuple-element.46), channel_id=1, source_target_pairs={{0,192},{64,0},{128,64},{192,128},{1,193},{65,1},{129,65},{193,129... | collective-permute-start | bytes 1572872 | tf_op jit(solution)/shard_map/ppermute | solution.py:41
  115.3 9.8 %shard_map.139 = bf16[256,5120]{1,0:T(8,128)(2,1)} custom-call(bf16[256,1024]{1,0:T(8,128)(2,1)S(1)} %get-tuple-element.47.kv, bf16[5120,1024]{1,0:T(8,128)(2,1)} %all-gather.2.cloned.1.call-done.w), custom_call_target="tpu_custom_call" | custom-call | tf_op jit(solution)/shard_map/pallas_call | solution.py:144
  125.1 10.1 %collective-permute-done.10.refs_1_ = bf16[1024,256]{1,0:T(8,128)(2,1)S(1)} collective-permute-done((bf16[1024,256]{1,0:T(8,128)(2,1)S(1)}, bf16[1024,256]{1,0:T(8,128)(2,1)S(1)}, u32[]{:S(2)}, u32[]{:S(2)}) %collective-permute-start.10) | collective-permute-done | bytes 524320 | tf_op jit(solution)/shard_map/ppermute | solution.py:41
  135.1 2.9 %collective-permute-done.12.refs_3_ = bf16[1024,256]{1,0:T(8,128)(2,1)S(1)} collective-permute-done((bf16[1024,256]{1,0:T(8,128)(2,1)S(1)}, bf16[1024,256]{1,0:T(8,128)(2,1)S(1)}, u32[]{:S(2)}, u32[]{:S(2)}) %collective-permute-start.12) | collective-permute-done | bytes 524320 | tf_op jit(solution)/shard_map/ppermute | solution.py:41
  140.3 2.6 %collective-permute-start.14 = (bf16[512,128]{1,0:T(8,128)(2,1)S(1)}, bf16[512,128]{1,0:T(8,128)(2,1)S(1)}, u32[]{:S(2)}, u32[]{:S(2)}) collective-permute-start(bf16[512,128]{1,0:T(8,128)(2,1)S(1)} %get-tuple-element.56), channel_id=1, source_target_pairs={{0,32},{16,48},{32,0},{48,16},{1,33},{17,49},{33,1},{49,17},{2,34}... | collective-permute-start | bytes 393224 | tf_op jit(solution)/shard_map/ppermute | solution.py:41
  142.9 1.6 collective-permute-start.15
  144.5 2.3 %collective-permute-done.13 = bf16[512,128]{1,0:T(8,128)(2,1)S(1)} collective-permute-done((bf16[512,128]{1,0:T(8,128)(2,1)S(1)}, bf16[512,128]{1,0:T(8,128)(2,1)S(1)}, u32[]{:S(2)}, u32[]{:S(2)}) %collective-permute-start.13) | collective-permute-done | bytes 131104 | tf_op jit(solution)/shard_map/ppermute | solution.py:41
  146.9 1.4 collective-permute-done.14
  148.7 2.0 %collective-permute-start.16 = (bf16[2,64,128]{2,1,0:T(8,128)(2,1)S(1)}, bf16[2,64,128]{2,1,0:T(8,128)(2,1)S(1)}, u32[]{:S(2)}, u32[]{:S(2)}) collective-permute-start(bf16[2,64,128]{2,1,0:T(8,128)(2,1)S(1)} %get-tuple-element.76), channel_id=1, source_target_pairs={{0,2},{2,0},{4,6},{6,4},{8,10},{10,8},{12,14},{14,12},{1,3},{3,1},... | collective-permute-start | bytes 98312 | tf_op jit(solution)/shard_map/ppermute | solution.py:45
  150.7 1.5 collective-permute-start.17
  153.2 7.3 %all-to-all-start = ((bf16[16,96,128]{2,1,0:T(8,128)(2,1)}), bf16[16,96,128]{2,1,0:T(8,128)(2,1)S(1)}, u32[]{:S(2)}, u32[]{:S(2)}) async-start(bf16[16,96,128]{2,1,0:T(8,128)(2,1)} %bitcast.65), calls=%async_computation.1 | async-start | bytes 786432 | tf_op jit(solution)/shard_map/all_to_all | solution.py:281
  160.6 3.7 %collective-permute-start.19 = (bf16[64,128]{1,0:T(8,128)(2,1)S(1)}, bf16[64,128]{1,0:T(8,128)(2,1)S(1)}, u32[]{:S(2)}, u32[]{:S(2)}) collective-permute-start(bf16[64,128]{1,0:T(8,128)(2,1)S(1)} %dynamic-slice_bitcast_fusion.4), channel_id=1, source_target_pairs={{0,8},{2,10},{4,12},{6,14},{8,0},{10,2},{12,4},{14,6},{1,9},{3,11}... | collective-permute-start | bytes 49160 | tf_op jit(solution)/shard_map/ppermute | solution.py:45
  164.3 4.1 %collective-permute-done.19 = bf16[64,128]{1,0:T(8,128)(2,1)S(1)} collective-permute-done((bf16[64,128]{1,0:T(8,128)(2,1)S(1)}, bf16[64,128]{1,0:T(8,128)(2,1)S(1)}, u32[]{:S(2)}, u32[]{:S(2)}) %collective-permute-start.19) | collective-permute-done | bytes 16416 | tf_op jit(solution)/shard_map/ppermute | solution.py:45
  (90 shorter events, 20.6 us)
Async XLA Ops:
  7.2 80.7 %all-gather.2.cloned.1.call-start = ((), (), s32[]{:S(2)}) async-start(), calls=%async_computation.2 | async-start | bytes 10813440 | tf_op jit(solution)/shard_map/all_gather | solution.py:249
  7.9 145.3 %reduce-scatter.2.cloned.1.call-start = ((), (), s32[]{:S(2)}) async-start(), calls=%async_computation.3 | async-start | bytes 3538944 | tf_op jit(solution)/shard_map/reduce_scatter | solution.py:269
  13.2 4.5 %collective-permute-start.1 = (f32[8,128]{1,0:T(8,128)S(1)}, f32[8,128]{1,0:T(8,128)S(1)}, u32[]{:S(2)}, u32[]{:S(2)}) collective-permute-start(f32[8,128]{1,0:T(8,128)S(1)} %broadcast_in_dim.57), channel_id=1, source_target_pairs={{0,1},{1,0},{2,3},{3,2},{4,5},{5,4},{6,7},{7,6},{8,9},{9,8},{10,11... | collective-permute-start | bytes 12296 | tf_op jit(solution)/shard_map/ppermute | solution.py:45
  18.4 5.5 %collective-permute-start.2 = (f32[8,128]{1,0:T(8,128)S(1)}, f32[8,128]{1,0:T(8,128)S(1)}, u32[]{:S(2)}, u32[]{:S(2)}) collective-permute-start(f32[8,128]{1,0:T(8,128)S(1)} %broadcast_add_fusion), channel_id=1, source_target_pairs={{0,64},{64,0},{128,192},{192,128},{1,65},{65,1},{129,193},{193,129... | collective-permute-start | bytes 12296 | tf_op jit(solution)/shard_map/ppermute | solution.py:45
  20.7 31.5 %copy-start.10 = (s32[1,256]{1,0:T(1,128)S(1)}, s32[1,256]{1,0:T(1,128)}, u32[]{:S(2)}) copy-start(s32[1,256]{1,0:T(1,128)} %param.13) | copy-start | bytes 3076
  20.7 31.5 %copy-start.11 = (f32[1,4]{1,0:T(1,128)S(1)}, f32[1,4]{1,0:T(1,128)}, u32[]{:S(2)}) copy-start(f32[1,4]{1,0:T(1,128)} %param.15) | copy-start | bytes 52
  23.7 32.1 %copy-start.3 = (bf16[16,1,160,256]{3,2,1,0:T(8,128)(2,1)}, bf16[16,1,160,256]{3,2,1,0:T(8,128)(2,1)S(1)}, u32[]{:S(2)}) copy-start(bf16[16,1,160,256]{3,2,1,0:T(8,128)(2,1)S(1)} %get-tuple-element.73) | copy-start | bytes 3932164
  23.7 32.1 %collective-permute-start = (bf16[16,160,256]{2,1,0:T(8,128)(2,1)}, bf16[16,160,256]{2,1,0:T(8,128)(2,1)S(1)}, u32[]{:S(2)}, u32[]{:S(2)}) collective-permute-start(bf16[16,160,256]{2,1,0:T(8,128)(2,1)} %get-tuple-element.72), channel_id=1, source_target_pairs={{0,1},{1,0},{2,3},{3,2},{4,5},{5,4},{6,7},{7,6},{8,9},{9,8},{10,11... | collective-permute-start | bytes 3932168 | tf_op jit(solution)/shard_map/ppermute | solution.py:41
  24.6 5.2 %collective-permute-start.3 = (f32[8,128]{1,0:T(8,128)S(1)}, f32[8,128]{1,0:T(8,128)S(1)}, u32[]{:S(2)}, u32[]{:S(2)}) collective-permute-start(f32[8,128]{1,0:T(8,128)S(1)} %fusion.12), channel_id=1, source_target_pairs={{0,128},{64,192},{128,0},{192,64},{1,129},{65,193},{129,1},{193,65... | collective-permute-start | bytes 12296 | tf_op jit(solution)/shard_map/ppermute | solution.py:45
  29.8 3.6 %collective-permute-start.4 = (f32[8,128]{1,0:T(8,128)S(1)}, f32[8,128]{1,0:T(8,128)S(1)}, u32[]{:S(2)}, u32[]{:S(2)}) collective-permute-start(f32[8,128]{1,0:T(8,128)S(1)} %add.107), channel_id=1, source_target_pairs={{0,16},{16,0},{1,17},{17,1},{2,18},{18,2},{3,19},{19,3},{4,20},{20... | collective-permute-start | bytes 12296 | tf_op jit(solution)/shard_map/ppermute | solution.py:45
  33.4 5.1 %collective-permute-start.5 = (f32[8,128]{1,0:T(8,128)S(1)}, f32[8,128]{1,0:T(8,128)S(1)}, u32[]{:S(2)}, u32[]{:S(2)}) collective-permute-start(f32[8,128]{1,0:T(8,128)S(1)} %add.108), channel_id=1, source_target_pairs={{0,32},{32,0},{1,33},{33,1},{2,34},{34,2},{3,35},{35,3},{4,36},{36... | collective-permute-start | bytes 12296 | tf_op jit(solution)/shard_map/ppermute | solution.py:45
  38.6 3.6 %collective-permute-start.6 = (f32[8,128]{1,0:T(8,128)S(1)}, f32[8,128]{1,0:T(8,128)S(1)}, u32[]{:S(2)}, u32[]{:S(2)}) collective-permute-start(f32[8,128]{1,0:T(8,128)S(1)} %add.109), channel_id=1, source_target_pairs={{0,2},{2,0},{4,6},{6,4},{8,10},{10,8},{12,14},{14,12},{1,3},{3,1},... | collective-permute-start | bytes 12296 | tf_op jit(solution)/shard_map/ppermute | solution.py:45
  42.2 4.6 %collective-permute-start.7 = (f32[8,128]{1,0:T(8,128)S(1)}, f32[8,128]{1,0:T(8,128)S(1)}, u32[]{:S(2)}, u32[]{:S(2)}) collective-permute-start(f32[8,128]{1,0:T(8,128)S(1)} %add.110), channel_id=1, source_target_pairs={{0,4},{2,6},{4,0},{6,2},{8,12},{10,14},{12,8},{14,10},{1,5},{3,7},... | collective-permute-start | bytes 12296 | tf_op jit(solution)/shard_map/ppermute | solution.py:45
  46.8 7.6 %collective-permute-start.8 = (f32[8,128]{1,0:T(8,128)S(1)}, f32[8,128]{1,0:T(8,128)S(1)}, u32[]{:S(2)}, u32[]{:S(2)}) collective-permute-start(f32[8,128]{1,0:T(8,128)S(1)} %add.111), channel_id=1, source_target_pairs={{0,8},{2,10},{4,12},{6,14},{8,0},{10,2},{12,4},{14,6},{1,9},{3,11}... | collective-permute-start | bytes 12296 | tf_op jit(solution)/shard_map/ppermute | solution.py:45
  57.0 1.7 copy-start.6
  87.9 6.5 %copy-start.1 = (bf16[256,2560]{1,0:T(8,128)(2,1)S(1)}, bf16[256,2560]{1,0:T(8,128)(2,1)}, u32[]{:S(2)}) copy-start(bf16[256,2560]{1,0:T(8,128)(2,1)} %q.1) | copy-start | bytes 3932164
  87.9 6.5 %copy-start.2 = (bf16[256,2560]{1,0:T(8,128)(2,1)S(1)}, bf16[256,2560]{1,0:T(8,128)(2,1)}, u32[]{:S(2)}) copy-start(bf16[256,2560]{1,0:T(8,128)(2,1)} %up.1) | copy-start | bytes 3932164
  101.7 1.9 %collective-permute-start.9 = (bf16[256,1024]{1,0:T(8,128)(2,1)S(1)}, bf16[256,1024]{1,0:T(8,128)(2,1)S(1)}, u32[]{:S(2)}, u32[]{:S(2)}) collective-permute-start(bf16[256,1024]{1,0:T(8,128)(2,1)S(1)} %get-tuple-element.47.kv), channel_id=1, source_target_pairs={{0,1},{1,0},{2,3},{3,2},{4,5},{5,4},{6,7},{7,6},{8,9},{9,8},{10,11... | collective-permute-start | bytes 1572872 | tf_op jit(solution)/shard_map/ppermute | solution.py:41
  110.2 24.9 %collective-permute-start.10 = (bf16[1024,256]{1,0:T(8,128)(2,1)S(1)}, bf16[1024,256]{1,0:T(8,128)(2,1)S(1)}, u32[]{:S(2)}, u32[]{:S(2)}) collective-permute-start(bf16[1024,256]{1,0:T(8,128)(2,1)S(1)} %get-tuple-element.44), channel_id=1, source_target_pairs={{0,64},{64,128},{128,192},{192,0},{1,65},{65,129},{129,193},{193,1... | collective-permute-start | bytes 1572872 | tf_op jit(solution)/shard_map/ppermute | solution.py:41
  112.3 22.9 %collective-permute-start.11 = (bf16[1024,256]{1,0:T(8,128)(2,1)S(1)}, bf16[1024,256]{1,0:T(8,128)(2,1)S(1)}, u32[]{:S(2)}, u32[]{:S(2)}) collective-permute-start(bf16[1024,256]{1,0:T(8,128)(2,1)S(1)} %get-tuple-element.45), channel_id=1, source_target_pairs={{0,128},{64,192},{128,0},{192,64},{1,129},{65,193},{129,1},{193,65... | collective-permute-start | bytes 1572872 | tf_op jit(solution)/shard_map/ppermute | solution.py:41
  113.3 24.7 %collective-permute-start.12 = (bf16[1024,256]{1,0:T(8,128)(2,1)S(1)}, bf16[1024,256]{1,0:T(8,128)(2,1)S(1)}, u32[]{:S(2)}, u32[]{:S(2)}) collective-permute-start(bf16[1024,256]{1,0:T(8,128)(2,1)S(1)} %get-tuple-element.46), channel_id=1, source_target_pairs={{0,192},{64,0},{128,64},{192,128},{1,193},{65,1},{129,65},{193,129... | collective-permute-start | bytes 1572872 | tf_op jit(solution)/shard_map/ppermute | solution.py:41
  125.1 43.4 %copy-start.7 = (f32[160,128]{1,0:T(8,128)S(1)}, f32[160,128]{1,0:T(8,128)}, u32[]{:S(2)}) copy-start(f32[160,128]{1,0:T(8,128)} %param.17) | copy-start | bytes 245764
  125.1 43.4 %copy-start.8 = (f32[160,128]{1,0:T(8,128)S(1)}, f32[160,128]{1,0:T(8,128)}, u32[]{:S(2)}) copy-start(f32[160,128]{1,0:T(8,128)} %param.18) | copy-start | bytes 245764
  125.1 43.4 %copy-start.9 = (f32[160,128]{1,0:T(8,128)S(1)}, f32[160,128]{1,0:T(8,128)}, u32[]{:S(2)}) copy-start(f32[160,128]{1,0:T(8,128)} %param.19) | copy-start | bytes 245764
  139.2 7.7 %collective-permute-start.13 = (bf16[512,128]{1,0:T(8,128)(2,1)S(1)}, bf16[512,128]{1,0:T(8,128)(2,1)S(1)}, u32[]{:S(2)}, u32[]{:S(2)}) collective-permute-start(bf16[512,128]{1,0:T(8,128)(2,1)S(1)} %get-tuple-element.55), channel_id=1, source_target_pairs={{0,16},{16,32},{32,48},{48,0},{1,17},{17,33},{33,49},{49,1},{2,18}... | collective-permute-start | bytes 393224 | tf_op jit(solution)/shard_map/ppermute | solution.py:41
  140.3 8.1 %collective-permute-start.14 = (bf16[512,128]{1,0:T(8,128)(2,1)S(1)}, bf16[512,128]{1,0:T(8,128)(2,1)S(1)}, u32[]{:S(2)}, u32[]{:S(2)}) collective-permute-start(bf16[512,128]{1,0:T(8,128)(2,1)S(1)} %get-tuple-element.56), channel_id=1, source_target_pairs={{0,32},{16,48},{32,0},{48,16},{1,33},{17,49},{33,1},{49,17},{2,34}... | collective-permute-start | bytes 393224 | tf_op jit(solution)/shard_map/ppermute | solution.py:41
  142.9 5.7 %collective-permute-start.15 = (bf16[512,128]{1,0:T(8,128)(2,1)S(1)}, bf16[512,128]{1,0:T(8,128)(2,1)S(1)}, u32[]{:S(2)}, u32[]{:S(2)}) collective-permute-start(bf16[512,128]{1,0:T(8,128)(2,1)S(1)} %get-tuple-element.57), channel_id=1, source_target_pairs={{0,48},{16,0},{32,16},{48,32},{1,49},{17,1},{33,17},{49,33},{2,50}... | collective-permute-start | bytes 393224 | tf_op jit(solution)/shard_map/ppermute | solution.py:41
  148.7 11.8 %collective-permute-start.16 = (bf16[2,64,128]{2,1,0:T(8,128)(2,1)S(1)}, bf16[2,64,128]{2,1,0:T(8,128)(2,1)S(1)}, u32[]{:S(2)}, u32[]{:S(2)}) collective-permute-start(bf16[2,64,128]{2,1,0:T(8,128)(2,1)S(1)} %get-tuple-element.76), channel_id=1, source_target_pairs={{0,2},{2,0},{4,6},{6,4},{8,10},{10,8},{12,14},{14,12},{1,3},{3,1},... | collective-permute-start | bytes 98312 | tf_op jit(solution)/shard_map/ppermute | solution.py:45
  150.7 9.9 %collective-permute-start.17 = (bf16[2,64,128]{2,1,0:T(8,128)(2,1)S(1)}, bf16[2,64,128]{2,1,0:T(8,128)(2,1)S(1)}, u32[]{:S(2)}, u32[]{:S(2)}) collective-permute-start(bf16[2,64,128]{2,1,0:T(8,128)(2,1)S(1)} %get-tuple-element.75), channel_id=1, source_target_pairs={{0,4},{2,6},{4,0},{6,2},{8,12},{10,14},{12,8},{14,10},{1,5},{3,7},... | collective-permute-start | bytes 98312 | tf_op jit(solution)/shard_map/ppermute | solution.py:45
  152.1 8.4 %collective-permute-start.18 = (bf16[2,64,128]{2,1,0:T(8,128)(2,1)S(1)}, bf16[2,64,128]{2,1,0:T(8,128)(2,1)S(1)}, u32[]{:S(2)}, u32[]{:S(2)}) collective-permute-start(bf16[2,64,128]{2,1,0:T(8,128)(2,1)S(1)} %get-tuple-element.74), channel_id=1, source_target_pairs={{0,6},{2,4},{4,2},{6,0},{8,14},{10,12},{12,10},{14,8},{1,7},{3,5},... | collective-permute-start | bytes 98312 | tf_op jit(solution)/shard_map/ppermute | solution.py:45
  153.2 15.2 %all-to-all-start = ((bf16[16,96,128]{2,1,0:T(8,128)(2,1)}), bf16[16,96,128]{2,1,0:T(8,128)(2,1)S(1)}, u32[]{:S(2)}, u32[]{:S(2)}) async-start(bf16[16,96,128]{2,1,0:T(8,128)(2,1)} %bitcast.65), calls=%async_computation.1 | async-start | bytes 786432 | tf_op jit(solution)/shard_map/all_to_all | solution.py:281
  160.6 7.8 %collective-permute-start.19 = (bf16[64,128]{1,0:T(8,128)(2,1)S(1)}, bf16[64,128]{1,0:T(8,128)(2,1)S(1)}, u32[]{:S(2)}, u32[]{:S(2)}) collective-permute-start(bf16[64,128]{1,0:T(8,128)(2,1)S(1)} %dynamic-slice_bitcast_fusion.4), channel_id=1, source_target_pairs={{0,8},{2,10},{4,12},{6,14},{8,0},{10,2},{12,4},{14,6},{1,9},{3,11}... | collective-permute-start | bytes 49160 | tf_op jit(solution)/shard_map/ppermute | solution.py:45
  (3 other events, 3.6 us)
Sparse Core Ops, SparseCore 0:
  9.9 77.9 all-gather.1
  107.4 45.6 reduce-scatter.1
